TPU v7x, 32 devices: a whole 2x2x4 slice. The times are simulated.
32 devices in a mesh: section: 2 (over z_hi), fsdp: 8 (over y, x, core), rep: 2 (over z_lo).
Axes of the slice: x: 2, y: 2, z: 4 (z_hi: 2, z_lo: 2; z = z_hi * 2 + z_lo), core: 2. Of those that a mesh axis runs over, the one named last changes fastest.
Arguments:
- section_inputs: bfloat16 [2, 2, 2, 1024, 2048], P('section', None, 'rep', 'fsdp'), may hold values from -6 to 6
- doc_lengths: int32 [2, 2, 3], P(None, 'rep'), may hold values from 1 to 1022, as said below
- mixer_gain: bfloat16 [2, 2048], P('section', 'fsdp'), may hold values from 0.25 to 1.75
- heads_weight: bfloat16 [2, 2048, 4096], P('section', 'fsdp'), may hold values from -0.125 to 0.125
- merge_weight: bfloat16 [2, 2048, 2048], P('section', 'fsdp'), may hold values from -0.5 to 0.5
- head_gain: bfloat16 [2, 256], P('section', 'fsdp'), may hold values from 0.25 to 1.75
- feed_gain: bfloat16 [2, 2048], P('section', 'fsdp'), may hold values from 0.25 to 1.75
- expand_weight: bfloat16 [2, 2048, 12288], P('section', 'fsdp'), may hold values from -0.125 to 0.125
- reduce_weight: bfloat16 [2, 6144, 2048], P('section', 'fsdp'), may hold values from -0.078125 to 0.078125
Outputs:
- section_outputs: float32 [2, 2, 2, 1024, 2048], P('section', None, 'rep', 'fsdp')
- grad_mixer_gain: float32 [2, 2048], P('section', 'fsdp')
- grad_heads_weight: float32 [2, 2048, 4096], P('section', 'fsdp')
- grad_merge_weight: float32 [2, 2048, 2048], P('section', 'fsdp')
- grad_head_gain: float32 [2, 256], P('section', 'fsdp')
- grad_feed_gain: float32 [2, 2048], P('section', 'fsdp')
- grad_expand_weight: float32 [2, 2048, 12288], P('section', 'fsdp')
- grad_reduce_weight: float32 [2, 6144, 2048], P('section', 'fsdp')
Inputs may be any that keep to these rules, and one draw needn't show every extreme that they name: `doc_lengths`: the 3 lengths of each sequence are positive and sum to 1024.
All inputs are finite; a program needn't handle non-finite values.
Results may differ from a plain program's by a relative error of at most 0.025.
Values may be sent and summed in bfloat16 or wider, within the bound.
A program may use at most 448 MiB of HBM per device.

v0:
```python
import math

import jax
import jax.numpy as jnp
from jax import lax
from jax.sharding import PartitionSpec as P

FF = 6144
QUERY_HEADS = 16
KEY_VALUE_HEADS = 8
HEAD_SIZE = 128


NORM_EPS = 1e-06
ROPE_BASE = 1000000.0
MASKED_SCORE = -1e30


def from_behind(array, axis, by):
    count = lax.axis_size(axis)
    pairs = [(i, i + by) for i in range(count) if 0 <= i + by < count]
    return lax.ppermute(array, axis, pairs)


def normed(values):
    return values * lax.rsqrt(jnp.mean(values * values, axis=-1, keepdims=True) + NORM_EPS)


def scaled(values, gain_row):
    return normed(values) * gain_row


def rotate(values, positions):
    half_width = values.shape[-1] // 2
    frequency = jnp.exp(
        jnp.arange(half_width, dtype=jnp.float32) * (-2.0 * math.log(ROPE_BASE) / values.shape[-1])
    )
    angles = positions.astype(jnp.float32)[:, None] * frequency[None, :]
    cosine = jnp.cos(angles)[:, None, :]
    sine_part = jnp.sin(angles)[:, None, :]
    lower_half = values[..., :half_width]
    upper_half = values[..., half_width:]
    return jnp.concatenate(
        [
            lower_half * cosine - upper_half * sine_part,
            upper_half * cosine + lower_half * sine_part,
        ],
        axis=-1,
    )


def places(doc_lengths, sequence_length):
    doc_ends = jnp.cumsum(doc_lengths)
    token_index = jnp.arange(sequence_length, dtype=jnp.int32)
    passed_ends = (token_index[:, None] >= doc_ends[None, :]).astype(jnp.int32)
    document_index = jnp.sum(passed_ends, axis=1)
    doc_start = jnp.sum(passed_ends * doc_lengths[None, :], axis=1)
    return (document_index, token_index - doc_start)


def heads_of(projected_output, head_gain, positions):
    count_of_tokens = projected_output.shape[0]
    query_rows = projected_output[:, : QUERY_HEADS * HEAD_SIZE].reshape(
        count_of_tokens, QUERY_HEADS, HEAD_SIZE
    )
    heads_of_keys = projected_output[
        :, QUERY_HEADS * HEAD_SIZE : (QUERY_HEADS + KEY_VALUE_HEADS) * HEAD_SIZE
    ].reshape(count_of_tokens, KEY_VALUE_HEADS, HEAD_SIZE)
    heads_of_values = projected_output[:, (QUERY_HEADS + KEY_VALUE_HEADS) * HEAD_SIZE :]
    return (
        rotate(scaled(query_rows, head_gain[:HEAD_SIZE]), positions),
        rotate(scaled(heads_of_keys, head_gain[HEAD_SIZE:]), positions),
        heads_of_values,
    )


def gated_unit(joined):
    return jax.nn.silu(joined[:, :FF]) * joined[:, FF:]


def times_transposed(left_side, right_side):
    return lax.dot_general(
        left_side, right_side, (((1,), (1,)), ((), ())), preferred_element_type=jnp.float32
    )


def allowed_mask(doc_rows, row_start, document_index):
    row_index = row_start + jnp.arange(doc_rows.shape[0], dtype=jnp.int32)
    key_index = jnp.arange(document_index.shape[0], dtype=jnp.int32)
    return (doc_rows[:, None] == document_index[None, :]) & (
        row_index[:, None] >= key_index[None, :]
    )


def raw_scores(query_rows_second, rows_of_keys, allowed):
    grouped_heads = query_rows_second.reshape(
        query_rows_second.shape[0], KEY_VALUE_HEADS, QUERY_HEADS // KEY_VALUE_HEADS, HEAD_SIZE
    )
    heads_of_keys = rows_of_keys.reshape(rows_of_keys.shape[0], KEY_VALUE_HEADS, HEAD_SIZE)
    scores = jnp.einsum(
        "rkgd,tkd->rkgt", grouped_heads, heads_of_keys, preferred_element_type=jnp.float32
    ) * HEAD_SIZE ** (-0.5)
    return jnp.where(allowed[:, None, None, :], scores, MASKED_SCORE)


def attend_rows(query_rows_second, rows_of_keys, rows_of_values, allowed):
    scores = raw_scores(query_rows_second, rows_of_keys, allowed)
    row_max = jnp.max(scores, axis=-1, keepdims=True)
    exp_scores = jnp.exp(scores - row_max)
    row_totals = jnp.sum(exp_scores, axis=-1, keepdims=True)
    attn_probs = (exp_scores / row_totals).astype(jnp.bfloat16)
    heads_of_values = rows_of_values.reshape(rows_of_values.shape[0], KEY_VALUE_HEADS, HEAD_SIZE)
    heads_mixed = jnp.einsum(
        "rkgt,tkd->rkgd", attn_probs, heads_of_values, preferred_element_type=jnp.float32
    )
    return (
        heads_mixed.reshape(query_rows_second.shape[0], QUERY_HEADS * HEAD_SIZE),
        row_max + jnp.log(row_totals),
    )


def attend_back(
    query_rows_second, rows_of_keys, rows_of_values, allowed, log_totals, mixed_gradient_second
):
    count_of_rows = query_rows_second.shape[0]
    count_of_keys = rows_of_keys.shape[0]
    grouped_heads = query_rows_second.reshape(
        count_of_rows, KEY_VALUE_HEADS, QUERY_HEADS // KEY_VALUE_HEADS, HEAD_SIZE
    )
    heads_of_keys = rows_of_keys.reshape(count_of_keys, KEY_VALUE_HEADS, HEAD_SIZE)
    heads_of_values = rows_of_values.reshape(count_of_keys, KEY_VALUE_HEADS, HEAD_SIZE)
    heads_gradient = mixed_gradient_second.reshape(
        count_of_rows, KEY_VALUE_HEADS, QUERY_HEADS // KEY_VALUE_HEADS, HEAD_SIZE
    )
    attn_probs = jnp.exp(raw_scores(query_rows_second, rows_of_keys, allowed) - log_totals)
    grad_probs = jnp.einsum(
        "rkgd,tkd->rkgt", heads_gradient, heads_of_values, preferred_element_type=jnp.float32
    )
    grad_scores = (
        attn_probs * (grad_probs - jnp.sum(grad_probs * attn_probs, axis=-1, keepdims=True))
    ).astype(jnp.bfloat16)
    queries_gradient = jnp.einsum(
        "rkgt,tkd->rkgd", grad_scores, heads_of_keys, preferred_element_type=jnp.float32
    ) * HEAD_SIZE ** (-0.5)
    keys_gradient = jnp.einsum(
        "rkgt,rkgd->tkd", grad_scores, grouped_heads, preferred_element_type=jnp.float32
    ) * HEAD_SIZE ** (-0.5)
    values_gradient = jnp.einsum(
        "rkgt,rkgd->tkd",
        attn_probs.astype(jnp.bfloat16),
        heads_gradient,
        preferred_element_type=jnp.float32,
    )
    return (
        queries_gradient.reshape(count_of_rows, QUERY_HEADS, HEAD_SIZE),
        keys_gradient.reshape(count_of_keys, KEY_VALUE_HEADS * HEAD_SIZE),
        values_gradient.reshape(count_of_keys, KEY_VALUE_HEADS * HEAD_SIZE),
    )


def layer_forward(inputs, layer_full, positions, allowed):
    mixer_gain, heads_weight, merge_weight, head_gain, feed_gain, expand_weight, reduce_weight = (
        layer_full
    )
    count_of_rows = inputs.shape[0]
    normal_a = scaled(inputs, mixer_gain).astype(jnp.bfloat16)
    projected_output = jnp.dot(normal_a, heads_weight, preferred_element_type=jnp.float32)
    query_rows, heads_of_keys, heads_of_values = heads_of(projected_output, head_gain, positions)
    rows_of_keys, rows_of_values = (
        lax.all_gather(
            heads_of_keys.reshape(count_of_rows, KEY_VALUE_HEADS * HEAD_SIZE).astype(jnp.bfloat16),
            "fsdp",
            axis=0,
            tiled=True,
        ),
        lax.all_gather(heads_of_values.astype(jnp.bfloat16), "fsdp", axis=0, tiled=True),
    )
    heads_mixed, log_totals = attend_rows(
        query_rows.astype(jnp.bfloat16), rows_of_keys, rows_of_values, allowed
    )
    mixed_b = heads_mixed.astype(jnp.bfloat16)
    middle = inputs + jnp.dot(mixed_b, merge_weight, preferred_element_type=jnp.float32)
    normal_b = scaled(middle, feed_gain).astype(jnp.bfloat16)
    joined = jnp.dot(normal_b, expand_weight, preferred_element_type=jnp.float32)
    hidden = gated_unit(joined).astype(jnp.bfloat16)
    result = middle + jnp.dot(hidden, reduce_weight, preferred_element_type=jnp.float32)
    return (
        result,
        (
            inputs,
            normal_a,
            projected_output,
            rows_of_keys,
            rows_of_values,
            log_totals,
            mixed_b,
            middle,
            normal_b,
            joined,
            hidden,
        ),
    )


def layer_backward(upstream, layer_full, saved, positions, allowed):
    mixer_gain, heads_weight, merge_weight, head_gain, feed_gain, expand_weight, reduce_weight = (
        layer_full
    )
    (
        inputs,
        normal_a,
        projected_output,
        rows_of_keys,
        rows_of_values,
        log_totals,
        mixed_b,
        middle,
        normal_b,
        joined,
        hidden,
    ) = saved
    count_of_rows = inputs.shape[0]
    upstream_b = upstream.astype(jnp.bfloat16)
    grad_hidden = times_transposed(upstream_b, reduce_weight)
    unused_joined, gated_back = jax.vjp(gated_unit, joined)
    grad_joined = gated_back(grad_hidden)[0].astype(jnp.bfloat16)
    unused_feed, feed_back = jax.vjp(scaled, middle, feed_gain)
    grad_middle_part, grad_feed = feed_back(times_transposed(grad_joined, expand_weight))
    grad_middle = upstream + grad_middle_part
    grad_middle_b = grad_middle.astype(jnp.bfloat16)
    grad_mixed = times_transposed(grad_middle_b, merge_weight).astype(jnp.bfloat16)
    head_values, heads_back = jax.vjp(
        lambda projected_rows, gain_rows: heads_of(projected_rows, gain_rows, positions),
        projected_output,
        head_gain,
    )
    queries_gradient, grad_keys_all, grad_values_all = attend_back(
        head_values[0].astype(jnp.bfloat16),
        rows_of_keys,
        rows_of_values,
        allowed,
        log_totals,
        grad_mixed,
    )
    keys_gradient, values_gradient = (
        lax.psum_scatter(
            grad_keys_all.astype(jnp.bfloat16), "fsdp", scatter_dimension=0, tiled=True
        ).astype(jnp.float32),
        lax.psum_scatter(
            grad_values_all.astype(jnp.bfloat16), "fsdp", scatter_dimension=0, tiled=True
        ).astype(jnp.float32),
    )
    grad_projected, grad_head = heads_back(
        (
            queries_gradient,
            keys_gradient.reshape(count_of_rows, KEY_VALUE_HEADS, HEAD_SIZE),
            values_gradient,
        )
    )
    grad_projected_b = grad_projected.astype(jnp.bfloat16)
    unused_mixer, mixer_back = jax.vjp(scaled, inputs, mixer_gain)
    grad_inputs_part, grad_mixer = mixer_back(times_transposed(grad_projected_b, heads_weight))
    operands = (
        normal_a,
        grad_projected_b,
        mixed_b,
        grad_middle_b,
        normal_b,
        grad_joined,
        hidden,
        upstream_b,
    )
    return (grad_middle + grad_inputs_part, operands, (grad_mixer, grad_feed, grad_head))


def product_term(left_side, right_side):
    return lax.dot_general(
        left_side, right_side, (((0,), (0,)), ((), ())), preferred_element_type=jnp.float32
    )


def reduce_grads(operands, gain_terms):
    (
        normal_a,
        grad_projected_b,
        mixed_b,
        grad_middle_b,
        normal_b,
        grad_joined,
        hidden,
        upstream_b,
    ) = operands
    heads_gradient = lax.psum_scatter(
        product_term(normal_a, grad_projected_b).astype(jnp.bfloat16),
        "fsdp",
        scatter_dimension=0,
        tiled=True,
    )
    grad_merge = lax.psum_scatter(
        product_term(mixed_b, grad_middle_b).astype(jnp.bfloat16),
        "fsdp",
        scatter_dimension=0,
        tiled=True,
    )
    grad_expand = lax.psum_scatter(
        product_term(normal_b, grad_joined).astype(jnp.bfloat16),
        "fsdp",
        scatter_dimension=0,
        tiled=True,
    )
    grad_reduce = lax.psum_scatter(
        product_term(hidden, upstream_b).astype(jnp.bfloat16),
        "fsdp",
        scatter_dimension=0,
        tiled=True,
    )
    grad_mixer, grad_feed, grad_head = (
        lax.psum_scatter(gain_terms[0], "fsdp", scatter_dimension=0, tiled=True),
        lax.psum_scatter(gain_terms[1], "fsdp", scatter_dimension=0, tiled=True),
        lax.psum_scatter(gain_terms[2], "fsdp", scatter_dimension=0, tiled=True),
    )
    return (
        lax.psum(grad_mixer.astype(jnp.bfloat16), "rep").astype(jnp.float32),
        lax.psum(heads_gradient, "rep").astype(jnp.float32),
        lax.psum(grad_merge, "rep").astype(jnp.float32),
        lax.psum(grad_head.astype(jnp.bfloat16), "rep").astype(jnp.float32),
        lax.psum(grad_feed.astype(jnp.bfloat16), "rep").astype(jnp.float32),
        lax.psum(grad_expand, "rep").astype(jnp.float32),
        lax.psum(grad_reduce, "rep").astype(jnp.float32),
    )


def body(
    section_inputs,
    doc_lengths,
    mixer_gain,
    heads_weight,
    merge_weight,
    head_gain,
    feed_gain,
    expand_weight,
    reduce_weight,
):
    section_index = lax.axis_index("section")
    head_section = section_index == 0
    shard_index = lax.axis_index("fsdp")
    count_of_rows = section_inputs.shape[3]
    sequence_length = count_of_rows * lax.axis_size("fsdp")
    own_rows = section_inputs[0, :, 0]
    micro_count = own_rows.shape[0]
    mixer_part = (
        lax.all_gather(mixer_gain, "fsdp", axis=1, tiled=True),
        lax.all_gather(heads_weight, "fsdp", axis=1, tiled=True),
        lax.all_gather(merge_weight, "fsdp", axis=1, tiled=True),
        lax.all_gather(head_gain, "fsdp", axis=1, tiled=True),
    )
    feed_part = (
        lax.all_gather(feed_gain, "fsdp", axis=1, tiled=True),
        lax.all_gather(expand_weight, "fsdp", axis=1, tiled=True),
        lax.all_gather(reduce_weight, "fsdp", axis=1, tiled=True),
    )
    layer_full = (
        mixer_part[0][0].astype(jnp.float32),
        mixer_part[1][0],
        mixer_part[2][0],
        mixer_part[3][0].astype(jnp.float32),
        feed_part[0][0].astype(jnp.float32),
        feed_part[1][0],
        feed_part[2][0],
    )

    def layout(micro_slot):
        document_index, positions = places(doc_lengths[micro_slot, 0], sequence_length)
        row_start = shard_index * count_of_rows
        doc_rows = lax.dynamic_slice_in_dim(document_index, row_start, count_of_rows)
        own_positions = lax.dynamic_slice_in_dim(positions, row_start, count_of_rows)
        return (own_positions, allowed_mask(doc_rows, row_start, document_index))

    results = jnp.zeros((micro_count, count_of_rows, own_rows.shape[2]), jnp.float32)
    saved_acts = None
    arrived = jnp.zeros((count_of_rows, own_rows.shape[2]), jnp.bfloat16)
    for step_index in range(micro_count + 1):
        slot_raw = step_index - section_index
        is_live = (slot_raw >= 0) & (slot_raw < micro_count)
        micro_slot = jnp.clip(slot_raw, 0, micro_count - 1)
        inputs = jnp.where(
            head_section, own_rows[min(step_index, micro_count - 1)], arrived
        ).astype(jnp.float32)
        positions, allowed = layout(micro_slot)
        result, saved = layer_forward(inputs, layer_full, positions, allowed)
        if saved_acts is None:
            saved_acts = tuple(
                (jnp.zeros((micro_count,) + current.shape, current.dtype) for current in saved)
            )
        saved_acts = tuple(
            (
                jnp.where(is_live, buffer.at[micro_slot].set(current), buffer)
                for buffer, current in zip(saved_acts, saved)
            )
        )
        results = jnp.where(
            is_live & jnp.logical_not(head_section), results.at[micro_slot].set(result), results
        )
        if step_index < micro_count:
            arrived = from_behind(result.astype(jnp.bfloat16), "section", 1)
    gradients = None
    stashed = None
    gain_sums = None
    from_next = jnp.zeros((count_of_rows, own_rows.shape[2]), jnp.bfloat16)
    for step_index in range(micro_count + 1):
        slot_raw = step_index - 1 + section_index
        is_live = (slot_raw >= 0) & (slot_raw < micro_count)
        micro_slot = jnp.clip(slot_raw, 0, micro_count - 1)
        upstream = jnp.where(
            head_section, from_next, own_rows[min(step_index, micro_count - 1)]
        ).astype(jnp.float32)
        upstream = jnp.where(is_live, upstream, 0.0)
        positions, allowed = layout(micro_slot)
        saved = tuple((buffer[micro_slot] for buffer in saved_acts))
        grad_inputs, operands, gain_terms = layer_backward(
            upstream, layer_full, saved, positions, allowed
        )
        results = jnp.where(
            is_live & head_section, results.at[micro_slot].set(grad_inputs), results
        )
        if step_index < micro_count:
            from_next = from_behind(grad_inputs.astype(jnp.bfloat16), "section", -1)
        if stashed is None:
            stashed = tuple(
                (jnp.zeros((micro_count,) + current.shape, current.dtype) for current in operands)
            )
            gain_sums = tuple((jnp.zeros_like(current) for current in gain_terms))
        stashed = tuple(
            (
                jnp.where(is_live, buffer.at[micro_slot].set(current), buffer)
                for buffer, current in zip(stashed, operands)
            )
        )
        gain_sums = tuple(
            (total_so_far + current for total_so_far, current in zip(gain_sums, gain_terms))
        )
    merged = tuple(
        (buffer.reshape((micro_count * count_of_rows,) + buffer.shape[2:]) for buffer in stashed)
    )
    gradients = reduce_grads(merged, gain_sums)
    grad_mixer, heads_gradient, grad_merge, grad_head, grad_feed, grad_expand, grad_reduce = (
        gradients
    )
    return (
        results[None, :, None],
        grad_mixer[None],
        heads_gradient[None],
        grad_merge[None],
        grad_head[None],
        grad_feed[None],
        grad_expand[None],
        grad_reduce[None],
    )


def solution(mesh):
    return jax.shard_map(
        body,
        mesh=mesh,
        in_specs=(
            P("section", None, "rep", "fsdp", None),
            P(None, "rep", None),
            P("section", "fsdp"),
            P("section", "fsdp", None),
            P("section", "fsdp", None),
            P("section", "fsdp"),
            P("section", "fsdp"),
            P("section", "fsdp", None),
            P("section", "fsdp", None),
        ),
        out_specs=(
            P("section", None, "rep", "fsdp", None),
            P("section", "fsdp"),
            P("section", "fsdp", None),
            P("section", "fsdp", None),
            P("section", "fsdp"),
            P("section", "fsdp"),
            P("section", "fsdp", None),
            P("section", "fsdp", None),
        ),
        check_vma=False,
    )
```

profile of v0, /device:TPU:0, one launch (start us, length us, event | category | flops | bytes accessed | tf_op | source)
XLA Modules:
  0.0 2490.9 jit_solution(12058736050100549240)
XLA Ops:
  8.0 10.6 all_gather.39
  23.4 13.5 all-reduce.33
  43.0 59.6 %all-gather.11.cloned.1.call-done = bf16[1,2048,4096]{2,1,0:T(8,128)(2,1)} async-done(((bf16[1,256,4096]{2,1,0:T(8,128)(2,1)}), bf16[1,2048,4096]{2,1,0:T(8,128)(2,1)}) %all-gather.11.cloned.1.call-update) | async-done | bytes 16777232 | tf_op jit(solution)/shard_map/all_gather | solution.py:353
  105.1 10.3 bitcast_dynamic-update-slice_fusion.3
  122.3 9.0 all_gather.45
  139.3 8.0 all-gather.15.cloned.1.call-done
  150.8 26.9 %all-gather.13.cloned.1.call-done = bf16[1024,1024]{1,0:T(8,128)(2,1)} async-done(((bf16[128,1024]{1,0:T(8,128)(2,1)}), bf16[1024,1024]{1,0:T(8,128)(2,1)}) %all-gather.13.cloned.1.call-update) | async-done | bytes 2097168 | tf_op jit(solution)/shard_map/all_gather | solution.py:176
  190.4 43.5 %all-gather.17.cloned.1.call-done = bf16[1,2048,2048]{2,1,0:T(8,128)(2,1)} async-done(((bf16[1,256,2048]{2,1,0:T(8,128)(2,1)}), bf16[1,2048,2048]{2,1,0:T(8,128)(2,1)}) %all-gather.17.cloned.1.call-update) | async-done | bytes 8388624 | tf_op jit(solution)/shard_map/all_gather | solution.py:354
  238.8 229.0 %all-gather.19.cloned.1.call-done = bf16[1,2048,12288]{2,1,0:T(8,128)(2,1)} async-done(((bf16[1,256,12288]{2,1,0:T(8,128)(2,1)}), bf16[1,2048,12288]{2,1,0:T(8,128)(2,1)}) %all-gather.19.cloned.1.call-update) | async-done | bytes 50331664 | tf_op jit(solution)/shard_map/all_gather | solution.py:359
  474.1 27.2 %bitcast_dynamic-update-slice_fusion = (f32[2,128,12288]{2,1,0:T(8,128)}, f32[128,12288]{1,0:T(8,128)}) fusion(f32[2,128,12288]{2,1,0:T(8,128)} %broadcast_in_dim.122, s32[]{:T(128)} %min.31, pred[]{:T(512)} %get-tuple-element.1008, pred[]{:T(512)S(6)} %and.296, bf16[1,2048,12288]{2,1,0:T(8,128)(2,1)} %all-gather.19.cloned.1.call-done, ...), kind=kOutput, calls=%fused_computation.95 | convolution fusion | flops 6446383104 | bytes 63972864 | tf_op jit(solution)/shard_map/dot_general | solution.py:184
  509.6 85.3 %all-gather.21.cloned.1.call-done = bf16[1,6144,2048]{2,1,0:T(8,128)(2,1)} async-done(((bf16[1,768,2048]{2,1,0:T(8,128)(2,1)}), bf16[1,6144,2048]{2,1,0:T(8,128)(2,1)}) %all-gather.21.cloned.1.call-update) | async-done | bytes 25165840 | tf_op jit(solution)/shard_map/all_gather | solution.py:360
  596.3 13.4 bitcast_dynamic-update-slice_fusion.8
  618.2 7.8 collective-permute-done
  629.3 10.8 fusion.150
  659.2 26.4 %all-gather.25.cloned.1.call-done = bf16[1024,1024]{1,0:T(8,128)(2,1)} async-done(((bf16[128,1024]{1,0:T(8,128)(2,1)}), bf16[1024,1024]{1,0:T(8,128)(2,1)}) %all-gather.25.cloned.1.call-update) | async-done | bytes 2097168 | tf_op jit(solution)/shard_map/all_gather | solution.py:170
  694.7 20.7 all-gather.23.cloned.1.call-done
  730.8 25.6 %fusion.69 = (f32[2,128,12288]{2,1,0:T(8,128)}, f32[128,12288]{1,0:T(8,128)}) fusion(f32[2,128,12288]{2,1,0:T(8,128)} %get-tuple-element.1032, s32[]{:T(128)} %min.33, pred[]{:T(512)} %get-tuple-element.1009, pred[]{:T(512)S(6)} %and.300, bf16[1,2048,12288]{2,1,0:T(8,128)(2,1)} %all-gather.19.cloned.1.call-done, f32[128,2048]{1,0:T(8,128)S(1)} %get-tuple-element.1019, ...), kind=kOutput, calls=%fused_computation.93 | convolution fusion | flops 6446383104 | bytes 70264320 | tf_op jit(solution)/shard_map/dot_general | solution.py:184
  762.8 13.9 fusion.181
  784.8 8.4 collective-permute-done.1
  859.3 16.8 all-gather.27.cloned.1.call-done
  892.4 25.8 %fusion.70 = (f32[2,128,12288]{2,1,0:T(8,128)}, f32[128,12288]{1,0:T(8,128)}) fusion(f32[2,128,12288]{2,1,0:T(8,128)} %get-tuple-element.1034, s32[]{:T(128)} %min.35, pred[]{:T(512)} %get-tuple-element.847, pred[]{:T(512)S(6)} %and.304, bf16[1,2048,12288]{2,1,0:T(8,128)(2,1)} %all-gather.19.cloned.1.call-done, f32[128,2048]{1,0:T(8,128)S(1)} %get-tuple-element.1031, ...), kind=kOutput, calls=%fused_computation.94 | convolution fusion | flops 6446383104 | bytes 70264320 | tf_op jit(solution)/shard_map/dot_general | solution.py:184
  918.2 12.0 dynamic-slice_bitcast_fusion
  930.2 15.3 multiply_multiply_fusion.2
  945.5 25.0 %fusion.230 = (f32[2048]{0:T(1024)}, f32[128]{0:T(128)S(1)}, f32[128]{0:T(128)}, f32[128,2048]{1,0:T(8,128)}) fusion(f32[2,128,2048]{2,1,0:T(8,128)S(1)} %fusion.183, s32[]{:T(128)} %min.37, f32[128]{0:T(128)S(1)} %fusion.304, f32[2048]{0:T(1024)S(1)} %bitcast.897, s32[]{:T(128)} %min.39, bf16[1,2048,12288]{2,1,0:T(8,128)(2,1)} %all-gather.19.cloned.1.call-done, ...), kind=kOutput, calls=%fused_computation.336 | convolution fusion | flops 6447691776 | bytes 59786760 | tf_op jit(solution)/shard_map/dot_general | solution.py:82
  1086.5 34.6 %reduce-scatter.19.cloned.1.call-done = bf16[128,1024]{1,0:T(8,128)(2,1)} async-done(((bf16[1024,1024]{1,0:T(8,128)(2,1)}), bf16[128,1024]{1,0:T(8,128)(2,1)}) %reduce-scatter.19.cloned.1.call-update) | async-done | bytes 262160 | tf_op jit(solution)/shard_map/reduce_scatter | solution.py:249
  1121.1 14.2 fusion.226
  1154.4 12.0 collective-permute-done.2
  1169.3 17.0 multiply_multiply_fusion.1
  1186.4 25.3 %fusion.222 = (f32[2048]{0:T(1024)}, f32[128]{0:T(128)S(1)}, f32[128]{0:T(128)S(1)}, f32[128,2048]{1,0:T(8,128)}) fusion(f32[2,128,2048]{2,1,0:T(8,128)S(1)} %fusion.183, s32[]{:T(128)} %min.39, f32[128]{0:T(128)S(1)} %fusion.306, f32[2048]{0:T(1024)S(1)} %bitcast.899, s32[]{:T(128)} %min.41, bf16[1,2048,12288]{2,1,0:T(8,128)(2,1)} %all-gather.19.cloned.1.call-done, ...), kind=kOutput, calls=%fused_computation.320 | convolution fusion | flops 6447691776 | bytes 59786760 | tf_op jit(solution)/shard_map/dot_general | solution.py:82
  1216.0 7.1 fusion.133
  1257.5 7.2 bitcast_convert_fusion.5
  1298.1 27.9 %reduce-scatter.21.cloned.1.call-done = bf16[128,1024]{1,0:T(8,128)(2,1)} async-done(((bf16[1024,1024]{1,0:T(8,128)(2,1)}), bf16[128,1024]{1,0:T(8,128)(2,1)}) %reduce-scatter.21.cloned.1.call-update) | async-done | bytes 262160 | tf_op jit(solution)/shard_map/reduce_scatter | solution.py:249
  1326.0 14.2 fusion.218
  1350.1 20.9 collective-permute-done.3
  1374.9 15.4 multiply_multiply_fusion
  1390.3 29.1 %fusion.214 = (f32[2048]{0:T(1024)}, f32[128]{0:T(128)S(1)}, f32[128,2048]{1,0:T(8,128)S(1)}) fusion(f32[2,128,2048]{2,1,0:T(8,128)S(1)} %fusion.183, s32[]{:T(128)} %min.41, f32[128]{0:T(128)S(1)} %fusion.308, f32[2048]{0:T(1024)S(1)} %bitcast.901, bf16[1,2048,12288]{2,1,0:T(8,128)(2,1)} %all-gather.19.cloned.1.call-done, ...), kind=kOutput, calls=%fused_computation.304 | convolution fusion | flops 6447167488 | bytes 58737668 | tf_op jit(solution)/shard_map/dot_general | solution.py:82
  1506.6 20.7 reduce-scatter.23.cloned.1.call-done
  1529.5 10.5 bitcast_convert_fusion.2
  1540.1 8.5 fusion.167
  1556.6 13.7 bitcast_convert_fusion.1
  1593.8 24.9 bitcast_convert_fusion
  1618.7 103.6 %reduce-scatter.25.cloned.1.call-done = bf16[256,4096]{1,0:T(8,128)(2,1)} async-done(((bf16[2048,4096]{1,0:T(8,128)(2,1)}), bf16[256,4096]{1,0:T(8,128)(2,1)}) %reduce-scatter.25.cloned.1.call-update) | async-done | bytes 2097168 | tf_op jit(solution)/shard_map/reduce_scatter | solution.py:293
  1722.3 161.0 %reduce-scatter.29.cloned.1.call-done = bf16[768,2048]{1,0:T(8,128)(2,1)} async-done(((bf16[6144,2048]{1,0:T(8,128)(2,1)}), bf16[768,2048]{1,0:T(8,128)(2,1)}) %reduce-scatter.29.cloned.1.call-update) | async-done | bytes 3145744 | tf_op jit(solution)/shard_map/reduce_scatter | solution.py:311
  1883.3 289.8 %reduce-scatter.37.cloned.1.call-done = bf16[256,12288]{1,0:T(8,128)(2,1)} async-done(((bf16[2048,12288]{1,0:T(8,128)(2,1)}), bf16[256,12288]{1,0:T(8,128)(2,1)}) %reduce-scatter.37.cloned.1.call-update) | async-done | bytes 6291472
  2174.9 12.6 fusion.145
  2191.1 13.6 fusion.210
  2204.8 23.0 all-reduce.38
  2238.4 228.4 %all-reduce.43.cloned.1.call-done = (bf16[1,256,4096]{2,1,0:T(8,128)(2,1)}, bf16[1,256,2048]{2,1,0:T(8,128)(2,1)}, bf16[1,256,12288]{2,1,0:T(8,128)(2,1)}, bf16[1,768,2048]{2,1,0:T(8,128)(2,1)}) async-done(((bf16[1,256,4096]{2,1,0:T(8,128)(2,1)}, bf16[1,256,2048]{2,1,0:T(8,128)(2,1)}, bf16[1,256,12288]{2,1,0:T(8,128)(2,1)}, bf16[1,768,2048]{2,1,0:T(8,128)(2,1)}), (bf16[1,256,4096]{2,1,0:T(8,128)(2,1)}, ...) | async-done | bytes 12582928 | tf_op jit(solution)/shard_map/psum | solution.py:324
  (869 shorter events, 590.8 us)
Async XLA Ops:
  7.2 95.4 %all-gather.11.cloned.1.call-start = ((), (), s32[]{:S(2)}) async-start(), calls=%async_computation.10 | async-start | bytes 18874368 | tf_op jit(solution)/shard_map/all_gather | solution.py:353
  7.9 97.2 %copy-start.17 = (bf16[1,2,1,128,2048]{4,3,2,1,0:T(8,128)(2,1)S(1)}, bf16[1,2,1,128,2048]{4,3,2,1,0:T(8,128)(2,1)}, u32[]{:S(2)}) copy-start(bf16[1,2,1,128,2048]{4,3,2,1,0:T(8,128)(2,1)} %param.135) | copy-start | bytes 3145732
  7.9 139.4 %all-gather.15.cloned.1.call-start = ((), (), s32[]{:S(2)}) async-start(), calls=%async_computation.12 | async-start | bytes 2359296 | tf_op jit(solution)/shard_map/all_gather | solution.py:170
  18.6 777.8 %copy-start.109 = (f32[1,2048]{1,0:T(1,128)}, f32[1,2048]{1,0:T(1,128)S(1)}, u32[]{:S(2)}) copy-start(f32[1,2048]{1,0:T(1,128)S(1)} %mul.1993) | copy-start | bytes 24580
  37.0 84.9 %copy-start.177 = (s32[1024]{0:T(1024)}, s32[1024]{0:T(1024)S(1)}, u32[]{:S(2)}) copy-start(s32[1024]{0:T(1024)S(1)} %get-tuple-element.842) | copy-start | bytes 12292
  37.0 85.0 %copy-start.178 = (s32[1024]{0:T(1024)}, s32[1024]{0:T(1024)S(1)}, u32[]{:S(2)}) copy-start(s32[1024]{0:T(1024)S(1)} %get-tuple-element.1053) | copy-start | bytes 12292
  37.2 85.0 %copy-start.179 = (s32[1024]{0:T(1024)}, s32[1024]{0:T(1024)S(1)}, u32[]{:S(2)}) copy-start(s32[1024]{0:T(1024)S(1)} %get-tuple-element.857) | copy-start | bytes 12292
  37.2 85.0 %copy-start.180 = (s32[1024]{0:T(1024)}, s32[1024]{0:T(1024)S(1)}, u32[]{:S(2)}) copy-start(s32[1024]{0:T(1024)S(1)} %get-tuple-element.1057) | copy-start | bytes 12292
  37.4 84.6 %copy-start.181 = (s32[1024]{0:T(1024)}, s32[1024]{0:T(1024)S(1)}, u32[]{:S(2)}) copy-start(s32[1024]{0:T(1024)S(1)} %get-tuple-element.848) | copy-start | bytes 12292
  37.4 84.7 %copy-start.182 = (s32[1024]{0:T(1024)}, s32[1024]{0:T(1024)S(1)}, u32[]{:S(2)}) copy-start(s32[1024]{0:T(1024)S(1)} %get-tuple-element.1055) | copy-start | bytes 12292
  40.5 74.9 %copy-start.183 = (f32[128]{0:T(128)}, f32[128]{0:T(128)S(1)}, u32[]{:S(2)}) copy-start(f32[128]{0:T(128)S(1)} %add_rsqrt_fusion.11) | copy-start | bytes 1540
  41.1 75.7 %copy-start.160 = (f32[128]{0:T(128)}, f32[128]{0:T(128)S(1)}, u32[]{:S(2)}) copy-start(f32[128]{0:T(128)S(1)} %get-tuple-element.983) | copy-start | bytes 1540
  119.2 58.4 %all-gather.13.cloned.1.call-start = ((), (), s32[]{:S(2)}) async-start(), calls=%async_computation.11 | async-start | bytes 2359296 | tf_op jit(solution)/shard_map/all_gather | solution.py:176
  120.0 113.8 %all-gather.17.cloned.1.call-start = ((), (), s32[]{:S(2)}) async-start(), calls=%async_computation.13 | async-start | bytes 9437184 | tf_op jit(solution)/shard_map/all_gather | solution.py:354
  120.6 347.2 %all-gather.19.cloned.1.call-start = ((), (), s32[]{:S(2)}) async-start(), calls=%async_computation.14 | async-start | bytes 56623104 | tf_op jit(solution)/shard_map/all_gather | solution.py:359
  121.2 473.7 %all-gather.21.cloned.1.call-start = ((), (), s32[]{:S(2)}) async-start(), calls=%async_computation.15 | async-start | bytes 28311552 | tf_op jit(solution)/shard_map/all_gather | solution.py:360
  121.8 563.8 %all-gather.25.cloned.1.call-start = ((), (), s32[]{:S(2)}) async-start(), calls=%async_computation.17 | async-start | bytes 2359296 | tf_op jit(solution)/shard_map/all_gather | solution.py:170
  238.8 235.3 %copy-start.21 = (f32[128,2048]{1,0:T(8,128)}, f32[128,2048]{1,0:T(8,128)S(1)}, u32[]{:S(2)}) copy-start(f32[128,2048]{1,0:T(8,128)S(1)} %get-tuple-element.1013) | copy-start | bytes 3145732
  609.8 16.3 collective-permute-start
  645.3 70.1 %all-gather.23.cloned.1.call-start = ((), (), s32[]{:S(2)}) async-start(), calls=%async_computation.16 | async-start | bytes 2359296 | tf_op jit(solution)/shard_map/all_gather | solution.py:176
  647.5 201.6 %all-gather.29.cloned.1.call-start = ((), (), s32[]{:S(2)}) async-start(), calls=%async_computation.19 | async-start | bytes 2359296 | tf_op jit(solution)/shard_map/all_gather | solution.py:170
  730.8 32.0 %copy-start.26 = (f32[128,2048]{1,0:T(8,128)}, f32[128,2048]{1,0:T(8,128)S(1)}, u32[]{:S(2)}) copy-start(f32[128,2048]{1,0:T(8,128)S(1)} %get-tuple-element.1019) | copy-start | bytes 3145732
  762.8 33.7 %slice-start = ((s8[16777216]{0:T(1024)(128)(4,1)}), s8[4194304]{0:T(1024)(128)(4,1)S(1)}, s32[]{:S(2)}) async-start(s8[16777216]{0:T(1024)(128)(4,1)} %bitcast.843), calls=%async_computation.31 | async-start | bytes 8388608
  762.8 33.7 %slice-start.1 = ((s8[16777216]{0:T(1024)(128)(4,1)}), s8[4194304]{0:T(1024)(128)(4,1)S(1)}, s32[]{:S(2)}) async-start(s8[16777216]{0:T(1024)(128)(4,1)} %bitcast.843), calls=%async_computation.32 | async-start | bytes 8388608
  762.8 33.7 %slice-start.2 = ((s8[16777216]{0:T(1024)(128)(4,1)}), s8[4194304]{0:T(1024)(128)(4,1)S(1)}, s32[]{:S(2)}) async-start(s8[16777216]{0:T(1024)(128)(4,1)} %bitcast.843), calls=%async_computation.33 | async-start | bytes 8388608
  776.7 16.5 collective-permute-start.1
  806.3 69.7 %all-gather.27.cloned.1.call-start = ((), (), s32[]{:S(2)}) async-start(), calls=%async_computation.18 | async-start | bytes 2359296 | tf_op jit(solution)/shard_map/all_gather | solution.py:176
  829.3 246.5 %reduce-scatter.31.cloned.1.call-start = ((), (), s32[]{:S(2)}) async-start(), calls=%async_computation.26 | async-start | bytes 2359296
  986.9 37.0 %copy-start.148 = (f32[128,8,2]{0,2,1:T(2,128)}, f32[128,8,2]{0,2,1:T(2,128)S(1)}, u32[]{:S(2)}) copy-start(f32[128,8,2]{0,2,1:T(2,128)S(1)} %get-tuple-element.958) | copy-start | bytes 24580
  986.9 245.5 %copy-start.146 = (f32[128,8,2]{0,2,1:T(2,128)}, f32[128,8,2]{0,2,1:T(2,128)S(1)}, u32[]{:S(2)}) copy-start(f32[128,8,2]{0,2,1:T(2,128)S(1)} %get-tuple-element.957) | copy-start | bytes 24580
  1034.6 86.5 %reduce-scatter.19.cloned.1.call-start = ((), (), s32[]{:S(2)}) async-start(), calls=%async_computation.20 | async-start | bytes 2359296 | tf_op jit(solution)/shard_map/reduce_scatter | solution.py:249
  1058.5 228.7 %reduce-scatter.33.cloned.1.call-start = ((), (), s32[]{:S(2)}) async-start(), calls=%async_computation.27 | async-start | bytes 2359296
  1082.0 39.1 %copy-start.110 = (f32[1,2048]{1,0:T(1,128)S(1)}, f32[1,2048]{1,0:T(1,128)}, u32[]{:S(2)}) copy-start(f32[1,2048]{1,0:T(1,128)} %copy-done.109) | copy-start | bytes 24580
  1082.0 39.1 %copy-start.189 = (f32[128]{0:T(128)S(1)}, f32[128]{0:T(128)}, u32[]{:S(2)}) copy-start(f32[128]{0:T(128)} %fusion.305) | copy-start | bytes 1540
  1138.4 28.0 %collective-permute-start.2 = (bf16[128,2048]{1,0:T(8,128)(2,1)}, bf16[128,2048]{1,0:T(8,128)(2,1)}, u32[]{:S(2)}, u32[]{:S(2)}) collective-permute-start(bf16[128,2048]{1,0:T(8,128)(2,1)} %get-tuple-element.889), channel_id=1, source_target_pairs={{16,0},{17,1},{18,2},{19,3},{20,4},{21,5},{22,6},{23,7},{24,8},{25... | collective-permute-start | bytes 1572872 | tf_op jit(solution)/shard_map/ppermute | solution.py:22
  1242.1 83.9 %reduce-scatter.21.cloned.1.call-start = ((), (), s32[]{:S(2)}) async-start(), calls=%async_computation.21 | async-start | bytes 2359296 | tf_op jit(solution)/shard_map/reduce_scatter | solution.py:249
  1268.7 229.3 %reduce-scatter.35.cloned.1.call-start = ((), (), s32[]{:S(2)}) async-start(), calls=%async_computation.28 | async-start | bytes 2359296
  1343.3 27.7 %collective-permute-start.3 = (bf16[128,2048]{1,0:T(8,128)(2,1)S(1)}, bf16[128,2048]{1,0:T(8,128)(2,1)S(1)}, u32[]{:S(2)}, u32[]{:S(2)}) collective-permute-start(bf16[128,2048]{1,0:T(8,128)(2,1)S(1)} %get-tuple-element.887), channel_id=1, source_target_pairs={{16,0},{17,1},{18,2},{19,3},{20,4},{21,5},{22,6},{23,7},{24,8},{25... | collective-permute-start | bytes 1572872 | tf_op jit(solution)/shard_map/ppermute | solution.py:22
  1344.6 30.3 %slice-start.8 = ((s8[6291456]{0:T(1024)(128)(4,1)}), s8[4194304]{0:T(1024)(128)(4,1)S(1)}, s32[]{:S(2)}) async-start(s8[6291456]{0:T(1024)(128)(4,1)} %bitcast.887), calls=%async_computation.39 | async-start | bytes 8388608
  1344.7 30.3 %slice-start.9 = ((s8[6291456]{0:T(1024)(128)(4,1)}), s8[2097152]{0:T(1024)(128)(4,1)S(1)}, s32[]{:S(2)}) async-start(s8[6291456]{0:T(1024)(128)(4,1)} %bitcast.887), calls=%async_computation.40 | async-start | bytes 4194304
  1444.0 83.3 %reduce-scatter.23.cloned.1.call-start = ((), (), s32[]{:S(2)}) async-start(), calls=%async_computation.22 | async-start | bytes 2359296 | tf_op jit(solution)/shard_map/reduce_scatter | solution.py:249
  1452.5 166.2 %reduce-scatter.27.cloned.1.call-start = ((), (), s32[]{:S(2)}) async-start(), calls=%async_computation.24 | async-start | bytes 9437184 | tf_op jit(solution)/shard_map/reduce_scatter | solution.py:299
  1465.2 257.1 %reduce-scatter.25.cloned.1.call-start = ((), (), s32[]{:S(2)}) async-start(), calls=%async_computation.23 | async-start | bytes 18874368 | tf_op jit(solution)/shard_map/reduce_scatter | solution.py:293
  1506.6 33.5 %copy-start.101 = (f32[16,8,8,128]{3,1,2,0:T(8,128)}, f32[16,8,8,128]{3,1,2,0:T(8,128)S(1)}, u32[]{:S(2)}) copy-start(f32[16,8,8,128]{3,1,2,0:T(8,128)S(1)} %copy.653) | copy-start | bytes 1572868
  1540.1 343.2 %reduce-scatter.29.cloned.1.call-start = ((), (), s32[]{:S(2)}) async-start(), calls=%async_computation.25 | async-start | bytes 28311552 | tf_op jit(solution)/shard_map/reduce_scatter | solution.py:311
  1570.4 602.7 %reduce-scatter.37.cloned.1.call-start = ((), (), s32[]{:S(2)}) async-start(), calls=%async_computation.29 | async-start | bytes 56623104
  1618.6 848.1 %all-reduce.43.cloned.1.call-start = ((), (), s32[]{:S(2)}) async-start(), calls=%async_computation.30 | async-start | bytes 25165824 | tf_op jit(solution)/shard_map/psum | solution.py:324
  2191.1 43.6 %copy-start.55 = (f32[128,2048]{1,0:T(8,128)S(1)}, f32[128,2048]{1,0:T(8,128)}, u32[]{:S(2)}) copy-start(f32[128,2048]{1,0:T(8,128)} %copy-done.54) | copy-start | bytes 3145732
  (189 other events, 1004.1 us)
Sparse Core Ops, SparseCore 0:
  9.9 92.6 all-gather.10
  119.3 27.8 all-gather.14
  149.7 27.8 all-gather.12
  179.4 54.3 all-gather.16
  235.6 232.1 all-gather.18
  469.6 125.3 all-gather.20
  645.4 40.1 all-gather.24
  687.5 27.8 all-gather.22
  806.5 39.9 all-gather.28
  848.2 27.8 all-gather.26
  1034.7 41.0 reduce-scatter.30
  1079.8 41.2 reduce-scatter.18
  1242.2 38.4 reduce-scatter.32
  1284.7 41.2 reduce-scatter.20
  1444.1 38.4 reduce-scatter.34
  1486.0 41.2 reduce-scatter.22
  1531.2 71.2 reduce-scatter.26
  1606.3 115.9 reduce-scatter.24
  1726.3 156.8 reduce-scatter.28
  1887.2 285.8 reduce-scatter.36
  2175.9 290.8 all-reduce.42
where the time goes:
time: 2500 us; the launch traced here: 2490 us
  waiting for transfers between devices  1430 us (57%)
  matrix products  498 us (20%)
  local copies, waits for them, and re-layouts  239 us (10%)
  other arithmetic  224 us (9%)
  blocking collectives  61.1 us (2%)
    unnamed x25, waiting for transfers between devices  292 us
    all_gather x1, waiting for transfers between devices, body(): lax.all_gather(expand_weight, 'fsdp', axis=1, tiled=True)  229 us
    psum x1, waiting for transfers between devices, reduce_grads(): lax.psum(heads_gradient, 'rep').astype(jnp.float32)  228 us
    dot_general x12, matrix products, times_transposed(): lax.dot_general(left_side, right_side, (((1,), (1,)), ((), ())), preferre...  190 us
    reduce_scatter x1, waiting for transfers between devices, reduce_grads(): lax.psum_scatter(product_term(hidden, upstream_b).astype(jnp.bfloat16), '...  161 us
    select_n x48, other arithmetic, body(): jnp.where(is_live, buffer.at[micro_slot].set(current), buffer)  116 us
    unnamed x484, local copies, waits for them, and re-layouts  105 us
    reduce_scatter x1, waiting for transfers between devices, reduce_grads(): lax.psum_scatter(product_term(normal_a, grad_projected_b).astype(jnp.bflo...  104 us
  transfers between devices with their start and end apart: 25, of which 21 were waited for; matrix products, arithmetic and copies ran while one was open for 18% of the time, Pallas kernels for 0%

commit v1 on v0

--- a/solution.py
+++ b/solution.py
@@ -1,8 +1,11 @@
+import functools
 import math
 
 import jax
 import jax.numpy as jnp
 from jax import lax
+from jax.experimental import pallas as pl
+from jax.experimental.pallas import tpu as pltpu
 from jax.sharding import PartitionSpec as P
 
 FF = 6144
@@ -14,6 +17,7 @@
 NORM_EPS = 1e-06
 ROPE_BASE = 1000000.0
 MASKED_SCORE = -1e30
+PLANE = 8
 
 
 def from_behind(array, axis, by):
@@ -458,9 +462,1110 @@
     )
 
 
+MESH = pl.DeviceIdType.MESH
+MERGED = QUERY_HEADS // KEY_VALUE_HEADS * HEAD_SIZE
+JOINT = MERGED + 2 * HEAD_SIZE
+VMEM_BYTES = 63 * 2**20
+
+
+def mm(left, right):
+    return jnp.dot(left, right, preferred_element_type=jnp.float32)
+
+
+def mm_t(left, right):
+    return lax.dot_general(
+        left, right, (((1,), (1,)), ((), ())), preferred_element_type=jnp.float32
+    )
+
+
+def t_mm(left, right):
+    return lax.dot_general(
+        left, right, (((0,), (0,)), ((), ())), preferred_element_type=jnp.float32
+    )
+
+
+def remote(src, dst, send, recv, device):
+    return pltpu.make_async_remote_copy(
+        src_ref=src,
+        dst_ref=dst,
+        send_sem=send,
+        recv_sem=recv,
+        device_id=device,
+        device_id_type=MESH,
+    )
+
+
+class Place:
+    def __init__(self):
+        self.index = lax.axis_index("fsdp")
+        self.core = lax.rem(self.index, 2)
+        self.chip = lax.div(self.index, 2)
+        self.x = lax.rem(self.chip, 2)
+        self.y = lax.div(self.chip, 2)
+        self.x_peer = {"fsdp": self.index + 2 - 4 * self.x}
+        self.y_peer = {"fsdp": self.index + 4 - 8 * self.y}
+        self.core_peer = {"fsdp": self.index + 1 - 2 * self.core}
+        self.section = lax.axis_index("section")
+        self.section_peer = {"section": 1 - self.section}
+
+    def chip_at(self, rel):
+        x, y = self.x, self.y
+        if rel in (1, 3):
+            x = 1 - x
+        if rel in (2, 3):
+            y = 1 - y
+        return 2 * y + x
+
+    def greet(self):
+        barrier = pltpu.get_barrier_semaphore()
+        peers = (self.x_peer, self.y_peer, self.core_peer, self.section_peer)
+        for peer in peers:
+            pl.semaphore_signal(barrier, inc=1, device_id=peer, device_id_type=MESH)
+        pl.semaphore_wait(barrier, len(peers))
+
+
+class Gather:
+    def __init__(self, place, full, send, recv, rows):
+        half = rows // 2
+
+        def span(rel, part=None):
+            first = (2 * place.chip_at(rel) + place.core) * rows
+            if part is None:
+                return pl.ds(pl.multiple_of(first, rows), rows)
+            return pl.ds(pl.multiple_of(first + part * half, half), half)
+
+        def copy(at, piece, peer):
+            block = full.at[piece]
+            return remote(block, block, send.at[at], recv.at[at], peer)
+
+        self.copies = [
+            copy(0, span(0, 1), place.x_peer),
+            copy(1, span(0, 0), place.x_peer),
+            copy(2, span(0, 0), place.y_peer),
+            copy(3, span(0, 1), place.y_peer),
+            copy(4, span(0), place.core_peer),
+            copy(5, span(1, 1), place.y_peer),
+            copy(6, span(2, 0), place.x_peer),
+            copy(7, span(1), place.core_peer),
+            copy(8, span(2), place.core_peer),
+            copy(9, span(3), place.core_peer),
+        ]
+
+    def start(self):
+        for at in (0, 2, 4, 1, 3):
+            self.copies[at].start()
+
+    def relay(self):
+        self.copies[0].wait_recv()
+        self.copies[5].start()
+        self.copies[2].wait_recv()
+        self.copies[6].start()
+
+    def near(self):
+        self.copies[1].wait_recv()
+        self.copies[7].start()
+        self.copies[3].wait_recv()
+        self.copies[8].start()
+
+    def far(self):
+        self.copies[5].wait_recv()
+        self.copies[6].wait_recv()
+        self.copies[9].start()
+
+    def wait(self, at):
+        self.copies[at].wait_recv()
+
+    def finish(self):
+        for entry in self.copies:
+            entry.wait_send()
+
+    def over_blocks(self, block):
+        self.start()
+        self.wait(4)
+        block(0)
+        self.relay()
+        self.near()
+        self.wait(7)
+        block(1)
+        self.wait(8)
+        block(2)
+        self.far()
+        self.wait(9)
+        block(3)
+
+
+class Scatter:
+    def __init__(self, place, held, to_core, from_core, to_x, to_y, from_x, from_y, send, recv, rows):
+        self.place, self.held, self.to_core, self.from_core = place, held, to_core, from_core
+        self.to_x, self.to_y, self.from_x, self.from_y = to_x, to_y, from_x, from_y
+        self.rows, self.half = rows, rows // 2
+
+        def copy(at, src, dst, peer):
+            return remote(src, dst, send.at[at], recv.at[at], peer)
+
+        self.copies = [
+            copy(rel, to_core.at[rel], from_core.at[rel], place.core_peer) for rel in range(4)
+        ] + [
+            copy(4, to_x.at[0], from_x.at[0], place.x_peer),
+            copy(5, to_y.at[0], from_y.at[0], place.y_peer),
+            copy(6, to_x.at[1], from_x.at[1], place.x_peer),
+            copy(7, to_y.at[1], from_y.at[1], place.y_peer),
+            copy(8, to_y.at[2], from_y.at[2], place.y_peer),
+            copy(9, to_x.at[2], from_x.at[2], place.x_peer),
+        ]
+
+    def put(self, rel, product, width):
+        step, rows, mine = 512, self.rows, self.place.core == 0
+
+        @pl.loop(0, width // step)
+        def _(at):
+            columns = pl.ds(pl.multiple_of(at * step, step), step)
+            value = product(columns)
+            low, high = value[:rows], value[rows:]
+            self.held[rel, :, columns] = jnp.where(mine, low, high)
+            self.to_core[rel, :, columns] = jnp.where(mine, high, low).astype(jnp.bfloat16)
+
+        self.copies[rel].start()
+
+    def pair(self, rel):
+        self.copies[rel].wait_recv()
+        half, held = self.half, self.held
+
+        @pl.loop(0, self.rows // 16)
+        def _(at):
+            span = pl.ds(pl.multiple_of(at * 16, 16), 16)
+            held[rel, span, :] += self.from_core[rel, span, :].astype(jnp.float32)
+
+        if rel == 3:
+            self.to_x[0] = held[3, :half].astype(jnp.bfloat16)
+            self.copies[4].start()
+            self.to_y[0] = held[3, half:].astype(jnp.bfloat16)
+            self.copies[5].start()
+        if rel == 1:
+            self.to_x[1] = held[1, :half].astype(jnp.bfloat16)
+            self.copies[6].start()
+        if rel == 2:
+            self.to_y[1] = held[2, half:].astype(jnp.bfloat16)
+            self.copies[7].start()
+
+    def relay(self):
+        half, held = self.half, self.held
+        self.copies[4].wait_recv()
+        self.to_y[2] = (held[2, :half] + self.from_x[0].astype(jnp.float32)).astype(jnp.bfloat16)
+        self.copies[8].start()
+        self.copies[5].wait_recv()
+        self.to_x[2] = (held[1, half:] + self.from_y[0].astype(jnp.float32)).astype(jnp.bfloat16)
+        self.copies[9].start()
+
+    def total(self, add):
+        for at in (6, 7, 8, 9):
+            self.copies[at].wait_recv()
+        count = self.half // 16
+
+        @pl.loop(0, count)
+        def _(at):
+            span = pl.ds(pl.multiple_of(at * 16, 16), 16)
+            low = self.held[0, span, :] + self.from_x[1, span, :].astype(jnp.float32)
+            add(span, low + self.from_y[2, span, :].astype(jnp.float32))
+
+        @pl.loop(0, count)
+        def _(at):
+            span = pl.ds(pl.multiple_of(at * 16, 16), 16)
+            below = pl.ds(pl.multiple_of(self.half + at * 16, 16), 16)
+            high = self.held[0, below, :] + self.from_y[1, span, :].astype(jnp.float32)
+            add(below, high + self.from_x[2, span, :].astype(jnp.float32))
+
+        for entry in self.copies:
+            entry.wait_send()
+
+
+def by_rows(count, body):
+    @pl.loop(0, count // 16)
+    def _(at):
+        body(pl.ds(pl.multiple_of(at * 16, 16), 16))
+
+
+def inverse_size(values):
+    return lax.rsqrt(jnp.mean(values * values, axis=-1, keepdims=True) + NORM_EPS)
+
+
+def norm_back(values, gain, upstream):
+    size = inverse_size(values)
+    scaled_up = upstream * gain
+    back = size * scaled_up - values * (
+        size * size * size * jnp.mean(values * scaled_up, axis=-1, keepdims=True)
+    )
+    return back, upstream * values * size
+
+
+def turn(values, cosine, sine):
+    return values * cosine + pltpu.roll(values, HEAD_SIZE // 2, 1) * sine
+
+
+def turn_back(values, cosine, sine):
+    return values * cosine + pltpu.roll(values * sine, HEAD_SIZE // 2, 1)
+
+
+def probabilities(queries, keys, first_keys, first_row):
+    scores = mm_t(queries, keys) * HEAD_SIZE ** (-0.5)
+    key_index = lax.broadcasted_iota(jnp.int32, scores.shape, 1)
+    row_index = first_row + lax.broadcasted_iota(jnp.int32, scores.shape, 0)
+    allowed = (key_index >= first_keys) & (key_index <= row_index)
+    scores = jnp.where(allowed, scores, MASKED_SCORE)
+    powers = jnp.exp(scores - jnp.max(scores, axis=-1, keepdims=True))
+    return powers / jnp.sum(powers, axis=-1, keepdims=True)
+
+
+def forward_kernel(
+    rows,
+    own_ref,
+    gains_ref,
+    head_gain_ref,
+    cos_ref,
+    sin_ref,
+    first_ref,
+    heads_w,
+    merge_w,
+    expand_w,
+    reduce_w,
+    out_results,
+    out_inputs,
+    out_normal_a,
+    out_projected,
+    out_heads,
+    out_mixed,
+    out_middle,
+    out_normal_b,
+    out_joined,
+    out_hidden,
+    wh,
+    wm,
+    we,
+    wr,
+    current,
+    arrived,
+    full_a,
+    full_b,
+    cosine,
+    sine,
+    first_key,
+    projected,
+    heads,
+    mixed,
+    joined,
+    hidden,
+    held,
+    to_core,
+    core_a,
+    core_b,
+    to_x,
+    to_y,
+    x_a,
+    y_a,
+    x_b,
+    y_b,
+    middle,
+    result,
+    result_b,
+    load_sem,
+    save_sem,
+    table_sem,
+    hand_send,
+    hand_recv,
+    ga_send,
+    ga_recv,
+    sa_send,
+    sa_recv,
+    gb_send,
+    gb_recv,
+    sb_send,
+    sb_recv,
+):
+    place = Place()
+    micro_count = own_ref.shape[0]
+    chip_rows = 2 * rows
+    width = current.shape[1]
+    hidden_width = wr.shape[0]
+    loads = [
+        pltpu.make_async_copy(src, dst, load_sem.at[at])
+        for at, (src, dst) in enumerate(
+            ((heads_w, wh), (merge_w, wm), (expand_w, we), (reduce_w, wr))
+        )
+    ]
+    for load in loads:
+        load.start()
+    place.greet()
+    head = place.section == 0
+    own_rows = pl.ds(pl.multiple_of(place.index * rows, rows), rows)
+
+    def block_rows(rel):
+        return pl.ds(pl.multiple_of(place.chip_at(rel) * chip_rows, chip_rows), chip_rows)
+
+    def hand(step):
+        return remote(
+            result_b, arrived.at[step], hand_send.at[step], hand_recv.at[step], place.section_peer
+        )
+
+    @pl.loop(0, micro_count + 1)
+    def _(step):
+        slot = jnp.clip(step - place.section, 0, micro_count - 1)
+        tables = [
+            pltpu.make_async_copy(src.at[slot], dst, table_sem.at[at])
+            for at, (src, dst) in enumerate(
+                ((cos_ref, cosine), (sin_ref, sine), (first_ref, first_key))
+            )
+        ]
+        for table in tables:
+            table.start()
+
+        @pl.when(head)
+        def _():
+            current[...] = own_ref[slot]
+
+        @pl.when(jnp.logical_not(head) & (step == 0))
+        def _():
+            current[...] = jnp.zeros_like(current)
+
+        @pl.when(jnp.logical_not(head) & (step > 0))
+        def _():
+            hand(step - 1).wait_recv()
+            current[...] = arrived[step - 1]
+
+        def save(at, src, dst):
+            copy = pltpu.make_async_copy(src, dst.at[slot], save_sem.at[at])
+            copy.start()
+            return copy
+
+        saves = [save(0, current, out_inputs)]
+
+        def enter(span):
+            values = current[span, :].astype(jnp.float32)
+            base = pl.multiple_of(place.index * rows + span.start, 16)
+            full_a[pl.ds(base, 16), :] = (
+                values * inverse_size(values) * gains_ref[0:1, :]
+            ).astype(jnp.bfloat16)
+
+        by_rows(rows, enter)
+        for table in tables:
+            table.wait()
+
+        @pl.when(step == 0)
+        def _():
+            loads[0].wait()
+
+        gather = Gather(place, full_a, ga_send, ga_recv, rows)
+
+        def heads_block(rel):
+            span = block_rows(rel)
+            values = mm(full_a[span, :], wh[...])
+            projected[span, :] = values
+            for at in range(3):
+                columns = pl.ds(at * HEAD_SIZE, HEAD_SIZE)
+                one = values[:, at * HEAD_SIZE : (at + 1) * HEAD_SIZE]
+                gain = head_gain_ref[0:1, :] if at < 2 else head_gain_ref[1:2, :]
+                heads[span, columns] = turn(
+                    one * inverse_size(one) * gain, cosine[span, :], sine[span, :]
+                ).astype(jnp.bfloat16)
+            heads[span, 3 * HEAD_SIZE :] = values[:, 3 * HEAD_SIZE :].astype(jnp.bfloat16)
+
+        gather.over_blocks(heads_block)
+        saves += [
+            save(1, full_a, out_normal_a),
+            save(2, projected, out_projected),
+            save(3, heads, out_heads),
+        ]
+
+        @pl.when(step == 0)
+        def _():
+            loads[1].wait()
+
+        scatter = Scatter(
+            place, held, to_core, core_a, to_x, to_y, x_a, y_a, sa_send, sa_recv, rows
+        )
+
+        def attend_block(rel):
+            first_row = place.chip_at(rel) * chip_rows
+            span = block_rows(rel)
+            for at in range(2):
+                columns = pl.ds(at * HEAD_SIZE, HEAD_SIZE)
+                probs = probabilities(
+                    heads[span, columns],
+                    heads[:, 2 * HEAD_SIZE : 3 * HEAD_SIZE],
+                    first_key[span, :],
+                    first_row,
+                )
+                mixed[span, columns] = mm(
+                    probs.astype(jnp.bfloat16), heads[:, 3 * HEAD_SIZE :]
+                ).astype(jnp.bfloat16)
+            scatter.put(rel, lambda columns: mm(mixed[span, :], wm[:, columns]), width)
+
+        attend_block(3)
+        attend_block(2)
+        scatter.pair(3)
+        attend_block(1)
+        scatter.pair(2)
+        attend_block(0)
+        scatter.pair(1)
+        saves.append(save(4, mixed, out_mixed))
+        scatter.relay()
+        scatter.pair(0)
+
+        def residual(span, value):
+            values = value + current[span, :].astype(jnp.float32)
+            middle[span, :] = values
+            base = pl.multiple_of(place.index * rows + span.start, 16)
+            full_b[pl.ds(base, 16), :] = (
+                values * inverse_size(values) * gains_ref[1:2, :]
+            ).astype(jnp.bfloat16)
+
+        scatter.total(residual)
+        gather.finish()
+        saves.append(save(5, middle, out_middle))
+        for copy in saves[:5]:
+            copy.wait()
+
+        @pl.when(step == 0)
+        def _():
+            loads[2].wait()
+            loads[3].wait()
+
+        gather_b = Gather(place, full_b, gb_send, gb_recv, rows)
+        scatter_b = Scatter(
+            place, held, to_core, core_b, to_x, to_y, x_b, y_b, sb_send, sb_recv, rows
+        )
+
+        joined_copies = {}
+
+        def feed_block(rel):
+            span = block_rows(rel)
+            stage = joined.at[rel % 2]
+            if rel >= 2:
+                joined_copies[rel - 2].wait()
+
+            @pl.loop(0, hidden_width // 256)
+            def _(at):
+                columns = pl.ds(pl.multiple_of(at * 256, 256), 256)
+                later = pl.ds(pl.multiple_of(hidden_width + at * 256, 256), 256)
+                gate = mm(full_b[span, :], we[:, columns])
+                up = mm(full_b[span, :], we[:, later])
+                stage[:, columns] = gate
+                stage[:, later] = up
+                hidden[span, columns] = (gate * jax.nn.sigmoid(gate) * up).astype(jnp.bfloat16)
+
+            copy = pltpu.make_async_copy(stage, out_joined.at[slot, span], save_sem.at[8 + rel % 2])
+            copy.start()
+            joined_copies[rel] = copy
+            scatter_b.put(rel, lambda columns: mm(hidden[span, :], wr[:, columns]), width)
+            if rel >= 1:
+                scatter_b.pair(rel - 1)
+
+        gather_b.over_blocks(feed_block)
+        later_saves = [save(6, full_b, out_normal_b), save(7, hidden, out_hidden)]
+        scatter_b.pair(3)
+        scatter_b.relay()
+
+        @pl.when(head & (step > 0))
+        def _():
+            hand(step - 1).wait_send()
+
+        def finish(span, value):
+            values = value + middle[span, :]
+            result[span, :] = values
+            result_b[span, :] = values.astype(jnp.bfloat16)
+
+        scatter_b.total(finish)
+
+        @pl.when(head & (step < micro_count))
+        def _():
+            hand(step).start()
+
+        final = save(0, result, out_results)
+        gather_b.finish()
+        for copy in [saves[5]] + later_saves + [joined_copies[2], joined_copies[3], final]:
+            copy.wait()
+
+
+def backward_kernel(
+    rows,
+    own_ref,
+    gains_ref,
+    head_gain_ref,
+    cos_ref,
+    sin_ref,
+    first_ref,
+    heads_w,
+    merge_w,
+    expand_w,
+    reduce_w,
+    in_inputs,
+    in_projected,
+    in_heads,
+    in_middle,
+    in_joined,
+    out_results,
+    out_upstream,
+    out_grad_joined,
+    out_grad_middle,
+    out_grad_projected,
+    out_gains,
+    out_head_gain,
+    wh,
+    wm,
+    we,
+    wr,
+    arrived,
+    current,
+    full_a,
+    full_b,
+    cosine,
+    sine,
+    first_key,
+    projected,
+    heads,
+    grad_mixed,
+    grad_queries,
+    grad_keys,
+    grad_values,
+    grad_projected,
+    joined,
+    grad_joined,
+    held,
+    to_core,
+    core_a,
+    core_b,
+    to_x,
+    to_y,
+    x_a,
+    y_a,
+    x_b,
+    y_b,
+    middle,
+    inputs,
+    result,
+    load_sem,
+    save_sem,
+    table_sem,
+    joined_sem,
+    hand_send,
+    hand_recv,
+    ga_send,
+    ga_recv,
+    sa_send,
+    sa_recv,
+    gb_send,
+    gb_recv,
+    sb_send,
+    sb_recv,
+):
+    place = Place()
+    micro_count = own_ref.shape[0]
+    chip_rows = 2 * rows
+    width = current.shape[1]
+    hidden_width = wr.shape[0]
+    length = full_a.shape[0]
+    loads = [
+        pltpu.make_async_copy(src, dst, load_sem.at[at])
+        for at, (src, dst) in enumerate(
+            ((reduce_w, wr), (expand_w, we), (merge_w, wm), (heads_w, wh))
+        )
+    ]
+    for load in loads:
+        load.start()
+    place.greet()
+    head = place.section == 0
+    own_rows = pl.ds(pl.multiple_of(place.index * rows, rows), rows)
+
+    def block_rows(rel):
+        return pl.ds(pl.multiple_of(place.chip_at(rel) * chip_rows, chip_rows), chip_rows)
+
+    def hand(step):
+        return remote(
+            current, arrived.at[step], hand_send.at[step], hand_recv.at[step], place.section_peer
+        )
+
+    @pl.loop(0, micro_count + 1)
+    def _(step):
+        slot = jnp.clip(step - 1 + place.section, 0, micro_count - 1)
+        tables = [
+            pltpu.make_async_copy(src.at[slot], dst, table_sem.at[at])
+            for at, (src, dst) in enumerate(
+                (
+                    (in_middle, middle),
+                    (cos_ref, cosine),
+                    (sin_ref, sine),
+                    (first_ref, first_key),
+                    (in_projected, projected),
+                    (in_heads, heads),
+                    (in_inputs, inputs),
+                )
+            )
+        ]
+        for table in tables:
+            table.start()
+
+        def joined_load(rel):
+            return pltpu.make_async_copy(
+                in_joined.at[slot, block_rows(rel)], joined.at[rel % 2], joined_sem.at[rel % 2]
+            )
+
+        joined_load(0).start()
+        joined_load(1).start()
+
+        @pl.when(jnp.logical_not(head) & (step > 0))
+        def _():
+            hand(step - 1).wait_send()
+
+        @pl.when(jnp.logical_not(head))
+        def _():
+            current[...] = own_ref[slot]
+
+        @pl.when(head & (step == 0))
+        def _():
+            current[...] = jnp.zeros_like(current)
+
+        @pl.when(head & (step > 0))
+        def _():
+            hand(step - 1).wait_recv()
+            current[...] = arrived[step - 1]
+
+        full_a[own_rows, :] = current[...]
+
+        def save(at, src, dst):
+            copy = pltpu.make_async_copy(src, dst.at[slot], save_sem.at[at])
+            copy.start()
+            return copy
+
+        @pl.when(step == 0)
+        def _():
+            loads[0].wait()
+            loads[1].wait()
+
+        gather = Gather(place, full_a, ga_send, ga_recv, rows)
+        scatter = Scatter(
+            place, held, to_core, core_a, to_x, to_y, x_a, y_a, sa_send, sa_recv, rows
+        )
+        grad_copies = {}
+
+        def feed_block(rel):
+            span = block_rows(rel)
+            stage, out = joined.at[rel % 2], grad_joined.at[rel % 2]
+            joined_load(rel).wait()
+            if rel >= 2:
+                grad_copies[rel - 2].wait()
+
+            @pl.loop(0, hidden_width // 256)
+            def _(at):
+                columns = pl.ds(pl.multiple_of(at * 256, 256), 256)
+                later = pl.ds(pl.multiple_of(hidden_width + at * 256, 256), 256)
+                grad = mm_t(full_a[span, :], wr[columns, :])
+                gate, up = stage[:, columns], stage[:, later]
+                sigmoid = jax.nn.sigmoid(gate)
+                unit = gate * sigmoid
+                out[:, columns] = (grad * up * (sigmoid + unit * (1.0 - sigmoid))).astype(
+                    jnp.bfloat16
+                )
+                out[:, later] = (grad * unit).astype(jnp.bfloat16)
+
+            if rel < 2:
+                joined_load(rel + 2).start()
+            copy = pltpu.make_async_copy(
+                out, out_grad_joined.at[slot, span], save_sem.at[8 + rel % 2]
+            )
+            copy.start()
+            grad_copies[rel] = copy
+            scatter.put(rel, lambda columns: mm_t(out[...], we[columns, :]), width)
+            if rel >= 1:
+                scatter.pair(rel - 1)
+
+        gather.over_blocks(feed_block)
+        upstream_save = save(0, full_a, out_upstream)
+        scatter.pair(3)
+        scatter.relay()
+        for table in tables:
+            table.wait()
+        out_gains[slot, 1:2, :] = jnp.zeros((1, width), jnp.float32)
+
+        def feed_norm(span, value):
+            back, gain_term = norm_back(middle[span, :], gains_ref[1:2, :], value)
+            out_gains[slot, 1:2, :] += jnp.sum(gain_term, axis=0, keepdims=True)
+            total = back + current[span, :].astype(jnp.float32)
+            result[span, :] = total
+            base = pl.multiple_of(place.index * rows + span.start, 16)
+            full_b[pl.ds(base, 16), :] = total.astype(jnp.bfloat16)
+
+        scatter.total(feed_norm)
+        gather.finish()
+        for copy in (upstream_save, grad_copies[2], grad_copies[3]):
+            copy.wait()
+
+        @pl.when(step == 0)
+        def _():
+            loads[2].wait()
+            loads[3].wait()
+
+        gather_b = Gather(place, full_b, gb_send, gb_recv, rows)
+        scatter_b = Scatter(
+            place, held, to_core, core_b, to_x, to_y, x_b, y_b, sb_send, sb_recv, rows
+        )
+
+        def mixed_block(rel):
+            span = block_rows(rel)
+            grad_mixed[span, :] = mm_t(full_b[span, :], wm[...]).astype(jnp.bfloat16)
+
+        gather_b.over_blocks(mixed_block)
+        middle_save = save(1, full_b, out_grad_middle)
+        grad_keys[...] = jnp.zeros_like(grad_keys)
+        grad_values[...] = jnp.zeros_like(grad_values)
+
+        for block in range(length // chip_rows):
+            span = pl.ds(block * chip_rows, chip_rows)
+            seen = (block + 1) * chip_rows
+            keys = heads[:seen, 2 * HEAD_SIZE : 3 * HEAD_SIZE]
+            values = heads[:seen, 3 * HEAD_SIZE :]
+            for at in range(2):
+                columns = pl.ds(at * HEAD_SIZE, HEAD_SIZE)
+                queries = heads[span, columns]
+                grad = grad_mixed[span, columns]
+                probs = probabilities(queries, keys, first_key[span, :], block * chip_rows)
+                grad_probs = mm_t(grad, values)
+                grad_scores = (
+                    probs * (grad_probs - jnp.sum(probs * grad_probs, axis=-1, keepdims=True))
+                ).astype(jnp.bfloat16)
+                grad_queries[span, columns] = mm(grad_scores, keys) * HEAD_SIZE ** (-0.5)
+                grad_keys[:seen, :] += t_mm(grad_scores, queries) * HEAD_SIZE ** (-0.5)
+                grad_values[:seen, :] += t_mm(probs.astype(jnp.bfloat16), grad)
+
+        out_head_gain[slot] = jnp.zeros_like(out_head_gain[slot])
+
+        def project_block(rel):
+            span = block_rows(rel)
+            for at in range(3):
+                columns = pl.ds(at * HEAD_SIZE, HEAD_SIZE)
+                which = 0 if at < 2 else 1
+                upstream = grad_queries[span, columns] if at < 2 else grad_keys[span, :]
+                back, gain_term = norm_back(
+                    projected[span, columns],
+                    head_gain_ref[which : which + 1, :],
+                    turn_back(upstream, cosine[span, :], sine[span, :]),
+                )
+                out_head_gain[slot, which : which + 1, :] += jnp.sum(
+                    gain_term, axis=0, keepdims=True
+                )
+                grad_projected[span, columns] = back.astype(jnp.bfloat16)
+            grad_projected[span, 3 * HEAD_SIZE :] = grad_values[span, :].astype(jnp.bfloat16)
+            scatter_b.put(rel, lambda columns: mm_t(grad_projected[span, :], wh[columns, :]), width)
+
+        project_block(3)
+        project_block(2)
+        scatter_b.pair(3)
+        project_block(1)
+        scatter_b.pair(2)
+        project_block(0)
+        scatter_b.pair(1)
+        projected_save = save(2, grad_projected, out_grad_projected)
+        scatter_b.relay()
+        scatter_b.pair(0)
+        out_gains[slot, 0:1, :] = jnp.zeros((1, width), jnp.float32)
+
+        def mixer_norm(span, value):
+            back, gain_term = norm_back(
+                inputs[span, :].astype(jnp.float32), gains_ref[0:1, :], value
+            )
+            out_gains[slot, 0:1, :] += jnp.sum(gain_term, axis=0, keepdims=True)
+            total = back + result[span, :]
+            result[span, :] = total
+            current[span, :] = total.astype(jnp.bfloat16)
+
+        scatter_b.total(mixer_norm)
+
+        @pl.when(jnp.logical_not(head) & (step < micro_count))
+        def _():
+            hand(step).start()
+
+        final = save(3, result, out_results)
+        gather_b.finish()
+        for copy in (middle_save, projected_save, final):
+            copy.wait()
+
+
+def sems(*counts):
+    return [pltpu.SemaphoreType.DMA((count,)) for count in counts]
+
+
+def vmem(*shapes):
+    return [pltpu.VMEM(shape, dtype) for *shape, dtype in shapes]
+
+
+def any_spec():
+    return pl.BlockSpec(memory_space=pl.ANY)
+
+
+def vmem_spec():
+    return pl.BlockSpec(memory_space=pltpu.VMEM)
+
+
+def exchange_buffers(rows, width):
+    half, b16 = rows // 2, jnp.bfloat16
+    return vmem(
+        (4, rows, width, jnp.float32),
+        (4, rows, width, b16),
+        (4, rows, width, b16),
+        (4, rows, width, b16),
+        *(((3, half, width, b16),) * 6),
+    )
+
+
+def run_forward(own, gains, head_gain, cosine, sine, first_key, weights):
+    micro, rows, width = own.shape
+    length = cosine.shape[1]
+    hidden_width = weights[3].shape[0]
+    f32, b16 = jnp.float32, jnp.bfloat16
+    shape = jax.ShapeDtypeStruct
+    return pl.pallas_call(
+        functools.partial(forward_kernel, rows),
+        out_shape=(
+            shape((micro, rows, width), f32),
+            shape((micro, rows, width), b16),
+            shape((micro, length, width), b16),
+            shape((micro, length, JOINT), f32),
+            shape((micro, length, JOINT), b16),
+            shape((micro, length, MERGED), b16),
+            shape((micro, rows, width), f32),
+            shape((micro, length, width), b16),
+            shape((micro, length, 2 * hidden_width), f32),
+            shape((micro, length, hidden_width), b16),
+        ),
+        in_specs=[vmem_spec()] * 3 + [any_spec()] * 7,
+        out_specs=(any_spec(),) * 10,
+        scratch_shapes=vmem(
+            (width, JOINT, b16),
+            (MERGED, width, b16),
+            (width, 2 * hidden_width, b16),
+            (hidden_width, width, b16),
+            (rows, width, b16),
+            (micro, rows, width, b16),
+            (length, width, b16),
+            (length, width, b16),
+            (length, HEAD_SIZE, f32),
+            (length, HEAD_SIZE, f32),
+            (length, 1, jnp.int32),
+            (length, JOINT, f32),
+            (length, JOINT, b16),
+            (length, MERGED, b16),
+            (2, 2 * rows, 2 * hidden_width, f32),
+            (length, hidden_width, b16),
+        )
+        + exchange_buffers(rows, width)
+        + vmem((rows, width, f32), (rows, width, f32), (rows, width, b16))
+        + sems(4, 10, 3, micro, micro, *((10,) * 8)),
+        compiler_params=pltpu.CompilerParams(
+            collective_id=1, has_side_effects=True, vmem_limit_bytes=VMEM_BYTES
+        ),
+    )(own, gains, head_gain, cosine, sine, first_key, *weights)
+
+
+def run_backward(own, gains, head_gain, cosine, sine, first_key, weights, saved):
+    micro, rows, width = own.shape
+    length = cosine.shape[1]
+    hidden_width = weights[3].shape[0]
+    f32, b16 = jnp.float32, jnp.bfloat16
+    shape = jax.ShapeDtypeStruct
+    return pl.pallas_call(
+        functools.partial(backward_kernel, rows),
+        out_shape=(
+            shape((micro, rows, width), f32),
+            shape((micro, length, width), b16),
+            shape((micro, length, 2 * hidden_width), b16),
+            shape((micro, length, width), b16),
+            shape((micro, length, JOINT), b16),
+            shape((micro, 2, width), f32),
+            shape((micro, 2, HEAD_SIZE), f32),
+        ),
+        in_specs=[vmem_spec()] * 3 + [any_spec()] * 12,
+        out_specs=(any_spec(),) * 5 + (vmem_spec(),) * 2,
+        scratch_shapes=vmem(
+            (width, JOINT, b16),
+            (MERGED, width, b16),
+            (width, 2 * hidden_width, b16),
+            (hidden_width, width, b16),
+            (micro, rows, width, b16),
+            (rows, width, b16),
+            (length, width, b16),
+            (length, width, b16),
+            (length, HEAD_SIZE, f32),
+            (length, HEAD_SIZE, f32),
+            (length, 1, jnp.int32),
+            (length, JOINT, f32),
+            (length, JOINT, b16),
+            (length, MERGED, b16),
+            (length, MERGED, f32),
+            (length, HEAD_SIZE, f32),
+            (length, HEAD_SIZE, f32),
+            (length, JOINT, b16),
+            (2, 2 * rows, 2 * hidden_width, f32),
+            (2, 2 * rows, 2 * hidden_width, b16),
+        )
+        + exchange_buffers(rows, width)
+        + vmem((rows, width, f32), (rows, width, b16), (rows, width, f32))
+        + sems(4, 10, 7, 2, micro, micro, *((10,) * 8)),
+        compiler_params=pltpu.CompilerParams(
+            collective_id=2, has_side_effects=True, vmem_limit_bytes=VMEM_BYTES
+        ),
+    )(own, gains, head_gain, cosine, sine, first_key, *weights, *saved)
+
+
+def position_tables(lengths, length):
+    document_index, positions = places(lengths, length)
+    half_width = HEAD_SIZE // 2
+    frequency = jnp.exp(
+        jnp.arange(half_width, dtype=jnp.float32) * (-2.0 * math.log(ROPE_BASE) / HEAD_SIZE)
+    )
+    angles = positions.astype(jnp.float32)[:, None] * frequency[None, :]
+    cosine, sine = jnp.cos(angles), jnp.sin(angles)
+    first_key = jnp.arange(length, dtype=jnp.int32) - positions
+    return (
+        jnp.concatenate([cosine, cosine], axis=-1),
+        jnp.concatenate([-sine, sine], axis=-1),
+        first_key[:, None],
+    )
+
+
+def tensor_parallel_body(
+    section_inputs,
+    doc_lengths,
+    mixer_gain,
+    heads_weight,
+    merge_weight,
+    head_gain,
+    feed_gain,
+    expand_weight,
+    reduce_weight,
+):
+    shards = lax.axis_size("fsdp")
+    own = section_inputs[0, :, 0]
+    micro, rows, width = own.shape
+    length = rows * shards
+    depth = heads_weight.shape[1]
+    hidden_width = reduce_weight.shape[1]
+    query_width = QUERY_HEADS * HEAD_SIZE
+
+    def by_shard(weight, parts):
+        return weight.reshape(weight.shape[0], parts, shards, -1).swapaxes(0, 2)
+
+    heads_parts = heads_weight[0]
+    pieces = jnp.concatenate(
+        [
+            heads_parts[:, :query_width].reshape(depth, shards, MERGED),
+            heads_parts[:, query_width : query_width + shards * HEAD_SIZE].reshape(
+                depth, shards, HEAD_SIZE
+            ),
+            heads_parts[:, query_width + shards * HEAD_SIZE :].reshape(depth, shards, HEAD_SIZE),
+        ],
+        axis=-1,
+    ).swapaxes(0, 1)
+    expand_pieces = (
+        expand_weight[0]
+        .reshape(depth, 2, shards, hidden_width)
+        .transpose(2, 0, 1, 3)
+        .reshape(shards, depth, 2 * hidden_width)
+    )
+    heads_full = lax.all_to_all(pieces, "fsdp", 0, 0, tiled=True).reshape(width, JOINT)
+    expand_full = lax.all_to_all(expand_pieces, "fsdp", 0, 0, tiled=True).reshape(
+        width, 2 * hidden_width
+    )
+    weights = (heads_full, merge_weight[0], expand_full, reduce_weight[0])
+    all_gains = lax.all_gather(
+        jnp.concatenate([mixer_gain[0], feed_gain[0], head_gain[0]]), "fsdp", axis=0
+    ).astype(jnp.float32)
+    gains = jnp.stack(
+        [all_gains[:, :depth].reshape(-1), all_gains[:, depth : 2 * depth].reshape(-1)]
+    )
+    head_gains = all_gains[:, 2 * depth :].reshape(2, HEAD_SIZE)
+    tables = [position_tables(doc_lengths[at, 0], length) for at in range(micro)]
+    cosine, sine, first_key = (jnp.stack(entry) for entry in zip(*tables))
+
+    (
+        results,
+        inputs,
+        normal_a,
+        projected,
+        heads,
+        mixed,
+        middle,
+        normal_b,
+        joined,
+        hidden,
+    ) = run_forward(own, gains, head_gains, cosine, sine, first_key, weights)
+    grad_results, upstream, grad_joined, grad_middle, grad_projected, gain_terms, head_terms = (
+        run_backward(
+            own,
+            gains,
+            head_gains,
+            cosine,
+            sine,
+            first_key,
+            weights,
+            (inputs, projected, heads, middle, joined),
+        )
+    )
+
+    def product(left, right):
+        return product_term(
+            left.reshape(micro * length, -1), right.reshape(micro * length, -1)
+        ).astype(jnp.bfloat16)
+
+    def with_replica(term):
+        other = lax.ppermute(term, "rep", [(0, 1), (1, 0)])
+        return term.astype(jnp.float32) + other.astype(jnp.float32)
+
+    def to_owners(term):
+        return lax.all_to_all(term.reshape(shards, depth, -1), "fsdp", 0, 0, tiled=True)
+
+    grad_reduce = with_replica(product(hidden, upstream))
+    expand_term = to_owners(product(normal_b, grad_joined))
+    grad_expand = with_replica(
+        expand_term.reshape(shards, depth, 2, hidden_width)
+        .transpose(1, 2, 0, 3)
+        .reshape(depth, 2 * shards * hidden_width)
+    )
+    grad_merge = with_replica(product(mixed, grad_middle))
+    heads_term = to_owners(product(normal_a, grad_projected)).swapaxes(0, 1)
+    grad_heads = with_replica(
+        jnp.concatenate(
+            [
+                heads_term[:, :, :MERGED].reshape(depth, -1),
+                heads_term[:, :, MERGED : MERGED + HEAD_SIZE].reshape(depth, -1),
+                heads_term[:, :, MERGED + HEAD_SIZE :].reshape(depth, -1),
+            ],
+            axis=-1,
+        )
+    )
+    terms = jnp.concatenate(
+        [jnp.sum(gain_terms, axis=0).reshape(-1), jnp.sum(head_terms, axis=0).reshape(-1)]
+    )
+    sums = lax.psum(terms, ("fsdp", "rep"))
+    index = lax.axis_index("fsdp")
+
+    def own_part(first, count):
+        return lax.dynamic_slice_in_dim(sums, first + index * count, count)[None]
+
+    head_count = head_gain.shape[1]
+    return (
+        jnp.where(lax.axis_index("section") == 0, grad_results, results)[None, :, None],
+        own_part(0, depth),
+        grad_heads[None],
+        grad_merge[None],
+        own_part(2 * width, head_count),
+        own_part(width, depth),
+        grad_expand[None],
+        grad_reduce[None],
+    )
+
+
 def solution(mesh):
+    plane = mesh.shape["fsdp"] == PLANE
     return jax.shard_map(
-        body,
+        tensor_parallel_body if plane else body,
         mesh=mesh,
         in_specs=(
             P("section", None, "rep", "fsdp", None),

time: 2500 us -> 1260 us (0.50)
  waiting for transfers between devices: 1430 us -> 95.7 us
  Pallas kernels: 0 us -> 629 us
  matrix products: 498 us -> 41.6 us
  blocking collectives: 61.1 us -> 344 us
  other arithmetic: 224 us -> 36.1 us
  local copies, waits for them, and re-layouts: 239 us -> 63.6 us
    pallas_call x0 -> x2, Pallas kernels: none -> 629 us  [the longest x1 337 us: run_backward(): pl.pallas_call(functools.partial(backward_kernel, rows), out_shape=(shape...]
    all_gather x10 -> x0, waiting for transfers between devices: 516 us -> none  [the longest x1 229 us: body(): lax.all_gather(expand_weight, 'fsdp', axis=1, tiled=True)]
    dot_general x45 -> x0, matrix products: 442 us -> none  [the longest x12 190 us: times_transposed(): lax.dot_general(left_side, right_side, (((1,), (1,)), ((), ())), preferre...]
    reduce_scatter x6 -> x0, waiting for transfers between devices: 348 us -> none  [the longest x1 161 us: reduce_grads(): lax.psum_scatter(product_term(hidden, upstream_b).astype(jnp.bfloat16), '...]
    unnamed x25 -> x0, waiting for transfers between devices: 292 us -> none
    psum x1, blocking collectives: 4.98 us -> 258 us  [tensor_parallel_body(): sums = lax.psum(terms, ('fsdp', 'rep'))]
    psum x1 -> x0, waiting for transfers between devices: 228 us -> none  [reduce_grads(): lax.psum(heads_gradient, 'rep').astype(jnp.float32)]
    select_n x51 -> x0, other arithmetic: 122 us -> none  [the longest x48 116 us: body(): jnp.where(is_live, buffer.at[micro_slot].set(current), buffer)]
  transfers between devices with their start and end apart: 25 -> 8, of which waited for: 21 -> 2; matrix products, arithmetic and copies ran while one was open for 18% -> 8% of each run, Pallas kernels for 0% -> 0%
where the time goes in v1:
time: 1260 us; the launch traced here: 1250 us
  Pallas kernels  629 us (50%)
  blocking collectives  344 us (27%)
  waiting for transfers between devices  95.7 us (8%)
  local copies, waits for them, and re-layouts  63.6 us (5%)
  matrix products  41.6 us (3%)
  other arithmetic  36.1 us (3%)
  starting transfers between devices  35.7 us (3%)
    pallas_call x1, Pallas kernels, run_backward(): pl.pallas_call(functools.partial(backward_kernel, rows), out_shape=(shape...  337 us
    pallas_call x1, Pallas kernels, run_forward(): pl.pallas_call(functools.partial(forward_kernel, rows), out_shape=(shape(...  292 us
    psum x1, blocking collectives, tensor_parallel_body(): sums = lax.psum(terms, ('fsdp', 'rep'))  258 us
    unnamed x1, blocking collectives  85.9 us
    all_to_all x2, waiting for transfers between devices, to_owners(): lax.all_to_all(term.reshape(shards, depth, -1), 'fsdp', 0, 0, tiled=True)  62.1 us
    dot_general x4, matrix products, product_term(): lax.dot_general(left_side, right_side, (((0,), (0,)), ((), ())), preferre...  41.6 us
    ppermute x4, waiting for transfers between devices, with_replica(): other = lax.ppermute(term, 'rep', [(0, 1), (1, 0)])  33.5 us
  transfers between devices with their start and end apart: 8, of which 2 were waited for; matrix products, arithmetic and copies ran while one was open for 8% of the time, Pallas kernels for 0%

profile of v1, /device:TPU:0, one launch (start us, length us, event | category | flops | bytes accessed | tf_op | source)
XLA Modules:
  0.0 1248.2 jit_solution(11463985910356716033)
XLA Ops:
  0.6 1.3 slice_bitcast_fusion.4
  1.9 1.3 slice.47
  3.3 0.2 copy_bitcast_fusion.1
  3.5 1.5 maximum_bitcast_fusion
  5.1 5.2 all-to-all-start
  10.2 4.7 copy.89
  14.9 7.6 copy.67
  22.5 14.4 %reshape.188 = bf16[8,256,1536]{2,1,0:T(8,128)(2,1)} reshape(bf16[8,256,2,768]{3,2,1,0:T(2,128)(2,1)} %copy.67) | data formatting | bytes 12582912 | tf_op jit(solution)/shard_map/reshape | solution.py:1470
  36.9 1.3 copy-done
  38.3 4.7 all-to-all-start.1
  43.5 0.2 copy.63
  43.7 0.2 copy.62
  44.0 0.6 dynamic-slice
  45.3 0.2 dynamic-update-slice
  45.5 85.9 %all-reduce = bf16[4352]{0:T(1024)(128)(2,1)S(1)} all-reduce(bf16[4352]{0:T(1024)(128)(2,1)S(1)} %dynamic-update-slice), channel_id=2, replica_groups=mesh['section'=2,'fsdp'=8,'rep'=2] {'fsdp'}, use_global_device_ids=true, to_apply=%add | all-reduce | flops 4352 | bytes 17408
  131.5 0.6 reshape.179.head_gain_ref
  132.2 3.7 fusion.1
  135.9 0.2 maximum_bitcast_fusion.1
  136.3 0.2 maximum_bitcast_fusion.3
  136.8 1.0 pad_maximum_fusion.1.sin_ref
  137.8 1.0 pad_maximum_fusion.cos_ref
  139.0 1.0 pad_add_fusion.first_ref
  140.0 0.6 pad_maximum_fusion.3.gains_ref
  140.6 292.3 %shard_map.152 = (f32[2,128,2048]{2,1,0:T(8,128)}, bf16[2,128,2048]{2,1,0:T(8,128)(2,1)}, bf16[2,1024,2048]{2,1,0:T(8,128)(2,1)}, f32[2,1024,512]{2,1,0:T(8,128)...) custom-call(bf16[2,128,2048]{2,1,0:T(8,128)(2,1)} %bitcast.126, ...), custom_call_target="tpu_custom_call" | custom-call | tf_op jit(solution)/shard_map/pallas_call | solution.py:1324
  433.0 336.9 %shard_map.153 = (f32[2,128,2048]{2,1,0:T(8,128)}, bf16[2,1024,2048]{2,1,0:T(8,128)(2,1)}, bf16[2,1024,1536]{2,1,0:T(8,128)(2,1)}, bf16[2,1024,2048]{2,1,0:T(8,1...) custom-call(bf16[2,128,2048]{2,1,0:T(8,128)(2,1)} %bitcast.127, ...), custom_call_target="tpu_custom_call" | custom-call | tf_op jit(solution)/shard_map/pallas_call | solution.py:1373
  769.8 19.1 %bitcast_convert_fusion = bf16[2048,1536]{1,0:T(8,128)(2,1)} fusion(bf16[2,1024,2048]{2,1,0:T(8,128)(2,1)} %get-tuple-element.38, bf16[2,1024,1536]{2,1,0:T(8,128)(2,1)} %get-tuple-element.39), kind=kOutput, calls=%fused_computation | convolution fusion | flops 12888047616 | bytes 20971520 | tf_op jit(solution)/shard_map/dot_general | solution.py:281
  788.9 4.9 all-to-all-start.3
  793.8 9.4 bitcast_convert_fusion.2
  803.3 62.1 %all-to-all-done.3 = bf16[8,256,1536]{2,1,0:T(8,128)(2,1)} async-done(((bf16[8,256,1536]{2,1,0:T(8,128)(2,1)}), bf16[8,256,1536]{2,1,0:T(8,128)(2,1)}, u32[]{:S(2)}, u32[]{:S(2)}) %all-to-all-start.3) | async-done | bytes 6291488 | tf_op jit(solution)/shard_map/all_to_all | solution.py:1522
  865.4 3.6 all-to-all-start.2
  869.0 13.6 %reshape.197 = bf16[8,256,2,768]{3,2,1,0:T(2,128)(2,1)} reshape(bf16[8,256,1536]{2,1,0:T(8,128)(2,1)} %all-to-all-done.3) | data formatting | bytes 12582912 | tf_op jit(solution)/shard_map/reshape | solution.py:1527
  882.6 9.5 copy.74
  892.1 5.5 copy.91
  897.6 15.2 %collective-permute-start.2 = (bf16[256,12288]{1,0:T(8,128)(2,1)}, bf16[256,12288]{1,0:T(8,128)(2,1)}, u32[]{:S(2)}, u32[]{:S(2)}) collective-permute-start(bf16[256,12288]{1,0:T(8,128)(2,1)} %bitcast.67), channel_id=1, source_target_pairs={{0,1},{1,0},{2,3},{3,2},{4,5},{5,4},{6,7},{7,6},{8,9},{9,8},{10,11... | collective-permute-start | bytes 18874376 | tf_op jit(solution)/shard_map/ppermute | solution.py:1518
  912.8 10.8 bitcast_convert_fusion.1
  923.7 2.3 fusion
  926.0 2.0 collective-permute-start.1
  928.1 258.5 %psum.7 = f32[4352]{0:T(1024)S(1)} all-reduce(f32[4352]{0:T(1024)S(1)} %pad_maximum_fusion.2), channel_id=1, replica_groups=mesh['section'=2,'fsdp'=8,'rep'=2] {'fsdp','rep'}, use_global_device_ids=true, to_apply=%region_6.7 | all-reduce | flops 4352 | bytes 34816 | tf_op jit(solution)/shard_map/psum | solution.py:1546
  1186.9 0.3 slice_bitcast_fusion.1
  1187.4 0.6 dynamic-slice_bitcast_fusion
  1188.0 0.6 fusion.3
  1188.6 0.3 copy-done.3
  1188.9 1.6 select_bitcast_fusion
  1190.5 2.9 add_bitcast_fusion.3
  1193.4 6.9 add_bitcast_fusion.1
  1200.3 33.5 %collective-permute-done = bf16[256,4096]{1,0:T(8,128)(2,1)S(1)} collective-permute-done((bf16[256,4096]{1,0:T(8,128)(2,1)S(1)}, bf16[256,4096]{1,0:T(8,128)(2,1)S(1)}, u32[]{:S(2)}, u32[]{:S(2)}) %collective-permute-start) | collective-permute-done | bytes 2097184 | tf_op jit(solution)/shard_map/ppermute | solution.py:1518
  1233.8 2.7 add_bitcast_fusion.2
  1236.5 11.5 add_bitcast_fusion
  (67 shorter events, 1.9 us)
Async XLA Ops:
  5.1 31.9 %all-to-all-start = ((bf16[8,256,512]{2,1,0:T(8,128)(2,1)}), bf16[8,256,512]{2,1,0:T(8,128)(2,1)S(1)}, u32[]{:S(2)}, u32[]{:S(2)}) async-start(bf16[8,256,512]{2,1,0:T(8,128)(2,1)} %maximum_bitcast_fusion), calls=%async_computation | async-start | bytes 4194304 | tf_op jit(solution)/shard_map/all_to_all | solution.py:1472
  36.9 6.1 copy-start.6
  36.9 7.1 copy-start.7
  36.9 7.1 copy-start.8
  36.9 7.1 copy-start.12
  36.9 8.4 copy-start.9
  36.9 1.3 copy-start
  38.3 102.4 %all-to-all-start.1 = ((bf16[8,256,1536]{2,1,0:T(8,128)(2,1)}), bf16[8,256,1536]{2,1,0:T(8,128)(2,1)}, u32[]{:S(2)}, u32[]{:S(2)}) async-start(bf16[8,256,1536]{2,1,0:T(8,128)(2,1)} %reshape.188), calls=%async_computation.1 | async-start | bytes 12582912 | tf_op jit(solution)/shard_map/all_to_all | solution.py:1473
  788.9 4.9 copy-start.11
  788.9 76.5 %all-to-all-start.3 = ((bf16[8,256,1536]{2,1,0:T(8,128)(2,1)}), bf16[8,256,1536]{2,1,0:T(8,128)(2,1)}, u32[]{:S(2)}, u32[]{:S(2)}) async-start(bf16[8,256,1536]{2,1,0:T(8,128)(2,1)} %bitcast.122), calls=%async_computation.3 | async-start | bytes 12582912 | tf_op jit(solution)/shard_map/all_to_all | solution.py:1522
  865.4 321.2 %all-to-all-start.2 = ((bf16[8,256,512]{2,1,0:T(8,128)(2,1)}), bf16[8,256,512]{2,1,0:T(8,128)(2,1)S(1)}, u32[]{:S(2)}, u32[]{:S(2)}) async-start(bf16[8,256,512]{2,1,0:T(8,128)(2,1)} %bitcast.132), calls=%async_computation.2 | async-start | bytes 4194304 | tf_op jit(solution)/shard_map/all_to_all | solution.py:1522
  892.1 20.7 %copy-start.10 = (bf16[2,1024,768]{2,1,0:T(8,128)(2,1)S(1)}, bf16[2,1024,768]{2,1,0:T(8,128)(2,1)}, u32[]{:S(2)}) copy-start(bf16[2,1024,768]{2,1,0:T(8,128)(2,1)} %get-tuple-element.40) | copy-start | bytes 9437188
  892.1 31.5 %slice-start = ((s8[8388608]{0:T(1024)(128)(4,1)}), s8[4194304]{0:T(1024)(128)(4,1)S(1)}, s32[]{:S(2)}) async-start(s8[8388608]{0:T(1024)(128)(4,1)} %bitcast.113), calls=%async_computation.4 | async-start | bytes 8388608
  897.6 338.9 %collective-permute-start.2 = (bf16[256,12288]{1,0:T(8,128)(2,1)}, bf16[256,12288]{1,0:T(8,128)(2,1)}, u32[]{:S(2)}, u32[]{:S(2)}) collective-permute-start(bf16[256,12288]{1,0:T(8,128)(2,1)} %bitcast.67), channel_id=1, source_target_pairs={{0,1},{1,0},{2,3},{3,2},{4,5},{5,4},{6,7},{7,6},{8,9},{9,8},{10,11... | collective-permute-start | bytes 18874376 | tf_op jit(solution)/shard_map/ppermute | solution.py:1518
  912.8 10.8 slice-start.1
  912.8 10.8 copy-start.1
  923.6 269.8 %collective-permute-start.3 = (bf16[768,2048]{1,0:T(8,128)(2,1)}, bf16[768,2048]{1,0:T(8,128)(2,1)}, u32[]{:S(2)}, u32[]{:S(2)}) collective-permute-start(bf16[768,2048]{1,0:T(8,128)(2,1)} %bitcast_convert_fusion.1), channel_id=1, source_target_pairs={{0,1},{1,0},{2,3},{3,2},{4,5},{5,4},{6,7},{7,6},{8,9},{9,8},{10,11... | collective-permute-start | bytes 9437192 | tf_op jit(solution)/shard_map/ppermute | solution.py:1518
  923.6 4.4 copy-start.4
  923.6 4.4 copy-start.5
  926.0 264.5 %collective-permute-start.1 = (bf16[256,2048]{1,0:T(8,128)(2,1)S(1)}, bf16[256,2048]{1,0:T(8,128)(2,1)}, u32[]{:S(2)}, u32[]{:S(2)}) collective-permute-start(bf16[256,2048]{1,0:T(8,128)(2,1)S(1)} %fusion), channel_id=1, source_target_pairs={{0,1},{1,0},{2,3},{3,2},{4,5},{5,4},{6,7},{7,6},{8,9},{9,8},{10,11... | collective-permute-start | bytes 3145736 | tf_op jit(solution)/shard_map/ppermute | solution.py:1518
  1186.7 2.0 copy-start.2
  1186.7 2.2 copy-start.3
  1187.3 46.5 %collective-permute-start = (bf16[256,4096]{1,0:T(8,128)(2,1)S(1)}, bf16[256,4096]{1,0:T(8,128)(2,1)S(1)}, u32[]{:S(2)}, u32[]{:S(2)}) collective-permute-start(bf16[256,4096]{1,0:T(8,128)(2,1)S(1)} %bitcast_dynamic-update-slice_fusion), channel_id=1, source_target_pairs={{0,1},{1,0},{2,3},{3,2},{4,5},{5,4},{6,7},{7,6},{8,9},{9,8},{10,11... | collective-permute-start | bytes 6291464 | tf_op jit(solution)/shard_map/ppermute | solution.py:1518

commit v2 on v1

--- a/solution.py
+++ b/solution.py
@@ -507,6 +507,7 @@
         self.core_peer = {"fsdp": self.index + 1 - 2 * self.core}
         self.section = lax.axis_index("section")
         self.section_peer = {"section": 1 - self.section}
+        self.rep_peer = {"rep": 1 - lax.axis_index("rep")}
 
     def chip_at(self, rel):
         x, y = self.x, self.y
@@ -516,9 +517,15 @@
             y = 1 - y
         return 2 * y + x
 
-    def greet(self):
+    def others(self):
+        order = ((3, 0), (3, 1), (1, 0), (1, 1), (2, 0), (2, 1), (0, 1), (0, 0))
+        return [
+            (at, 2 * self.chip_at(rel) + (1 - self.core if other else self.core))
+            for at, (rel, other) in enumerate(order)
+        ]
+
+    def greet(self, peers):
         barrier = pltpu.get_barrier_semaphore()
-        peers = (self.x_peer, self.y_peer, self.core_peer, self.section_peer)
         for peer in peers:
             pl.semaphore_signal(barrier, inc=1, device_id=peer, device_id_type=MESH)
         pl.semaphore_wait(barrier, len(peers))
@@ -719,8 +726,7 @@
 def forward_kernel(
     rows,
     own_ref,
-    gains_ref,
-    head_gain_ref,
+    gain_ref,
     cos_ref,
     sin_ref,
     first_ref,
@@ -738,6 +744,11 @@
     out_normal_b,
     out_joined,
     out_hidden,
+    out_heads_w,
+    out_expand_w,
+    gains_ref,
+    head_gain_ref,
+    all_gains,
     wh,
     wm,
     we,
@@ -768,6 +779,8 @@
     result,
     result_b,
     load_sem,
+    spread_send,
+    spread_recv,
     save_sem,
     table_sem,
     hand_send,
@@ -786,21 +799,81 @@
     chip_rows = 2 * rows
     width = current.shape[1]
     hidden_width = wr.shape[0]
+    depth = heads_w.shape[0]
+    query_width, key_width = QUERY_HEADS * HEAD_SIZE, KEY_VALUE_HEADS * HEAD_SIZE
     loads = [
         pltpu.make_async_copy(src, dst, load_sem.at[at])
-        for at, (src, dst) in enumerate(
-            ((heads_w, wh), (merge_w, wm), (expand_w, we), (reduce_w, wr))
-        )
+        for at, (src, dst) in enumerate(((merge_w, wm), (reduce_w, wr)))
     ]
     for load in loads:
         load.start()
-    place.greet()
+    shard_rows = pl.ds(pl.multiple_of(place.index * depth, depth), depth)
+
+    def spread(at, device, piece, src, dst):
+        if at < 7:
+            return remote(
+                src, dst, spread_send.at[piece, at], spread_recv.at[piece, at], {"fsdp": device}
+            )
+        return pltpu.make_async_copy(src, dst, load_sem.at[2 + piece])
+
+    def columns_of(first, device, count):
+        return pl.ds(pl.multiple_of(first + device * count, 128), count)
+
+    gain_copies = [
+        spread(at, device, 0, gain_ref, all_gains.at[place.index])
+        for at, device in place.others()
+    ]
+    heads_copies, expand_copies = [], []
+    for at, device in place.others():
+        for piece, first, count, into in (
+            (1, 0, MERGED, 0),
+            (2, query_width, HEAD_SIZE, MERGED),
+            (3, query_width + key_width, HEAD_SIZE, MERGED + HEAD_SIZE),
+        ):
+            src = heads_w.at[:, columns_of(first, device, count)]
+            heads_copies.append(
+                spread(at, device, piece, src, wh.at[shard_rows, pl.ds(into, count)])
+            )
+        for piece in range(2):
+            src = expand_w.at[:, columns_of(piece * FF, device, hidden_width)]
+            expand_copies.append(
+                spread(
+                    at,
+                    device,
+                    4 + piece,
+                    src,
+                    we.at[shard_rows, pl.ds(piece * hidden_width, hidden_width)],
+                )
+            )
+
+    def arrive(copies, pieces):
+        for at, copy in enumerate(copies):
+            if at // pieces < 7:
+                copy.wait_recv()
+            else:
+                copy.wait()
+
+    heads_out = pltpu.make_async_copy(wh, out_heads_w, load_sem.at[8])
+    expand_out = pltpu.make_async_copy(we, out_expand_w, load_sem.at[9])
+    place.greet([{"fsdp": device} for _, device in place.others()[:7]] + [place.section_peer])
+    for copy in gain_copies + heads_copies:
+        copy.start()
+    arrive(gain_copies, 1)
+    for shard in range(PLANE):
+        part = slice(shard * depth, (shard + 1) * depth)
+        gains_ref[0:1, part] = all_gains[shard][:, :depth]
+        gains_ref[1:2, part] = all_gains[shard][:, depth : 2 * depth]
+    per_row = PLANE // 2
+    count = 2 * HEAD_SIZE // PLANE
+    for row in range(2):
+        head_gain_ref[row : row + 1, :] = jnp.concatenate(
+            [
+                all_gains[row * per_row + at][:, 2 * depth : 2 * depth + count]
+                for at in range(per_row)
+            ],
+            axis=1,
+        )
     head = place.section == 0
-    own_rows = pl.ds(pl.multiple_of(place.index * rows, rows), rows)
-
-    def block_rows(rel):
-        return pl.ds(pl.multiple_of(place.chip_at(rel) * chip_rows, chip_rows), chip_rows)
-
     def hand(step):
         return remote(
             result_b, arrived.at[step], hand_send.at[step], hand_recv.at[step], place.section_peer
@@ -849,14 +922,17 @@
         for table in tables:
             table.wait()
 
-        @pl.when(step == 0)
-        def _():
-            loads[0].wait()
-
         gather = Gather(place, full_a, ga_send, ga_recv, rows)
 
         def heads_block(rel):
-            span = block_rows(rel)
+            span = block_rows(place, rel, rows)
+            if rel == 0:
+
+                @pl.when(step == 0)
+                def _():
+                    arrive(heads_copies, 3)
+                    heads_out.start()
+
             values = mm(full_a[span, :], wh[...])
             projected[span, :] = values
             for at in range(3):
@@ -877,7 +953,9 @@
 
         @pl.when(step == 0)
         def _():
-            loads[1].wait()
+            for copy in expand_copies:
+                copy.start()
+            loads[0].wait()
 
         scatter = Scatter(
             place, held, to_core, core_a, to_x, to_y, x_a, y_a, sa_send, sa_recv, rows
@@ -885,7 +963,7 @@
 
         def attend_block(rel):
             first_row = place.chip_at(rel) * chip_rows
-            span = block_rows(rel)
+            span = block_rows(place, rel, rows)
             for at in range(2):
                 columns = pl.ds(at * HEAD_SIZE, HEAD_SIZE)
                 probs = probabilities(
@@ -926,8 +1004,9 @@
 
         @pl.when(step == 0)
         def _():
-            loads[2].wait()
-            loads[3].wait()
+            arrive(expand_copies, 2)
+            expand_out.start()
+            loads[1].wait()
 
         gather_b = Gather(place, full_b, gb_send, gb_recv, rows)
         scatter_b = Scatter(
@@ -937,7 +1016,7 @@
         joined_copies = {}
 
         def feed_block(rel):
-            span = block_rows(rel)
+            span = block_rows(place, rel, rows)
             stage = joined.at[rel % 2]
             if rel >= 2:
                 joined_copies[rel - 2].wait()
@@ -983,6 +1062,12 @@
         gather_b.finish()
         for copy in [saves[5]] + later_saves + [joined_copies[2], joined_copies[3], final]:
             copy.wait()
+
+    heads_out.wait()
+    expand_out.wait()
+    for pieces, copies in ((1, gain_copies), (3, heads_copies), (2, expand_copies)):
+        for copy in copies[: 7 * pieces]:
+            copy.wait_send()
 
 
 def backward_kernel(
@@ -1062,7 +1147,6 @@
     chip_rows = 2 * rows
     width = current.shape[1]
     hidden_width = wr.shape[0]
-    length = full_a.shape[0]
     loads = [
         pltpu.make_async_copy(src, dst, load_sem.at[at])
         for at, (src, dst) in enumerate(
@@ -1071,12 +1155,9 @@
     ]
     for load in loads:
         load.start()
-    place.greet()
+    place.greet((place.x_peer, place.y_peer, place.core_peer, place.section_peer))
     head = place.section == 0
     own_rows = pl.ds(pl.multiple_of(place.index * rows, rows), rows)
-
-    def block_rows(rel):
-        return pl.ds(pl.multiple_of(place.chip_at(rel) * chip_rows, chip_rows), chip_rows)
 
     def hand(step):
         return remote(
@@ -1105,7 +1186,7 @@
 
         def joined_load(rel):
             return pltpu.make_async_copy(
-                in_joined.at[slot, block_rows(rel)], joined.at[rel % 2], joined_sem.at[rel % 2]
+                in_joined.at[slot, block_rows(place, rel, rows)], joined.at[rel % 2], joined_sem.at[rel % 2]
             )
 
         joined_load(0).start()
@@ -1147,7 +1228,7 @@
         grad_copies = {}
 
         def feed_block(rel):
-            span = block_rows(rel)
+            span = block_rows(place, rel, rows)
             stage, out = joined.at[rel % 2], grad_joined.at[rel % 2]
             joined_load(rel).wait()
             if rel >= 2:
@@ -1203,89 +1284,444 @@
             loads[2].wait()
             loads[3].wait()
 
-        gather_b = Gather(place, full_b, gb_send, gb_recv, rows)
-        scatter_b = Scatter(
-            place, held, to_core, core_b, to_x, to_y, x_b, y_b, sb_send, sb_recv, rows
+        save_result = save(3, result, out_results)
+
+        @pl.when(step < micro_count)
+        def _():
+            save_result.wait()
+            gather_b = Gather(place, full_b, gb_send, gb_recv, rows)
+            scatter_b = Scatter(
+                place, held, to_core, core_b, to_x, to_y, x_b, y_b, sb_send, sb_recv, rows
+            )
+
+            def mixed_block(rel):
+                span = block_rows(place, rel, rows)
+                grad_mixed[span, :] = mm_t(full_b[span, :], wm[...]).astype(jnp.bfloat16)
+
+            gather_b.over_blocks(mixed_block)
+            middle_save = save(1, full_b, out_grad_middle)
+            attention_back(
+                heads, grad_mixed, first_key, grad_queries, grad_keys, grad_values, 2 * rows
+            )
+            project_back(
+                place,
+                scatter_b,
+                projected,
+                head_gain_ref,
+                cosine,
+                sine,
+                grad_queries,
+                grad_keys,
+                grad_values,
+                grad_projected,
+                out_head_gain.at[slot],
+                wh,
+                rows,
+            )
+            projected_save = save(2, grad_projected, out_grad_projected)
+            scatter_b.relay()
+            scatter_b.pair(0)
+            input_back(scatter_b, inputs, gains_ref, out_gains.at[slot], result, current)
+
+            @pl.when(jnp.logical_not(head))
+            def _():
+                hand(step).start()
+
+            final = save(3, result, out_results)
+            gather_b.finish()
+            for copy in (middle_save, projected_save, final):
+                copy.wait()
+
+        @pl.when(step == micro_count)
+        def _():
+            save_result.wait()
+
+
+def block_rows(place, rel, rows):
+    return pl.ds(pl.multiple_of(place.chip_at(rel) * 2 * rows, 2 * rows), 2 * rows)
+
+
+def attention_back(
+    heads, grad_mixed, first_key, grad_queries, grad_keys, grad_values, chip_rows
+):
+    grad_keys[...] = jnp.zeros_like(grad_keys)
+    grad_values[...] = jnp.zeros_like(grad_values)
+    for block in range(heads.shape[0] // chip_rows):
+        span = pl.ds(block * chip_rows, chip_rows)
+        seen = (block + 1) * chip_rows
+        keys = heads[:seen, 2 * HEAD_SIZE : 3 * HEAD_SIZE]
+        values = heads[:seen, 3 * HEAD_SIZE :]
+        for at in range(2):
+            columns = pl.ds(at * HEAD_SIZE, HEAD_SIZE)
+            queries = heads[span, columns]
+            grad = grad_mixed[span, columns]
+            probs = probabilities(queries, keys, first_key[span, :], block * chip_rows)
+            grad_probs = mm_t(grad, values)
+            grad_scores = (
+                probs * (grad_probs - jnp.sum(probs * grad_probs, axis=-1, keepdims=True))
+            ).astype(jnp.bfloat16)
+            grad_queries[span, columns] = mm(grad_scores, keys) * HEAD_SIZE ** (-0.5)
+            grad_keys[:seen, :] += t_mm(grad_scores, queries) * HEAD_SIZE ** (-0.5)
+            grad_values[:seen, :] += t_mm(probs.astype(jnp.bfloat16), grad)
+
+
+def project_back(
+    place,
+    scatter,
+    projected,
+    head_gain_ref,
+    cosine,
+    sine,
+    grad_queries,
+    grad_keys,
+    grad_values,
+    grad_projected,
+    out_head_gain,
+    wh,
+    rows,
+):
+    out_head_gain[...] = jnp.zeros_like(out_head_gain)
+
+    def project_block(rel):
+        span = block_rows(place, rel, rows)
+        for at in range(3):
+            columns = pl.ds(at * HEAD_SIZE, HEAD_SIZE)
+            which = 0 if at < 2 else 1
+            upstream = grad_queries[span, columns] if at < 2 else grad_keys[span, :]
+            back, gain_term = norm_back(
+                projected[span, columns],
+                head_gain_ref[which : which + 1, :],
+                turn_back(upstream, cosine[span, :], sine[span, :]),
+            )
+            out_head_gain[which : which + 1, :] += jnp.sum(gain_term, axis=0, keepdims=True)
+            grad_projected[span, columns] = back.astype(jnp.bfloat16)
+        grad_projected[span, 3 * HEAD_SIZE :] = grad_values[span, :].astype(jnp.bfloat16)
+        scatter.put(rel, lambda columns: mm_t(grad_projected[span, :], wh[columns, :]), wh.shape[0])
+
+    project_block(3)
+    project_block(2)
+    scatter.pair(3)
+    project_block(1)
+    scatter.pair(2)
+    project_block(0)
+    scatter.pair(1)
+
+
+def input_back(scatter, inputs, gains_ref, out_gains, result, result_b):
+    out_gains[0:1, :] = jnp.zeros_like(out_gains[0:1, :])
+
+    def mixer_norm(span, value):
+        back, gain_term = norm_back(inputs[span, :].astype(jnp.float32), gains_ref[0:1, :], value)
+        out_gains[0:1, :] += jnp.sum(gain_term, axis=0, keepdims=True)
+        total = back + result[span, :]
+        result[span, :] = total
+        if result_b is not None:
+            result_b[span, :] = total.astype(jnp.bfloat16)
+
+    scatter.total(mixer_norm)
+
+
+def gradient_kernel(
+    rows,
+    gains_ref,
+    head_gain_ref,
+    cos_ref,
+    sin_ref,
+    first_ref,
+    heads_w,
+    merge_w,
+    in_inputs,
+    in_projected,
+    in_heads,
+    in_result,
+    hidden_all,
+    upstream_all,
+    normal_b_all,
+    grad_joined_all,
+    mixed_all,
+    grad_middle_all,
+    normal_a_all,
+    grad_projected_all,
+    out_result,
+    own_heads,
+    other_heads,
+    own_merge,
+    other_merge,
+    own_expand,
+    other_expand,
+    own_reduce,
+    other_reduce,
+    out_gains,
+    out_head_gain,
+    wh,
+    wm,
+    full,
+    cosine,
+    sine,
+    first_key,
+    projected,
+    heads,
+    grad_mixed,
+    grad_queries,
+    grad_keys,
+    grad_values,
+    grad_projected,
+    held,
+    to_core,
+    from_core,
+    to_x,
+    to_y,
+    from_x,
+    from_y,
+    inputs,
+    result,
+    tiles,
+    turned,
+    wide,
+    narrow,
+    first_projected,
+    expand_blocks,
+    reduce_block,
+    load_sem,
+    tile_sem,
+    save_sem,
+    g_send,
+    g_recv,
+    s_send,
+    s_recv,
+    spread_send,
+    spread_recv,
+    rep_send,
+    rep_recv,
+):
+    place = Place()
+    length, width = full.shape
+    depth = wm.shape[0]
+    hidden_width = reduce_block.shape[0]
+    last = in_inputs.shape[0] - 1
+    tokens = wide.shape[0]
+    query_width, key_width = QUERY_HEADS * HEAD_SIZE, KEY_VALUE_HEADS * HEAD_SIZE
+
+    def load(at, src, dst):
+        copy = pltpu.make_async_copy(src, dst, load_sem.at[at])
+        copy.start()
+        return copy
+
+    result_load = load(0, in_result.at[last], result)
+    wide_load = load(1, upstream_all, wide)
+    others = place.others()
+    jobs = (
+        [(hidden_all, at) for at in range(hidden_width // depth)]
+        + [(normal_b_all, device) for _, device in others]
+        + [(mixed_all, 0)]
+        + [(normal_a_all, device) for _, device in others]
+    )
+
+    def tile_load(job):
+        source, at = jobs[job]
+        columns = pl.ds(pl.multiple_of(at * depth, depth), depth)
+        return pltpu.make_async_copy(
+            source.at[:, columns], tiles.at[job % 2], tile_sem.at[job % 2]
         )
 
-        def mixed_block(rel):
-            span = block_rows(rel)
-            grad_mixed[span, :] = mm_t(full_b[span, :], wm[...]).astype(jnp.bfloat16)
-
-        gather_b.over_blocks(mixed_block)
-        middle_save = save(1, full_b, out_grad_middle)
-        grad_keys[...] = jnp.zeros_like(grad_keys)
-        grad_values[...] = jnp.zeros_like(grad_values)
-
-        for block in range(length // chip_rows):
-            span = pl.ds(block * chip_rows, chip_rows)
-            seen = (block + 1) * chip_rows
-            keys = heads[:seen, 2 * HEAD_SIZE : 3 * HEAD_SIZE]
-            values = heads[:seen, 3 * HEAD_SIZE :]
-            for at in range(2):
-                columns = pl.ds(at * HEAD_SIZE, HEAD_SIZE)
-                queries = heads[span, columns]
-                grad = grad_mixed[span, columns]
-                probs = probabilities(queries, keys, first_key[span, :], block * chip_rows)
-                grad_probs = mm_t(grad, values)
-                grad_scores = (
-                    probs * (grad_probs - jnp.sum(probs * grad_probs, axis=-1, keepdims=True))
-                ).astype(jnp.bfloat16)
-                grad_queries[span, columns] = mm(grad_scores, keys) * HEAD_SIZE ** (-0.5)
-                grad_keys[:seen, :] += t_mm(grad_scores, queries) * HEAD_SIZE ** (-0.5)
-                grad_values[:seen, :] += t_mm(probs.astype(jnp.bfloat16), grad)
-
-        out_head_gain[slot] = jnp.zeros_like(out_head_gain[slot])
-
-        def project_block(rel):
-            span = block_rows(rel)
-            for at in range(3):
-                columns = pl.ds(at * HEAD_SIZE, HEAD_SIZE)
-                which = 0 if at < 2 else 1
-                upstream = grad_queries[span, columns] if at < 2 else grad_keys[span, :]
-                back, gain_term = norm_back(
-                    projected[span, columns],
-                    head_gain_ref[which : which + 1, :],
-                    turn_back(upstream, cosine[span, :], sine[span, :]),
+    def take(job):
+        tile_load(job).wait()
+
+        @pl.loop(0, tokens // 256)
+        def _(at):
+            span = pl.ds(pl.multiple_of(at * 256, 256), 256)
+            turned[:, span] = tiles[job % 2, span, :].T
+
+        if job + 2 < len(jobs):
+            tile_load(job + 2).start()
+
+    tile_load(0).start()
+    tile_load(1).start()
+    narrow_load = load(2, grad_joined_all, narrow)
+    loads = [
+        load(at + 3, src, dst)
+        for at, (src, dst) in enumerate(
+            (
+                (merge_w, wm),
+                (heads_w, wh),
+                (cos_ref.at[last], cosine),
+                (sin_ref.at[last], sine),
+                (first_ref.at[last], first_key),
+                (in_projected.at[last], projected),
+                (in_heads.at[last], heads),
+                (in_inputs.at[last], inputs),
+                (grad_projected_all.at[0], first_projected),
+            )
+        )
+    ]
+    place.greet([{"fsdp": device} for _, device in others[:7]] + [place.rep_peer])
+
+    def rep_copy(at, src, dst):
+        return remote(src, dst, rep_send.at[at], rep_recv.at[at], place.rep_peer)
+
+    def spread(at, device, piece, src, dst):
+        if at < 7:
+            return remote(
+                src, dst, spread_send.at[piece, at], spread_recv.at[piece, at], {"fsdp": device}
+            )
+        return pltpu.make_async_copy(src, dst, save_sem.at[4 + piece])
+
+    def columns_of(first, device, count):
+        return pl.ds(pl.multiple_of(first + device * count, 128), count)
+
+    result_load.wait()
+
+    def enter(span):
+        base = pl.multiple_of(place.index * rows + span.start, 16)
+        full[pl.ds(base, 16), :] = result[span, :].astype(jnp.bfloat16)
+
+    by_rows(rows, enter)
+    gather = Gather(place, full, g_send, g_recv, rows)
+    gather.start()
+
+    wide_load.wait()
+    own_saves, rep_copies = [], []
+    for at in range(hidden_width // depth):
+        take(at)
+        span = pl.ds(at * depth, depth)
+
+        @pl.loop(0, width // 512)
+        def _(chunk):
+            columns = pl.ds(pl.multiple_of(chunk * 512, 512), 512)
+            reduce_block[span, columns] = mm(turned[...], wide[:, columns]).astype(jnp.bfloat16)
+
+        copy = rep_copy(at, reduce_block.at[span], other_reduce.at[span])
+        copy.start()
+        rep_copies.append(copy)
+        copy = pltpu.make_async_copy(reduce_block.at[span], own_reduce.at[span], save_sem.at[at])
+        copy.start()
+        own_saves.append(copy)
+        if at == 0:
+            gather.relay()
+            gather.near()
+    gather.far()
+    middle_load = load(12, grad_middle_all.at[0], wide.at[pl.ds(0, length)])
+    narrow_load.wait()
+    job = hidden_width // depth
+    expand_copies, expand_reps = [], []
+    for at, device in others:
+        take(job)
+        job += 1
+
+        @pl.loop(0, narrow.shape[1] // 512)
+        def _(chunk):
+            columns = pl.ds(pl.multiple_of(chunk * 512, 512), 512)
+            expand_blocks[at, :, columns] = mm(turned[...], narrow[:, columns]).astype(
+                jnp.bfloat16
+            )
+
+        for piece in range(2):
+            src = expand_blocks.at[at, :, pl.ds(piece * hidden_width, hidden_width)]
+            first = piece * FF
+            copy = spread(
+                at,
+                device,
+                piece,
+                src,
+                own_expand.at[:, columns_of(first, place.index, hidden_width)],
+            )
+            copy.start()
+            expand_copies.append(copy)
+            theirs = columns_of(first, device, hidden_width)
+            expand_reps.append(
+                rep_copy(
+                    4 + 2 * at + piece,
+                    own_expand.at[:, theirs] if at < 7 else src,
+                    other_expand.at[:, theirs],
                 )
-                out_head_gain[slot, which : which + 1, :] += jnp.sum(
-                    gain_term, axis=0, keepdims=True
-                )
-                grad_projected[span, columns] = back.astype(jnp.bfloat16)
-            grad_projected[span, 3 * HEAD_SIZE :] = grad_values[span, :].astype(jnp.bfloat16)
-            scatter_b.put(rel, lambda columns: mm_t(grad_projected[span, :], wh[columns, :]), width)
-
-        project_block(3)
-        project_block(2)
-        scatter_b.pair(3)
-        project_block(1)
-        scatter_b.pair(2)
-        project_block(0)
-        scatter_b.pair(1)
-        projected_save = save(2, grad_projected, out_grad_projected)
-        scatter_b.relay()
-        scatter_b.pair(0)
-        out_gains[slot, 0:1, :] = jnp.zeros((1, width), jnp.float32)
-
-        def mixer_norm(span, value):
-            back, gain_term = norm_back(
-                inputs[span, :].astype(jnp.float32), gains_ref[0:1, :], value
             )
-            out_gains[slot, 0:1, :] += jnp.sum(gain_term, axis=0, keepdims=True)
-            total = back + result[span, :]
-            result[span, :] = total
-            current[span, :] = total.astype(jnp.bfloat16)
-
-        scatter_b.total(mixer_norm)
-
-        @pl.when(jnp.logical_not(head) & (step < micro_count))
-        def _():
-            hand(step).start()
-
-        final = save(3, result, out_results)
-        gather_b.finish()
-        for copy in (middle_save, projected_save, final):
-            copy.wait()
+    for copy in expand_reps[14:]:
+        copy.start()
+    for copy in loads:
+        copy.wait()
+    for rel, at in ((0, 4), (1, 7), (2, 8), (3, 9)):
+        gather.wait(at)
+        span = block_rows(place, rel, rows)
+        grad_mixed[span, :] = mm_t(full[span, :], wm[...]).astype(jnp.bfloat16)
+    attention_back(heads, grad_mixed, first_key, grad_queries, grad_keys, grad_values, 2 * rows)
+    scatter = Scatter(
+        place, held, to_core, from_core, to_x, to_y, from_x, from_y, s_send, s_recv, rows
+    )
+    project_back(
+        place,
+        scatter,
+        projected,
+        head_gain_ref,
+        cosine,
+        sine,
+        grad_queries,
+        grad_keys,
+        grad_values,
+        grad_projected,
+        out_head_gain,
+        wh,
+        rows,
+    )
+    scatter.relay()
+    scatter.pair(0)
+    input_back(scatter, inputs, gains_ref, out_gains, result, None)
+    result_save = pltpu.make_async_copy(result, out_result, save_sem.at[9])
+    result_save.start()
+
+    for at in range(14):
+        expand_copies[at].wait_recv()
+        expand_reps[at].start()
+
+    middle_load.wait()
+    take(job)
+    job += 1
+
+    @pl.loop(0, width // 512)
+    def _(chunk):
+        columns = pl.ds(pl.multiple_of(chunk * 512, 512), 512)
+        value = mm(turned[:, :length], wide[:length, columns])
+        value += mm(turned[:, length:], full[:, columns])
+        wm[:, columns] = value.astype(jnp.bfloat16)
+
+    merge_rep = rep_copy(3, wm, other_merge)
+    merge_rep.start()
+    merge_save = pltpu.make_async_copy(wm, own_merge, save_sem.at[3])
+    merge_save.start()
+    heads_copies = []
+    for at, device in others:
+        take(job)
+        job += 1
+        value = mm(turned[:, :length], first_projected[...])
+        value += mm(turned[:, length:], grad_projected[...])
+        block = pl.ds(at * depth, depth)
+        wh[block, :] = value.astype(jnp.bfloat16)
+        for piece, first, count, start in (
+            (2, 0, MERGED, 0),
+            (3, query_width, HEAD_SIZE, MERGED),
+            (4, query_width + key_width, HEAD_SIZE, MERGED + HEAD_SIZE),
+        ):
+            copy = spread(
+                at,
+                device,
+                piece,
+                wh.at[block, pl.ds(start, count)],
+                own_heads.at[:, columns_of(first, place.index, count)],
+            )
+            copy.start()
+            heads_copies.append(copy)
+    for copy in heads_copies[:21]:
+        copy.wait_recv()
+    for copy in heads_copies[21:]:
+        copy.wait()
+    heads_rep = rep_copy(20, own_heads, other_heads)
+    heads_rep.start()
+    gather.finish()
+    for copy in expand_copies[14:] + own_saves + [result_save, merge_save]:
+        copy.wait()
+    for copy in expand_copies[:14] + heads_copies[:21]:
+        copy.wait_send()
+    for copy in rep_copies + expand_reps + [merge_rep, heads_rep]:
+        copy.wait()
 
 
 def sems(*counts):
@@ -1315,7 +1751,7 @@
     )
 
 
-def run_forward(own, gains, head_gain, cosine, sine, first_key, weights):
+def run_forward(own, gain_row, cosine, sine, first_key, weights):
     micro, rows, width = own.shape
     length = cosine.shape[1]
     hidden_width = weights[3].shape[0]
@@ -1334,10 +1770,15 @@
             shape((micro, length, width), b16),
             shape((micro, length, 2 * hidden_width), f32),
             shape((micro, length, hidden_width), b16),
+            shape((width, JOINT), b16),
+            shape((width, 2 * hidden_width), b16),
+            shape((2, width), f32),
+            shape((2, HEAD_SIZE), f32),
         ),
-        in_specs=[vmem_spec()] * 3 + [any_spec()] * 7,
-        out_specs=(any_spec(),) * 10,
+        in_specs=[vmem_spec()] * 2 + [any_spec()] * 7,
+        out_specs=(any_spec(),) * 12 + (vmem_spec(),) * 2,
         scratch_shapes=vmem(
+            (PLANE, *gain_row.shape, f32),
             (width, JOINT, b16),
             (MERGED, width, b16),
             (width, 2 * hidden_width, b16),
@@ -1357,11 +1798,13 @@
         )
         + exchange_buffers(rows, width)
         + vmem((rows, width, f32), (rows, width, f32), (rows, width, b16))
-        + sems(4, 10, 3, micro, micro, *((10,) * 8)),
+        + sems(10)
+        + [pltpu.SemaphoreType.DMA((6, PLANE - 1))] * 2
+        + sems(10, 3, micro, micro, *((10,) * 8)),
         compiler_params=pltpu.CompilerParams(
             collective_id=1, has_side_effects=True, vmem_limit_bytes=VMEM_BYTES
         ),
-    )(own, gains, head_gain, cosine, sine, first_key, *weights)
+    )(own, gain_row, cosine, sine, first_key, *weights)
 
 
 def run_backward(own, gains, head_gain, cosine, sine, first_key, weights, saved):
@@ -1414,6 +1857,58 @@
     )(own, gains, head_gain, cosine, sine, first_key, *weights, *saved)
 
 
+def run_gradients(gains, head_gain, cosine, sine, first_key, weights, saved, operands):
+    micro, rows, width = saved[0].shape
+    length = cosine.shape[1]
+    hidden_width = operands[0].shape[1]
+    depth = weights[1].shape[0]
+    f32, b16 = jnp.float32, jnp.bfloat16
+    shape = jax.ShapeDtypeStruct
+    terms = ((depth, PLANE * JOINT), (depth, width), (depth, 2 * FF), (hidden_width, width))
+    return pl.pallas_call(
+        functools.partial(gradient_kernel, rows),
+        out_shape=(shape((rows, width), f32),)
+        + tuple(shape(term, b16) for term in terms for _ in range(2))
+        + (shape((1, width), f32), shape((2, HEAD_SIZE), f32)),
+        in_specs=[vmem_spec()] * 2 + [any_spec()] * 17,
+        out_specs=(any_spec(),) * 9 + (vmem_spec(),) * 2,
+        scratch_shapes=vmem(
+            (width, JOINT, b16),
+            (MERGED, width, b16),
+            (length, width, b16),
+            (length, HEAD_SIZE, f32),
+            (length, HEAD_SIZE, f32),
+            (length, 1, jnp.int32),
+            (length, JOINT, f32),
+            (length, JOINT, b16),
+            (length, MERGED, b16),
+            (length, MERGED, f32),
+            (length, HEAD_SIZE, f32),
+            (length, HEAD_SIZE, f32),
+            (length, JOINT, b16),
+            (4, rows, width, f32),
+            (4, rows, width, b16),
+            (4, rows, width, b16),
+            *(((3, rows // 2, width, b16),) * 4),
+            (rows, width, b16),
+            (rows, width, f32),
+            (2, micro * length, depth, b16),
+            (depth, micro * length, b16),
+            (micro * length, width, b16),
+            (micro * length, 2 * hidden_width, b16),
+            (length, JOINT, b16),
+            (PLANE, depth, 2 * hidden_width, b16),
+            (hidden_width, width, b16),
+        )
+        + sems(13, 2, 10, *((10,) * 4))
+        + [pltpu.SemaphoreType.DMA((5, PLANE - 1))] * 2
+        + sems(21, 21),
+        compiler_params=pltpu.CompilerParams(
+            collective_id=3, has_side_effects=True, vmem_limit_bytes=VMEM_BYTES
+        ),
+    )(gains, head_gain, cosine, sine, first_key, *weights, *saved, *operands)
+
+
 def position_tables(lengths, length):
     document_index, positions = places(lengths, length)
     half_width = HEAD_SIZE // 2
@@ -1449,38 +1944,8 @@
     hidden_width = reduce_weight.shape[1]
     query_width = QUERY_HEADS * HEAD_SIZE
 
-    def by_shard(weight, parts):
-        return weight.reshape(weight.shape[0], parts, shards, -1).swapaxes(0, 2)
-
-    heads_parts = heads_weight[0]
-    pieces = jnp.concatenate(
-        [
-            heads_parts[:, :query_width].reshape(depth, shards, MERGED),
-            heads_parts[:, query_width : query_width + shards * HEAD_SIZE].reshape(
-                depth, shards, HEAD_SIZE
-            ),
-            heads_parts[:, query_width + shards * HEAD_SIZE :].reshape(depth, shards, HEAD_SIZE),
-        ],
-        axis=-1,
-    ).swapaxes(0, 1)
-    expand_pieces = (
-        expand_weight[0]
-        .reshape(depth, 2, shards, hidden_width)
-        .transpose(2, 0, 1, 3)
-        .reshape(shards, depth, 2 * hidden_width)
-    )
-    heads_full = lax.all_to_all(pieces, "fsdp", 0, 0, tiled=True).reshape(width, JOINT)
-    expand_full = lax.all_to_all(expand_pieces, "fsdp", 0, 0, tiled=True).reshape(
-        width, 2 * hidden_width
-    )
-    weights = (heads_full, merge_weight[0], expand_full, reduce_weight[0])
-    all_gains = lax.all_gather(
-        jnp.concatenate([mixer_gain[0], feed_gain[0], head_gain[0]]), "fsdp", axis=0
-    ).astype(jnp.float32)
-    gains = jnp.stack(
-        [all_gains[:, :depth].reshape(-1), all_gains[:, depth : 2 * depth].reshape(-1)]
-    )
-    head_gains = all_gains[:, 2 * depth :].reshape(2, HEAD_SIZE)
+    gain_row = jnp.concatenate([mixer_gain[0], feed_gain[0], head_gain[0]]).astype(jnp.float32)
+    gain_row = jnp.pad(gain_row, (0, -gain_row.shape[0] % 128))[None]
     tables = [position_tables(doc_lengths[at, 0], length) for at in range(micro)]
     cosine, sine, first_key = (jnp.stack(entry) for entry in zip(*tables))
 
@@ -1495,7 +1960,18 @@
         normal_b,
         joined,
         hidden,
-    ) = run_forward(own, gains, head_gains, cosine, sine, first_key, weights)
+        heads_full,
+        expand_full,
+        gains,
+        head_gains,
+    ) = run_forward(
+        own,
+        gain_row,
+        cosine,
+        sine,
+        first_key,
+        (heads_weight[0], merge_weight[0], expand_weight[0], reduce_weight[0]),
+    )
     grad_results, upstream, grad_joined, grad_middle, grad_projected, gain_terms, head_terms = (
         run_backward(
             own,
@@ -1504,61 +1980,59 @@
             cosine,
             sine,
             first_key,
-            weights,
+            (heads_full, merge_weight[0], expand_full, reduce_weight[0]),
             (inputs, projected, heads, middle, joined),
         )
     )
 
-    def product(left, right):
-        return product_term(
-            left.reshape(micro * length, -1), right.reshape(micro * length, -1)
-        ).astype(jnp.bfloat16)
-
-    def with_replica(term):
-        other = lax.ppermute(term, "rep", [(0, 1), (1, 0)])
-        return term.astype(jnp.float32) + other.astype(jnp.float32)
-
-    def to_owners(term):
-        return lax.all_to_all(term.reshape(shards, depth, -1), "fsdp", 0, 0, tiled=True)
-
-    grad_reduce = with_replica(product(hidden, upstream))
-    expand_term = to_owners(product(normal_b, grad_joined))
-    grad_expand = with_replica(
-        expand_term.reshape(shards, depth, 2, hidden_width)
-        .transpose(1, 2, 0, 3)
-        .reshape(depth, 2 * shards * hidden_width)
-    )
-    grad_merge = with_replica(product(mixed, grad_middle))
-    heads_term = to_owners(product(normal_a, grad_projected)).swapaxes(0, 1)
-    grad_heads = with_replica(
-        jnp.concatenate(
-            [
-                heads_term[:, :, :MERGED].reshape(depth, -1),
-                heads_term[:, :, MERGED : MERGED + HEAD_SIZE].reshape(depth, -1),
-                heads_term[:, :, MERGED + HEAD_SIZE :].reshape(depth, -1),
-            ],
-            axis=-1,
-        )
-    )
-    terms = jnp.concatenate(
-        [jnp.sum(gain_terms, axis=0).reshape(-1), jnp.sum(head_terms, axis=0).reshape(-1)]
-    )
-    sums = lax.psum(terms, ("fsdp", "rep"))
+    def flat(array):
+        return array.reshape(micro * length, -1)
+
+    last_result, *terms, mixer_term, head_term = run_gradients(
+        gains,
+        head_gains,
+        cosine,
+        sine,
+        first_key,
+        (heads_full, merge_weight[0]),
+        (inputs, projected, heads, grad_results),
+        (
+            flat(hidden),
+            flat(upstream),
+            flat(normal_b),
+            flat(grad_joined),
+            flat(mixed),
+            grad_middle,
+            flat(normal_a),
+            grad_projected,
+        ),
+    )
+    grad_heads, grad_merge, grad_expand, grad_reduce = (
+        (terms[at].astype(jnp.float32) + terms[at + 1].astype(jnp.float32))[None]
+        for at in range(0, 8, 2)
+    )
+    mixer_term = mixer_term[0] + jnp.sum(gain_terms[:-1, 0], axis=0)
+    head_term = head_term + jnp.sum(head_terms[:-1], axis=0)
+    sums = lax.psum(
+        jnp.concatenate([mixer_term, jnp.sum(gain_terms[:, 1], axis=0), head_term.reshape(-1)]),
+        ("fsdp", "rep"),
+    )
     index = lax.axis_index("fsdp")
 
     def own_part(first, count):
         return lax.dynamic_slice_in_dim(sums, first + index * count, count)[None]
 
     head_count = head_gain.shape[1]
+    grad_results = jnp.concatenate([grad_results[:-1], last_result[None]])
     return (
         jnp.where(lax.axis_index("section") == 0, grad_results, results)[None, :, None],
         own_part(0, depth),
-        grad_heads[None],
-        grad_merge[None],
+        grad_heads,
+        grad_merge,
         own_part(2 * width, head_count),
         own_part(width, depth),
-        grad_expand[None],
-        grad_reduce[None],
+        grad_expand,
+        grad_reduce,
     )
 
 

time: 1260 us -> 1080 us (0.86)
  Pallas kernels: 629 us -> 987 us
  blocking collectives: 344 us -> 50.8 us
  waiting for transfers between devices: 95.7 us -> 0 us
  local copies, waits for them, and re-layouts: 63.6 us -> 4.84 us
  matrix products: 41.6 us -> 0 us
  starting transfers between devices: 35.7 us -> 0 us
    pallas_call x0 -> x1, Pallas kernels: none -> 318 us  [run_gradients(): pl.pallas_call(functools.partial(gradient_kernel, rows), out_shape=(shape...]
    psum x1, blocking collectives: 258 us -> 50.8 us  [tensor_parallel_body(): lax.psum(jnp.concatenate([mixer_term, jnp.sum(gain_terms[:, 1], axis=0),...]
    pallas_call x1, Pallas kernels: 292 us -> 378 us  [run_forward(): pl.pallas_call(functools.partial(forward_kernel, rows), out_shape=(shape(...]
    unnamed x1 -> x0, blocking collectives: 85.9 us -> none
    all_to_all x4 -> x0, waiting for transfers between devices: 62.2 us -> none  [the longest x2 62.1 us: to_owners(): lax.all_to_all(term.reshape(shards, depth, -1), 'fsdp', 0, 0, tiled=True)]
    pallas_call x1, Pallas kernels: 337 us -> 290 us  [run_backward(): pl.pallas_call(functools.partial(backward_kernel, rows), out_shape=(shape...]
    dot_general x4 -> x0, matrix products: 41.6 us -> none  [product_term(): lax.dot_general(left_side, right_side, (((0,), (0,)), ((), ())), preferre...]
    reshape x7 -> x0, local copies, waits for them, and re-layouts: 38.6 us -> none  [the longest x2 23.1 us: tensor_parallel_body(): expand_term.reshape(shards, depth, 2, hidden_width).transpose(1, 2, 0, 3)]
  transfers between devices with their start and end apart: 8 -> 0, of which waited for: 2 -> 0; matrix products, arithmetic and copies ran while one was open for 8% -> 0% of each run, Pallas kernels for 0% -> 0%
where the time goes in v2:
time: 1080 us
  Pallas kernels  987 us (91%)
  blocking collectives  50.8 us (5%)
  other arithmetic  35.7 us (3%)
    pallas_call x1, Pallas kernels, run_forward(): pl.pallas_call(functools.partial(forward_kernel, rows), out_shape=(shape(...  378 us
    pallas_call x1, Pallas kernels, run_gradients(): pl.pallas_call(functools.partial(gradient_kernel, rows), out_shape=(shape...  318 us
    pallas_call x1, Pallas kernels, run_backward(): pl.pallas_call(functools.partial(backward_kernel, rows), out_shape=(shape...  290 us
    psum x1, blocking collectives, tensor_parallel_body(): lax.psum(jnp.concatenate([mixer_term, jnp.sum(gain_terms[:, 1], axis=0),...  50.8 us
    broadcast_in_dim x4, other arithmetic, tensor_parallel_body(): (terms[at].astype(jnp.float32) + terms[at + 1].astype(jnp.float32))[None]  22.5 us

profile of v2, /device:TPU:0, one launch (start us, length us, event | category | flops | bytes accessed | tf_op | source)
XLA Modules:
  0.0 1079.1 jit_solution(4843581579292824117)
XLA Ops:
  0.6 0.7 reduce.2
  1.3 0.7 reduce.1
  2.0 0.7 fusion.8
  2.7 0.6 reshape.158.gain_ref
  3.3 0.7 slice_bitcast_fusion.3
  4.0 0.2 reduce-window.17
  4.1 0.2 reduce-window.16
  4.3 0.1 select_reduce_fusion
  4.4 3.7 fusion.1
  8.2 0.2 maximum_bitcast_fusion.1
  8.4 0.2 maximum_bitcast_fusion
  8.6 1.0 pad_maximum_fusion.cos_ref
  9.6 0.2 maximum_bitcast_fusion.3
  9.8 0.2 maximum_bitcast_fusion.2
  10.0 1.0 pad_maximum_fusion.1.sin_ref
  11.1 0.2 copy.28
  11.3 0.1 subtract_subtract_fusion
  11.4 0.2 copy.27
  11.6 0.1 subtract_subtract_fusion.1
  11.7 1.0 pad_add_fusion.first_ref
  12.7 378.5 %shard_map.152 = (f32[2,128,2048]{2,1,0:T(8,128)}, bf16[2,128,2048]{2,1,0:T(8,128)(2,1)}, bf16[2,1024,2048]{2,1,0:T(8,128)(2,1)}, f32[2,1024,512]{2,1,0:T(8,128)...) custom-call(bf16[2,128,2048]{2,1,0:T(8,128)(2,1)} %bitcast.67, ...), custom_call_target="tpu_custom_call" | custom-call | tf_op jit(solution)/shard_map/pallas_call | solution.py:1760
  391.2 290.2 %shard_map.153 = (f32[2,128,2048]{2,1,0:T(8,128)}, bf16[2,1024,2048]{2,1,0:T(8,128)(2,1)}, bf16[2,1024,1536]{2,1,0:T(8,128)(2,1)}, bf16[2,1024,2048]{2,1,0:T(8,1...) custom-call(bf16[2,128,2048]{2,1,0:T(8,128)(2,1)} %bitcast.68, ...), custom_call_target="tpu_custom_call" | custom-call | tf_op jit(solution)/shard_map/pallas_call | solution.py:1816
  681.4 318.1 %shard_map.154 = (f32[128,2048]{1,0:T(8,128)}, bf16[256,4096]{1,0:T(8,128)(2,1)}, bf16[256,4096]{1,0:T(8,128)(2,1)}, bf16[256,2048]{1,0:T(8,128)(2,1)}, bf16[256...) custom-call(f32[2,2048]{1,0:T(2,128)} %get-tuple-element.40.gains_re, ...), custom_call_target="tpu_custom_call" | custom-call | tf_op jit(solution)/shard_map/pallas_call | solution.py:1868
  999.5 0.0 copy-start.2
  999.5 1.4 slice.20
  1000.9 0.4 copy-done.2
  1001.4 0.0 copy-start.7
  1001.4 0.0 copy-start.8
  1001.4 0.0 copy-start.5
  1001.4 0.0 copy-start.6
  1001.4 2.8 fusion
  1004.2 0.0 copy-done.7
  1004.2 0.0 copy-done.8
  1004.2 0.0 copy-done.5
  1004.3 0.0 copy-done.6
  1004.3 50.8 %psum.7 = f32[4352]{0:T(1024)S(1)} all-reduce(f32[4352]{0:T(1024)S(1)} %pad_maximum_fusion.2), channel_id=1, replica_groups=mesh['section'=2,'fsdp'=8,'rep'=2] {'fsdp','rep'}, use_global_device_ids=true, to_apply=%region_5.6 | all-reduce | flops 4352 | bytes 34816 | tf_op jit(solution)/shard_map/psum | solution.py:2016
  1055.1 0.6 fusion.10
  1055.7 0.0 copy-start.3
  1055.7 0.0 copy-start.4
  1055.7 5.1 add_bitcast_fusion.2
  1060.9 0.0 copy-done.3
  1060.9 0.0 copy-done.4
  1060.9 1.7 add_bitcast_fusion.3
  1062.5 0.6 dynamic-slice_bitcast_fusion
  1063.1 11.7 %add_bitcast_fusion = f32[1,256,12288]{2,1,0:T(8,128)} fusion(bf16[256,12288]{1,0:T(8,128)(2,1)} %get-tuple-element.69, bf16[256,12288]{1,0:T(8,128)(2,1)} %get-tuple-element.68), kind=kLoop, calls=%fused_computation | loop fusion | flops 9437184 | bytes 25165824 | tf_op jit(solution)/shard_map/broadcast_in_dim | solution.py:2011
  1074.8 0.0 copy-done
  1074.8 0.0 copy-done.1
  1074.8 4.0 add_bitcast_fusion.1
  (10 shorter events, 0.1 us)
Async XLA Ops:
  999.5 1.9 copy-start.2
  1001.4 2.8 copy-start.7
  1001.4 2.8 copy-start.8
  1001.4 2.8 copy-start.5
  1001.4 2.9 copy-start.6
  1055.7 5.1 copy-start.3
  1055.7 5.1 copy-start.4
  1063.1 11.7 %copy-start = (bf16[768,2048]{1,0:T(8,128)(2,1)S(1)}, bf16[768,2048]{1,0:T(8,128)(2,1)}, u32[]{:S(2)}) copy-start(bf16[768,2048]{1,0:T(8,128)(2,1)} %get-tuple-element.70) | copy-start | bytes 9437188
  1063.1 11.7 %copy-start.1 = (bf16[768,2048]{1,0:T(8,128)(2,1)S(1)}, bf16[768,2048]{1,0:T(8,128)(2,1)}, u32[]{:S(2)}) copy-start(bf16[768,2048]{1,0:T(8,128)(2,1)} %get-tuple-element.71) | copy-start | bytes 9437188

commit v3 on v0

--- a/solution.py
+++ b/solution.py
@@ -1,8 +1,13 @@
+import functools
 import math
+import types
+import typing
 
 import jax
 import jax.numpy as jnp
 from jax import lax
+from jax.experimental import pallas as pl
+from jax.experimental.pallas import tpu as pltpu
 from jax.sharding import PartitionSpec as P
 
 FF = 6144
@@ -14,6 +19,7 @@
 NORM_EPS = 1e-06
 ROPE_BASE = 1000000.0
 MASKED_SCORE = -1e30
+PLANE = 8
 
 
 def from_behind(array, axis, by):
@@ -458,9 +464,1749 @@
     )
 
 
+MESH = pl.DeviceIdType.MESH
+MERGED = QUERY_HEADS // KEY_VALUE_HEADS * HEAD_SIZE
+JOINT = MERGED + 2 * HEAD_SIZE
+VMEM_BYTES = 63 * 2**20
+
+
+def mm(left, right):
+    return jnp.dot(left, right, preferred_element_type=jnp.float32)
+
+
+def mm_t(left, right):
+    return lax.dot_general(
+        left, right, (((1,), (1,)), ((), ())), preferred_element_type=jnp.float32
+    )
+
+
+def t_mm(left, right):
+    return lax.dot_general(
+        left, right, (((0,), (0,)), ((), ())), preferred_element_type=jnp.float32
+    )
+
+
+def remote(src, dst, send, recv, device):
+    return pltpu.make_async_remote_copy(
+        src_ref=src,
+        dst_ref=dst,
+        send_sem=send,
+        recv_sem=recv,
+        device_id=device,
+        device_id_type=MESH,
+    )
+
+
+class Place:
+    def __init__(self):
+        self.index = lax.axis_index("fsdp")
+        self.core = lax.rem(self.index, 2)
+        self.chip = lax.div(self.index, 2)
+        self.x = lax.rem(self.chip, 2)
+        self.y = lax.div(self.chip, 2)
+        self.x_peer = {"fsdp": self.index + 2 - 4 * self.x}
+        self.y_peer = {"fsdp": self.index + 4 - 8 * self.y}
+        self.core_peer = {"fsdp": self.index + 1 - 2 * self.core}
+        self.section = lax.axis_index("section")
+        self.section_peer = {"section": 1 - self.section}
+        self.replica = lax.axis_index("rep")
+        self.rep_peer = {"rep": 1 - self.replica}
+
+    def chip_at(self, rel):
+        x, y = self.x, self.y
+        if rel in (1, 3):
+            x = 1 - x
+        if rel in (2, 3):
+            y = 1 - y
+        return 2 * y + x
+
+    def others(self):
+        order = ((3, 0), (3, 1), (1, 0), (1, 1), (2, 0), (2, 1), (0, 1), (0, 0))
+        return [
+            (at, 2 * self.chip_at(rel) + (1 - self.core if other else self.core))
+            for at, (rel, other) in enumerate(order)
+        ]
+
+    def greet(self, peers):
+        barrier = pltpu.get_barrier_semaphore()
+        for peer in peers:
+            pl.semaphore_signal(barrier, inc=1, device_id=peer, device_id_type=MESH)
+        pl.semaphore_wait(barrier, len(peers))
+
+
+class Gather:
+    def __init__(self, place, full, send, recv, rows):
+        half = rows // 2
+
+        def span(rel, part=None):
+            first = (2 * place.chip_at(rel) + place.core) * rows
+            if part is None:
+                return pl.ds(pl.multiple_of(first, rows), rows)
+            return pl.ds(pl.multiple_of(first + part * half, half), half)
+
+        def copy(at, piece, peer):
+            block = full.at[piece]
+            return remote(block, block, send.at[at], recv.at[at], peer)
+
+        self.copies = [
+            copy(0, span(0, 1), place.x_peer),
+            copy(1, span(0, 0), place.x_peer),
+            copy(2, span(0, 0), place.y_peer),
+            copy(3, span(0, 1), place.y_peer),
+            copy(4, span(0), place.core_peer),
+            copy(5, span(1, 1), place.y_peer),
+            copy(6, span(2, 0), place.x_peer),
+            copy(7, span(1), place.core_peer),
+            copy(8, span(2), place.core_peer),
+            copy(9, span(3), place.core_peer),
+        ]
+
+    def start(self):
+        for at in (0, 2, 4, 1, 3):
+            self.copies[at].start()
+
+    def relay(self):
+        self.copies[0].wait_recv()
+        self.copies[5].start()
+        self.copies[2].wait_recv()
+        self.copies[6].start()
+
+    def near(self):
+        self.copies[1].wait_recv()
+        self.copies[7].start()
+        self.copies[3].wait_recv()
+        self.copies[8].start()
+
+    def far(self):
+        self.copies[5].wait_recv()
+        self.copies[6].wait_recv()
+        self.copies[9].start()
+
+    def wait(self, at):
+        self.copies[at].wait_recv()
+
+    def finish(self):
+        for entry in self.copies:
+            entry.wait_send()
+
+    def over_blocks(self, block, between=lambda: None, early=lambda at: None):
+        self.start()
+        early(0)
+        self.wait(4)
+        block(0)
+        early(1)
+        self.relay()
+        early(2)
+        self.near()
+        self.wait(7)
+        block(1)
+        early(3)
+        self.wait(8)
+        block(2)
+        early(4)
+        between()
+        self.far()
+        self.wait(9)
+        block(3)
+
+
+class Scatter:
+    def __init__(self, place, held, to_core, from_core, to_x, to_y, from_x, from_y, send, recv, rows):
+        self.place, self.held, self.to_core, self.from_core = place, held, to_core, from_core
+        self.to_x, self.to_y, self.from_x, self.from_y = to_x, to_y, from_x, from_y
+        self.rows, self.half = rows, rows // 2
+
+        def copy(at, src, dst, peer):
+            return remote(src, dst, send.at[at], recv.at[at], peer)
+
+        self.copies = [
+            copy(rel, to_core.at[rel], from_core.at[rel], place.core_peer) for rel in range(4)
+        ] + [
+            copy(4, to_x.at[0], from_x.at[0], place.x_peer),
+            copy(5, to_y.at[0], from_y.at[0], place.y_peer),
+            copy(6, to_x.at[1], from_x.at[1], place.x_peer),
+            copy(7, to_y.at[1], from_y.at[1], place.y_peer),
+            copy(8, to_y.at[2], from_y.at[2], place.y_peer),
+            copy(9, to_x.at[2], from_x.at[2], place.x_peer),
+        ]
+
+    def put(self, rel, product, width):
+        step, rows, mine = 512, self.rows, self.place.core == 0
+
+        @pl.loop(0, width // step)
+        def _(at):
+            columns = pl.ds(pl.multiple_of(at * step, step), step)
+            value = product(columns)
+            low, high = value[:rows], value[rows:]
+            self.held[rel, :, columns] = jnp.where(mine, low, high)
+            self.to_core[rel, :, columns] = jnp.where(mine, high, low).astype(jnp.bfloat16)
+
+        self.copies[rel].start()
+
+    def pair(self, rel):
+        self.copies[rel].wait_recv()
+        half, held = self.half, self.held
+
+        @pl.loop(0, self.rows // 16)
+        def _(at):
+            span = pl.ds(pl.multiple_of(at * 16, 16), 16)
+            held[rel, span, :] += self.from_core[rel, span, :].astype(jnp.float32)
+
+        if rel == 3:
+            self.to_x[0] = held[3, :half].astype(jnp.bfloat16)
+            self.copies[4].start()
+            self.to_y[0] = held[3, half:].astype(jnp.bfloat16)
+            self.copies[5].start()
+        if rel == 1:
+            self.to_x[1] = held[1, :half].astype(jnp.bfloat16)
+            self.copies[6].start()
+        if rel == 2:
+            self.to_y[1] = held[2, half:].astype(jnp.bfloat16)
+            self.copies[7].start()
+
+    def relay(self):
+        half, held = self.half, self.held
+        self.copies[4].wait_recv()
+        self.to_y[2] = (held[2, :half] + self.from_x[0].astype(jnp.float32)).astype(jnp.bfloat16)
+        self.copies[8].start()
+        self.copies[5].wait_recv()
+        self.to_x[2] = (held[1, half:] + self.from_y[0].astype(jnp.float32)).astype(jnp.bfloat16)
+        self.copies[9].start()
+
+    def total(self, add):
+        for at in (6, 7, 8, 9):
+            self.copies[at].wait_recv()
+        count = self.half // 16
+
+        @pl.loop(0, count)
+        def _(at):
+            span = pl.ds(pl.multiple_of(at * 16, 16), 16)
+            low = self.held[0, span, :] + self.from_x[1, span, :].astype(jnp.float32)
+            add(span, low + self.from_y[2, span, :].astype(jnp.float32))
+
+        @pl.loop(0, count)
+        def _(at):
+            span = pl.ds(pl.multiple_of(at * 16, 16), 16)
+            below = pl.ds(pl.multiple_of(self.half + at * 16, 16), 16)
+            high = self.held[0, below, :] + self.from_y[1, span, :].astype(jnp.float32)
+            add(below, high + self.from_x[2, span, :].astype(jnp.float32))
+
+        for entry in self.copies:
+            entry.wait_send()
+
+
+def by_rows(count, body):
+    @pl.loop(0, count // 16)
+    def _(at):
+        body(pl.ds(pl.multiple_of(at * 16, 16), 16))
+
+
+def inverse_size(values):
+    return lax.rsqrt(jnp.mean(values * values, axis=-1, keepdims=True) + NORM_EPS)
+
+
+def norm_back(values, gain, upstream):
+    size = inverse_size(values)
+    scaled_up = upstream * gain
+    back = size * scaled_up - values * (
+        size * size * size * jnp.mean(values * scaled_up, axis=-1, keepdims=True)
+    )
+    return back, upstream * values * size
+
+
+def turn(values, cosine, sine):
+    return values * cosine + pltpu.roll(values, HEAD_SIZE // 2, 1) * sine
+
+
+def turn_back(values, cosine, sine):
+    return values * cosine + pltpu.roll(values * sine, HEAD_SIZE // 2, 1)
+
+
+def probabilities(queries, keys, first_keys, first_row):
+    scores = mm_t(queries, keys) * HEAD_SIZE ** (-0.5)
+    key_index = lax.broadcasted_iota(jnp.int32, scores.shape, 1)
+    row_index = first_row + lax.broadcasted_iota(jnp.int32, scores.shape, 0)
+    allowed = (key_index >= first_keys) & (key_index <= row_index)
+    scores = jnp.where(allowed, scores, MASKED_SCORE)
+    powers = jnp.exp(scores - jnp.max(scores, axis=-1, keepdims=True))
+    return powers / jnp.sum(powers, axis=-1, keepdims=True)
+
+
+def block_rows(place, rel, rows):
+    return pl.ds(pl.multiple_of(place.chip_at(rel) * 2 * rows, 2 * rows), 2 * rows)
+
+
+def shard_columns(first, device, count):
+    return pl.ds(pl.multiple_of(first + device * count, 128), count)
+
+
+def layer_forward_step(place, rows, refs, buffers, slot, step, hooks):
+    (wh, wm, we, wr), gains_ref, head_gain_ref = refs.weights, refs.gains, refs.head_gain
+    current, middle, result, result_b = (
+        buffers.current,
+        buffers.middle,
+        buffers.result,
+        buffers.result_b,
+    )
+    full_a, full_b = buffers.full_a, buffers.full_b
+    projected, heads, mixed = buffers.projected, buffers.heads, buffers.mixed
+    joined, hidden = buffers.joined, buffers.hidden
+    chip_rows, width, hidden_width = 2 * rows, current.shape[1], wr.shape[0]
+    save_sem = buffers.save_sem
+    tables = [
+        pltpu.make_async_copy(src.at[slot], dst, buffers.table_sem.at[at])
+        for at, (src, dst) in enumerate(zip(refs.tables, buffers.tables))
+    ]
+    cosine, sine, first_key = buffers.tables
+    for table in tables:
+        table.start()
+
+    def save(at, src, dst):
+        copy = pltpu.make_async_copy(src, dst.at[slot], save_sem.at[at])
+        copy.start()
+        return copy
+
+    saves = [save(0, current, refs.inputs)]
+
+    def enter(span):
+        values = current[span, :].astype(jnp.float32)
+        base = pl.multiple_of(place.index * rows + span.start, 16)
+        full_a[pl.ds(base, 16), :] = (
+            values * inverse_size(values) * gains_ref[0:1, :]
+        ).astype(jnp.bfloat16)
+
+    by_rows(rows, enter)
+    for table in tables:
+        table.wait()
+    gather = Gather(place, full_a, *buffers.gather_a, rows)
+
+    def heads_block(rel):
+        span = block_rows(place, rel, rows)
+        if rel == 0:
+            hooks.heads()
+        values = mm(full_a[span, :], wh[...])
+        projected[span, :] = values
+        for at in range(3):
+            columns = pl.ds(at * HEAD_SIZE, HEAD_SIZE)
+            one = values[:, at * HEAD_SIZE : (at + 1) * HEAD_SIZE]
+            gain = head_gain_ref[0:1, :] if at < 2 else head_gain_ref[1:2, :]
+            heads[span, columns] = turn(
+                one * inverse_size(one) * gain, cosine[span, :], sine[span, :]
+            ).astype(jnp.bfloat16)
+        heads[span, 3 * HEAD_SIZE :] = values[:, 3 * HEAD_SIZE :].astype(jnp.bfloat16)
+
+    gather.over_blocks(heads_block)
+    hooks.service()
+    saves += [
+        save(1, full_a, refs.normal_a),
+        save(2, projected, refs.projected),
+        save(3, heads, refs.heads),
+    ]
+    scatter = Scatter(place, *buffers.scatter, *buffers.scatter_a, rows)
+
+    def attend_block(rel):
+        first_row = place.chip_at(rel) * chip_rows
+        span = block_rows(place, rel, rows)
+        for at in range(2):
+            columns = pl.ds(at * HEAD_SIZE, HEAD_SIZE)
+            probs = probabilities(
+                heads[span, columns],
+                heads[:, 2 * HEAD_SIZE : 3 * HEAD_SIZE],
+                first_key[span, :],
+                first_row,
+            )
+            mixed[span, columns] = mm(
+                probs.astype(jnp.bfloat16), heads[:, 3 * HEAD_SIZE :]
+            ).astype(jnp.bfloat16)
+        scatter.put(rel, lambda columns: mm(mixed[span, :], wm[:, columns]), width)
+
+    attend_block(3)
+    scatter.pair(3)
+    attend_block(2)
+    scatter.pair(2)
+    attend_block(1)
+    scatter.pair(1)
+    attend_block(0)
+    saves.append(save(4, mixed, refs.mixed))
+    scatter.relay()
+    scatter.pair(0)
+
+    def residual(span, value):
+        values = value + current[span, :].astype(jnp.float32)
+        middle[span, :] = values
+        base = pl.multiple_of(place.index * rows + span.start, 16)
+        full_b[pl.ds(base, 16), :] = (
+            values * inverse_size(values) * gains_ref[1:2, :]
+        ).astype(jnp.bfloat16)
+
+    scatter.total(residual)
+    gather.finish()
+    saves.append(save(5, middle, refs.middle))
+    for copy in saves[:5]:
+        copy.wait()
+    gather_b = Gather(place, full_b, *buffers.gather_b, rows)
+    scatter_b = Scatter(place, *buffers.scatter, *buffers.scatter_b, rows)
+    joined_copies = {}
+
+    def feed_block(rel):
+        span = block_rows(place, rel, rows)
+        stage = joined.at[rel % 2]
+        if rel == 0:
+            hooks.feed()
+        if rel >= 2:
+            joined_copies[rel - 2].wait()
+
+        @pl.loop(0, hidden_width // 256)
+        def _(at):
+            columns = pl.ds(pl.multiple_of(at * 256, 256), 256)
+            later = pl.ds(pl.multiple_of(hidden_width + at * 256, 256), 256)
+            gate = mm(full_b[span, :], we[:, columns])
+            up = mm(full_b[span, :], we[:, later])
+            stage[:, columns] = gate
+            stage[:, later] = up
+            hidden[span, columns] = (gate * jax.nn.sigmoid(gate) * up).astype(jnp.bfloat16)
+
+        copy = pltpu.make_async_copy(
+            stage, refs.joined.at[slot, span], save_sem.at[8 + rel % 2]
+        )
+        copy.start()
+        joined_copies[rel] = copy
+        scatter_b.put(rel, lambda columns: mm(hidden[span, :], wr[:, columns]), width)
+        if rel in (1, 2):
+            scatter_b.pair(rel - 1)
+
+    gather_b.over_blocks(feed_block, lambda: scatter_b.pair(2))
+    later_saves = [save(6, full_b, refs.normal_b), save(7, hidden, refs.hidden)]
+    scatter_b.pair(3)
+    scatter_b.relay()
+    hooks.finish()
+
+    def finish(span, value):
+        values = value + middle[span, :]
+        result[span, :] = values
+        result_b[span, :] = values.astype(jnp.bfloat16)
+
+    scatter_b.total(finish)
+    hooks.hand()
+    gather_b.finish()
+    for copy in [saves[5]] + later_saves + [joined_copies[2], joined_copies[3]]:
+        copy.wait()
+    hooks.after()
+
+
+def feed_back(place, rows, gather, scatter, full, weights, joined, joined_load, out_of, done):
+    wm, we, wr = weights
+    hidden_width, width = wr.shape
+
+    def feed_block(rel):
+        span = block_rows(place, rel, rows)
+        stage, out = joined.at[rel % 2], out_of(rel)
+        joined_load(rel).wait()
+
+        @pl.loop(0, hidden_width // 256)
+        def _(at):
+            columns = pl.ds(pl.multiple_of(at * 256, 256), 256)
+            later = pl.ds(pl.multiple_of(hidden_width + at * 256, 256), 256)
+            grad = mm_t(full[span, :], wr[columns, :])
+            gate, up = stage[:, columns], stage[:, later]
+            sigmoid = jax.nn.sigmoid(gate)
+            unit = gate * sigmoid
+            out[:, columns] = (grad * up * (sigmoid + unit * (1.0 - sigmoid))).astype(jnp.bfloat16)
+            out[:, later] = (grad * unit).astype(jnp.bfloat16)
+
+        if rel < 2:
+            joined_load(rel + 2).start()
+        done(rel, out)
+        scatter.put(rel, lambda columns: mm_t(out[...], we[columns, :]), width)
+        if rel in (1, 2):
+            scatter.pair(rel - 1)
+
+    gather.over_blocks(feed_block, lambda: scatter.pair(2))
+    scatter.pair(3)
+
+
+def feed_input_back(place, rows, scatter, middle, gains_ref, out_gains, current, result, full_b):
+    out_gains[1:2, :] = jnp.zeros_like(out_gains[1:2, :])
+
+    def feed_norm(span, value):
+        back, gain_term = norm_back(middle[span, :], gains_ref[1:2, :], value)
+        out_gains[1:2, :] += jnp.sum(gain_term, axis=0, keepdims=True)
+        total = back + current[span, :].astype(jnp.float32)
+        result[span, :] = total
+        base = pl.multiple_of(place.index * rows + span.start, 16)
+        full_b[pl.ds(base, 16), :] = total.astype(jnp.bfloat16)
+
+    scatter.total(feed_norm)
+
+
+def attention_back(
+    heads, grad_mixed, first_key, grad_queries, grad_keys, grad_values, chip_rows
+):
+    grad_keys[...] = jnp.zeros_like(grad_keys)
+    grad_values[...] = jnp.zeros_like(grad_values)
+    for block in range(heads.shape[0] // chip_rows):
+        span = pl.ds(block * chip_rows, chip_rows)
+        seen = (block + 1) * chip_rows
+        keys = heads[:seen, 2 * HEAD_SIZE : 3 * HEAD_SIZE]
+        values = heads[:seen, 3 * HEAD_SIZE :]
+        for at in range(2):
+            columns = pl.ds(at * HEAD_SIZE, HEAD_SIZE)
+            queries = heads[span, columns]
+            grad = grad_mixed[span, columns]
+            probs = probabilities(queries, keys, first_key[span, :], block * chip_rows)
+            grad_probs = mm_t(grad, values)
+            grad_scores = (
+                probs * (grad_probs - jnp.sum(probs * grad_probs, axis=-1, keepdims=True))
+            ).astype(jnp.bfloat16)
+            grad_queries[span, columns] = mm(grad_scores, keys) * HEAD_SIZE ** (-0.5)
+            grad_keys[:seen, :] += t_mm(grad_scores, queries) * HEAD_SIZE ** (-0.5)
+            grad_values[:seen, :] += t_mm(probs.astype(jnp.bfloat16), grad)
+
+
+def project_back(
+    place, rows, scatter, buffers, head_gain_ref, out_head_gain, wh
+):
+    projected, grad_projected = buffers.projected, buffers.grad_projected
+    grad_queries, grad_keys, grad_values = buffers.attention_grads
+    cosine, sine, _ = buffers.tables
+    out_head_gain[...] = jnp.zeros_like(out_head_gain)
+
+    def project_block(rel):
+        span = block_rows(place, rel, rows)
+        for at in range(3):
+            columns = pl.ds(at * HEAD_SIZE, HEAD_SIZE)
+            which = 0 if at < 2 else 1
+            upstream = grad_queries[span, columns] if at < 2 else grad_keys[span, :]
+            back, gain_term = norm_back(
+                projected[span, columns],
+                head_gain_ref[which : which + 1, :],
+                turn_back(upstream, cosine[span, :], sine[span, :]),
+            )
+            out_head_gain[which : which + 1, :] += jnp.sum(gain_term, axis=0, keepdims=True)
+            grad_projected[span, columns] = back.astype(jnp.bfloat16)
+        grad_projected[span, 3 * HEAD_SIZE :] = grad_values[span, :].astype(jnp.bfloat16)
+        scatter.put(rel, lambda columns: mm_t(grad_projected[span, :], wh[columns, :]), wh.shape[0])
+
+    project_block(3)
+    scatter.pair(3)
+    project_block(2)
+    scatter.pair(2)
+    project_block(1)
+    scatter.pair(1)
+    project_block(0)
+
+
+def input_back(scatter, inputs, gains_ref, out_gains, result, result_b):
+    out_gains[0:1, :] = jnp.zeros_like(out_gains[0:1, :])
+
+    def mixer_norm(span, value):
+        back, gain_term = norm_back(inputs[span, :].astype(jnp.float32), gains_ref[0:1, :], value)
+        out_gains[0:1, :] += jnp.sum(gain_term, axis=0, keepdims=True)
+        total = back + result[span, :]
+        result[span, :] = total
+        if result_b is not None:
+            result_b[span, :] = total.astype(jnp.bfloat16)
+
+    scatter.total(mixer_norm)
+
+
+def layer_backward_step(place, rows, refs, buffers, slot, hooks):
+    (wh, wm, we, wr), gains_ref = refs.weights, refs.gains
+    current, middle, result, result_b, inputs = (
+        buffers.current,
+        buffers.middle,
+        buffers.result,
+        buffers.result_b,
+        buffers.inputs,
+    )
+    full_a, full_b, joined = buffers.full_a, buffers.full_b, buffers.joined
+    save_sem, grad_joined = buffers.save_sem, buffers.grad_joined
+    tables = [
+        pltpu.make_async_copy(src.at[slot], dst, buffers.table_sem.at[at])
+        for at, (src, dst) in enumerate(
+            [
+                *zip(refs.tables, buffers.tables),
+                (refs.middle, middle),
+                (refs.projected, buffers.projected),
+                (refs.heads, buffers.heads),
+                (refs.inputs, inputs),
+            ]
+        )
+    ]
+    for table in tables:
+        table.start()
+
+    def joined_load(rel):
+        return pltpu.make_async_copy(
+            refs.joined.at[slot, block_rows(place, rel, rows)],
+            joined.at[rel % 2],
+            buffers.joined_sem.at[rel % 2],
+        )
+
+    joined_load(0).start()
+    joined_load(1).start()
+    own_rows = pl.ds(pl.multiple_of(place.index * rows, rows), rows)
+    full_a[own_rows, :] = current[...]
+
+    def save(at, src, dst):
+        copy = pltpu.make_async_copy(src, dst.at[slot], save_sem.at[at])
+        copy.start()
+        return copy
+
+    gather = Gather(place, full_a, *buffers.gather_a, rows)
+    scatter = Scatter(place, *buffers.scatter, *buffers.scatter_a, rows)
+    def out_of(rel):
+        return grad_joined.at[block_rows(place, rel, rows)]
+
+    feed_back(
+        place,
+        rows,
+        gather,
+        scatter,
+        full_a,
+        (wm, we, wr),
+        joined,
+        joined_load,
+        out_of,
+        lambda rel, out: None,
+    )
+    upstream_save = save(0, full_a, refs.upstream)
+    scatter.relay()
+    for table in tables:
+        table.wait()
+    out_gains = refs.out_gains.at[slot]
+    feed_input_back(place, rows, scatter, middle, gains_ref, out_gains, current, result, full_b)
+    gather.finish()
+    upstream_save.wait()
+    gather_b = Gather(place, full_b, *buffers.gather_b, rows)
+    scatter_b = Scatter(place, *buffers.scatter, *buffers.scatter_b, rows)
+    grad_mixed = buffers.mixed
+
+    def mixed_block(rel):
+        span = block_rows(place, rel, rows)
+        grad_mixed[span, :] = mm_t(full_b[span, :], wm[...]).astype(jnp.bfloat16)
+
+    gather_b.over_blocks(mixed_block, early=hooks.early)
+    middle_save = save(1, full_b, refs.grad_middle)
+    attention_back(
+        buffers.heads,
+        grad_mixed,
+        buffers.tables[2],
+        *buffers.attention_grads,
+        2 * rows,
+    )
+    project_back(
+        place, rows, scatter_b, buffers, refs.head_gain, refs.out_head_gain.at[slot], wh
+    )
+    projected_save = save(2, buffers.grad_projected, refs.grad_projected)
+    hooks.early(5)
+    scatter_b.relay()
+    scatter_b.pair(0)
+    hooks.finish()
+    input_back(scatter_b, inputs, gains_ref, out_gains, result, result_b)
+    hooks.hand()
+    gather_b.finish()
+    for copy in (middle_save, projected_save):
+        copy.wait()
+
+
+class Saved(typing.NamedTuple):
+    inputs: typing.Any
+    normal_a: typing.Any
+    projected: typing.Any
+    heads: typing.Any
+    mixed: typing.Any
+    middle: typing.Any
+    normal_b: typing.Any
+    joined: typing.Any
+    hidden: typing.Any
+    upstream: typing.Any
+    grad_middle: typing.Any
+    grad_projected: typing.Any
+
+
+class Layers(typing.NamedTuple):
+    rows: typing.Any
+    saved: Saved
+    handed: typing.Any
+    own_first: typing.Any
+    other_first: typing.Any
+    other_normal: typing.Any
+    heads_w: typing.Any
+    expand_w: typing.Any
+    gains: typing.Any
+    head_gain: typing.Any
+    gain_terms: typing.Any
+    head_terms: typing.Any
+
+
+class LayerBuffers(typing.NamedTuple):
+    current: typing.Any
+    inputs: typing.Any
+    middle: typing.Any
+    result: typing.Any
+    result_b: typing.Any
+    full_a: typing.Any
+    full_b: typing.Any
+    projected: typing.Any
+    heads: typing.Any
+    mixed: typing.Any
+    joined: typing.Any
+    hidden: typing.Any
+    grad_joined: typing.Any
+    grad_projected: typing.Any
+
+
+class GradientBuffers(typing.NamedTuple):
+    current: typing.Any
+    inputs: typing.Any
+    result: typing.Any
+    full_a: typing.Any
+    full_b: typing.Any
+    projected: typing.Any
+    heads: typing.Any
+    mixed: typing.Any
+    joined: typing.Any
+    grad_projected: typing.Any
+
+
+def layers_kernel(rows, *refs):
+    refs = list(refs)
+
+    def some(count):
+        taken = refs[:count]
+        del refs[:count]
+        return taken
+
+    own_ref, gain_ref = some(2)
+    table_refs = some(3)
+    heads_w, merge_w, expand_w, reduce_w = some(4)
+    (out_rows,) = some(1)
+    saved = types.SimpleNamespace(**Saved(*some(12))._asdict())
+    out_handed, own_first, other_first, other_normal = some(4)
+    out_heads_w, out_expand_w = some(2)
+    gains_ref, head_gain_ref, out_gains, out_head_gain = some(4)
+    all_gains, wh, wm, we, wr, arrived = some(6)
+    buffers = types.SimpleNamespace(**LayerBuffers(*some(14))._asdict())
+    buffers.tables = some(3)
+    buffers.attention_grads = some(3)
+    buffers.scatter = some(7)
+    first_tiles, first_turned, first_stage = some(3)
+    load_sem, spread_send, spread_recv = some(3)
+    share_send, share_recv = some(2)
+    tile_sem, first_sem, first_send, first_recv, normal_send, normal_recv = some(6)
+    buffers.save_sem, buffers.table_sem, buffers.joined_sem = some(3)
+    hand_send, hand_recv, out_sem = some(3)
+    buffers.gather_a, buffers.scatter_a = some(2), some(2)
+    buffers.gather_b, buffers.scatter_b = some(2), some(2)
+    saved.weights, saved.tables = (wh, wm, we, wr), table_refs
+    saved.gains, saved.head_gain = gains_ref, head_gain_ref
+    saved.out_gains, saved.out_head_gain = out_gains, out_head_gain
+    place = Place()
+    head = place.section == 0
+    rest = jnp.logical_not(head)
+    hidden_width = wr.shape[0]
+    depth = heads_w.shape[0]
+    query_width, key_width = QUERY_HEADS * HEAD_SIZE, KEY_VALUE_HEADS * HEAD_SIZE
+    loads = [
+        pltpu.make_async_copy(src, dst, load_sem.at[at])
+        for at, (src, dst) in enumerate(((merge_w, wm), (reduce_w, wr)))
+    ]
+    for load in loads:
+        load.start()
+    shard_rows = pl.ds(pl.multiple_of(place.index * depth, depth), depth)
+
+    def spread(at, device, piece, src, dst):
+        if at < 7:
+            return remote(
+                src, dst, spread_send.at[piece, at], spread_recv.at[piece, at], {"fsdp": device}
+            )
+        return pltpu.make_async_copy(src, dst, load_sem.at[2 + piece])
+
+    gain_copies = [
+        spread(at, device, 0, gain_ref, all_gains.at[place.index])
+        for at, device in place.others()
+    ]
+    heads_copies, expand_copies = [], []
+    for at, device in place.others():
+        for piece, first, count, into in (
+            (1, 0, MERGED, 0),
+            (2, query_width, HEAD_SIZE, MERGED),
+            (3, query_width + key_width, HEAD_SIZE, MERGED + HEAD_SIZE),
+        ):
+            src = heads_w.at[:, shard_columns(first, device, count)]
+            heads_copies.append(
+                spread(at, device, piece, src, wh.at[shard_rows, pl.ds(into, count)])
+            )
+        for piece in range(2):
+            src = expand_w.at[:, shard_columns(piece * FF, device, hidden_width)]
+            dst = we.at[shard_rows, pl.ds(piece * hidden_width, hidden_width)]
+            expand_copies.append(spread(at, device, 4 + piece, src, dst))
+
+    def arrive(copies, pieces):
+        for copy in copies[:-pieces]:
+            copy.wait_recv()
+        for copy in copies[-pieces:]:
+            copy.wait()
+
+    heads_out = pltpu.make_async_copy(wh, out_heads_w, load_sem.at[8])
+    expand_out = pltpu.make_async_copy(we, out_expand_w, load_sem.at[9])
+
+    def share(at, device, kind, weight):
+        block = weight.at[pl.ds(pl.multiple_of(device * depth, depth), depth)]
+        return remote(
+            block, block, share_send.at[kind, at], share_recv.at[kind, at], place.rep_peer
+        )
+
+    def start_all(copies, pieces, shared, first=0, last=PLANE):
+        for at, device in place.others()[first:last]:
+            mine = copies[at * pieces : (at + 1) * pieces]
+
+            def begin():
+                for copy in mine:
+                    copy.start()
+
+            if at < shared:
+                pl.when(place.replica == at % 2)(begin)
+            else:
+                begin()
+
+    def pass_on(copies, pieces, kind, weight, first, last):
+        for at, device in place.others()[first:last]:
+            mine = copies[at * pieces : (at + 1) * pieces]
+
+            @pl.when(place.replica == at % 2)
+            def _():
+                for copy in mine:
+                    copy.wait_recv()
+                share(at, device, kind, weight).start()
+
+    def take_shared(kind, weight, shared):
+        for at, device in place.others()[:shared]:
+
+            @pl.when(place.replica != at % 2)
+            def _():
+                share(at, device, kind, weight).wait_recv()
+
+    def sent(copies, pieces, kind, weight, shared):
+        for at, device in place.others()[:7]:
+            mine = copies[at * pieces : (at + 1) * pieces]
+
+            def settle():
+                for copy in mine:
+                    copy.wait_send()
+                if at < shared:
+                    share(at, device, kind, weight).wait_send()
+
+            if at < shared:
+                pl.when(place.replica == at % 2)(settle)
+            else:
+                settle()
+
+    place.greet(
+        [{"fsdp": device} for _, device in place.others()[:7]]
+        + [place.section_peer, place.rep_peer]
+    )
+    for copy in gain_copies:
+        copy.start()
+    start_all(heads_copies, 3, 2)
+
+    arrive(gain_copies, 1)
+    for shard in range(PLANE):
+        part = slice(shard * depth, (shard + 1) * depth)
+        gains_ref[0:1, part] = all_gains[shard][:, :depth]
+        gains_ref[1:2, part] = all_gains[shard][:, depth : 2 * depth]
+    per_row = PLANE // 2
+    count = 2 * HEAD_SIZE // PLANE
+    for row in range(2):
+        head_gain_ref[row : row + 1, :] = jnp.concatenate(
+            [
+                all_gains[row * per_row + at][:, 2 * depth : 2 * depth + count]
+                for at in range(per_row)
+            ],
+            axis=1,
+        )
+
+    current, result, result_b = buffers.current, buffers.result, buffers.result_b
+    length = buffers.full_a.shape[0]
+
+    def tile_rows(at):
+        return pl.ds(at * depth, depth)
+
+    def first_tile(at):
+        return pltpu.make_async_copy(
+            saved.normal_b.at[0, :, tile_rows(at)], first_tiles.at[at % 2], tile_sem.at[at % 2]
+        )
+
+    def first_save(at):
+        return pltpu.make_async_copy(
+            first_stage.at[at % 2], own_first.at[tile_rows(at)], first_sem.at[at % 2]
+        )
+
+    def first_copy(at):
+        block = tile_rows(at)
+        return remote(
+            own_first.at[block],
+            other_first.at[block],
+            first_send.at[at],
+            first_recv.at[at],
+            place.rep_peer,
+        )
+
+    def early_tile(at):
+        first_tile(at).wait()
+
+        @pl.loop(0, length // 256)
+        def _(chunk):
+            span = pl.ds(pl.multiple_of(chunk * 256, 256), 256)
+            first_turned[:, span] = first_tiles[at % 2, span, :].T
+
+        if at + 2 < PLANE:
+            first_tile(at + 2).start()
+
+        @pl.loop(0, 2 * hidden_width // 512)
+        def _(chunk):
+            columns = pl.ds(pl.multiple_of(chunk * 512, 512), 512)
+            first_stage[at % 2, :, columns] = mm(
+                first_turned[...], buffers.grad_joined[:, columns]
+            ).astype(jnp.bfloat16)
+
+        first_save(at).start()
+        if at:
+            first_save(at - 1).wait()
+            pl.when(head)(first_copy(at - 1).start)
+        if at == PLANE - 1:
+            first_save(at).wait()
+            pl.when(head)(first_copy(at).start)
+
+    half = length // 2
+    half_rows = pl.ds(pl.multiple_of(place.core * half, half), half)
+    normal_copy = remote(
+        saved.normal_b.at[1, half_rows],
+        other_normal.at[half_rows],
+        normal_send.at[0],
+        normal_recv.at[0],
+        place.rep_peer,
+    )
+    normal_pass = remote(
+        other_normal.at[half_rows],
+        other_normal.at[half_rows],
+        normal_send.at[1],
+        normal_recv.at[1],
+        place.core_peer,
+    )
+
+    def hand(slot):
+        return remote(
+            result_b, arrived.at[slot], hand_send.at[slot], hand_recv.at[slot], place.section_peer
+        )
+
+    def rows_copy(slot):
+        return pltpu.make_async_copy(result, out_rows.at[slot], out_sem.at[0])
+
+    def save_rows(slot):
+        copy = rows_copy(slot)
+        copy.start()
+        copy.wait()
+
+    def heads_ready():
+        pass_on(heads_copies, 3, 0, wh, 0, 2)
+        arrive(heads_copies[6:], 3)
+        take_shared(0, wh, 2)
+        heads_out.start()
+        start_all(expand_copies, 2, 2, 0, 2)
+
+    def expand_service():
+        pass_on(expand_copies, 2, 1, we, 0, 2)
+        start_all(expand_copies, 2, 2, 2)
+
+    def feed_ready():
+        arrive(expand_copies[4:], 2)
+        take_shared(1, we, 2)
+        expand_out.start()
+
+    @pl.when(rest)
+    def _():
+        heads_ready()
+        expand_service()
+        feed_ready()
+
+    for load in loads:
+        load.wait()
+
+    @pl.loop(0, 5)
+    def _(step):
+        forward = (head & (step <= 1)) | (rest & ((step == 1) | (step == 3)))
+        backward = (step == 4) | (rest & (step == 2))
+
+        @pl.when(forward)
+        def _():
+            slot = jnp.where(head, step, lax.div(step - 1, 2))
+
+            @pl.when(head)
+            def _():
+                current[...] = own_ref[slot]
+
+            @pl.when(rest)
+            def _():
+                hand(slot).wait_recv()
+                current[...] = arrived[slot]
+
+            def first(body):
+                return lambda: pl.when(head & (slot == 0))(body)
+
+
+            def finish():
+                @pl.when(slot == 1)
+                def _():
+                    hand(0).wait_send()
+
+            def handing():
+                @pl.when(head)
+                def _():
+                    hand(slot).start()
+
+                @pl.when(rest)
+                def _():
+                    save_rows(slot)
+
+            def after():
+                pl.when(slot == 1)(normal_copy.start)
+
+            layer_forward_step(
+                place,
+                rows,
+                saved,
+                buffers,
+                slot,
+                step,
+                types.SimpleNamespace(
+                    heads=first(heads_ready),
+                    feed=first(feed_ready),
+                    service=first(expand_service),
+                    finish=finish,
+                    hand=handing,
+                    after=after,
+                ),
+            )
+
+        @pl.when(backward)
+        def _():
+            slot = jnp.where(head, 0, lax.div(step - 2, 2))
+
+            @pl.when(head)
+            def _():
+                hand(0).wait_recv()
+                current[...] = arrived[0]
+
+            @pl.when(rest)
+            def _():
+                current[...] = own_ref[slot]
+
+            def finish():
+                @pl.when(head)
+                def _():
+                    hand(1).wait_send()
+
+            def handing():
+                @pl.when(rest)
+                def _():
+                    hand(slot).start()
+
+                @pl.when(rest & (slot == 0))
+                def _():
+                    for at in range(PLANE):
+                        first_copy(at).start()
+
+                @pl.when(head)
+                def _():
+                    rows_copy(slot).start()
+
+            def early(at):
+                groups = ((), (0, 1, 2), (3,), (4,), (5, 6), (7,))
+
+                @pl.when(slot == 0)
+                def _():
+                    if at == 0:
+                        first_tile(0).start()
+                        first_tile(1).start()
+                    for tile in groups[at]:
+                        early_tile(tile)
+
+            hooks = types.SimpleNamespace(finish=finish, hand=handing, early=early)
+            layer_backward_step(place, rows, saved, buffers, slot, hooks)
+
+    @pl.when(head)
+    def _():
+        hand(1).wait_recv()
+        current[...] = arrived[1]
+
+    @pl.when(rest)
+    def _():
+        hand(1).wait_send()
+        current[...] = own_ref[1]
+
+    handed = pltpu.make_async_copy(current, out_handed, out_sem.at[1])
+    handed.start()
+    normal_copy.wait_recv()
+    normal_pass.start()
+    heads_out.wait()
+    expand_out.wait()
+    for copy in gain_copies[:7]:
+        copy.wait_send()
+    sent(heads_copies, 3, 0, wh, 2)
+    sent(expand_copies, 2, 1, we, 2)
+    for at in range(PLANE):
+        first_copy(at).wait()
+    normal_copy.wait_send()
+    normal_pass.wait()
+    handed.wait()
+    pl.when(head)(lambda: rows_copy(0).wait())
+
+
+def gradient_kernel(rows, *refs):
+    refs = list(refs)
+
+    def some(count):
+        taken = refs[:count]
+        del refs[:count]
+        return taken
+
+    gains_ref, head_gain_ref, first_gains, first_head_gain = some(4)
+    table_refs = some(3)
+    heads_w, merge_w, expand_w, reduce_w = some(4)
+    in_handed, in_inputs, in_projected, in_heads, in_middle, in_joined = some(6)
+    hidden_all, upstream_all, normal_b_all, other_normal = some(4)
+    mixed_all, grad_middle_all, normal_a_all, grad_projected_all = some(4)
+    own_first, other_first = some(2)
+    (out_result,) = some(1)
+    own_heads, other_heads, own_merge, other_merge = some(4)
+    own_expand, own_reduce, other_reduce = some(3)
+    (out_gain,) = some(1)
+    wh, wm, we, wr = some(4)
+    buffers = types.SimpleNamespace(**GradientBuffers(*some(10))._asdict())
+    buffers.tables = some(3)
+    buffers.attention_grads = some(3)
+    buffers.scatter = some(7)
+    tiles, turned, wide, narrow, first_projected = some(5)
+    gains, head_gain, gain_out, gain_in, gain_sum, gain_other = some(6)
+    load_sem, tile_sem, joined_sem, save_sem = some(4)
+    buffers.gather_a, buffers.scatter_a = some(2), some(2)
+    buffers.gather_b, buffers.scatter_b = some(2), some(2)
+    spread_send, spread_recv, rep_send, rep_recv = some(4)
+    current, inputs, result = buffers.current, buffers.inputs, buffers.result
+    full_a, full_b, grad_mixed = buffers.full_a, buffers.full_b, buffers.mixed
+    joined, grad_projected = buffers.joined, buffers.grad_projected
+
+    place = Place()
+    length, width = full_a.shape
+    depth = wm.shape[0]
+    hidden_width = wr.shape[0]
+    last = in_inputs.shape[0] - 1
+    tokens = narrow.shape[0]
+    query_width, key_width = QUERY_HEADS * HEAD_SIZE, KEY_VALUE_HEADS * HEAD_SIZE
+    others = place.others()
+
+    def load(at, src, dst):
+        copy = pltpu.make_async_copy(src, dst, load_sem.at[at])
+        copy.start()
+        return copy
+
+    upstream_load = load(0, in_handed, current)
+    reduce_load = load(1, reduce_w, wr)
+
+    def joined_load(rel):
+        return pltpu.make_async_copy(
+            in_joined.at[last, block_rows(place, rel, rows)],
+            joined.at[rel % 2],
+            joined_sem.at[rel % 2],
+        )
+
+    joined_load(0).start()
+    joined_load(1).start()
+    expand_load = load(2, expand_w, we)
+    middle_load = load(3, in_middle.at[last], result)
+    wide_load = load(4, upstream_all.at[0], wide)
+    plain = [(hidden_all, at) for at in range(hidden_width // depth)] + [(mixed_all, 0)]
+    plain += [(normal_a_all, device) for _, device in others]
+    job_count = len(plain) + len(others)
+
+    def token_rows(replica):
+        return pl.ds(pl.multiple_of(replica * length, length), length)
+
+    def tile_loads(job):
+        source, at = plain[job] if job < len(plain) else (None, others[job - len(plain)][1])
+        columns = pl.ds(pl.multiple_of(at * depth, depth), depth)
+        if source is not None:
+            return [
+                pltpu.make_async_copy(
+                    source.at[:, columns], tiles.at[job % 2], tile_sem.at[job % 2, 0]
+                )
+            ]
+        parts = (
+            (normal_b_all.at[last, :, columns], place.replica),
+            (other_normal.at[:, columns], 1 - place.replica),
+        )
+        return [
+            pltpu.make_async_copy(
+                src, tiles.at[job % 2, token_rows(replica)], tile_sem.at[job % 2, part]
+            )
+            for part, (src, replica) in enumerate(parts)
+        ]
+
+    def tile_start(job):
+        for copy in tile_loads(job):
+            copy.start()
+
+    def take(job):
+        for copy in tile_loads(job):
+            copy.wait()
+
+        @pl.loop(0, tokens // 256)
+        def _(at):
+            span = pl.ds(pl.multiple_of(at * 256, 256), 256)
+            turned[:, span] = tiles[job % 2, span, :].T
+
+        if job + 2 < job_count:
+            tile_start(job + 2)
+
+    tile_start(0)
+    tile_start(1)
+    projected_load = load(5, grad_projected_all.at[0], first_projected)
+    loads = [
+        load(at + 6, src, dst)
+        for at, (src, dst) in enumerate(
+            [(merge_w, wm), (heads_w, wh)]
+            + [(src.at[last], dst) for src, dst in zip(table_refs, buffers.tables)]
+            + [
+                (in_projected.at[last], buffers.projected),
+                (in_heads.at[last], buffers.heads),
+                (in_inputs.at[last], inputs),
+            ]
+        )
+    ]
+    place.greet([{"fsdp": device} for _, device in others[:7]] + [place.rep_peer])
+
+    def rep_copy(at, src, dst):
+        return remote(src, dst, rep_send.at[at], rep_recv.at[at], place.rep_peer)
+
+    def spread(at, device, piece, src, dst):
+        if at < 7:
+            return remote(
+                src, dst, spread_send.at[piece, at], spread_recv.at[piece, at], {"fsdp": device}
+            )
+        return pltpu.make_async_copy(src, dst, save_sem.at[4 + piece])
+
+    upstream_load.wait()
+    own_rows = pl.ds(pl.multiple_of(place.index * rows, rows), rows)
+    full_a[own_rows, :] = current[...]
+    reduce_load.wait()
+    expand_load.wait()
+    gather = Gather(place, full_a, *buffers.gather_a, rows)
+    scatter = Scatter(place, *buffers.scatter, *buffers.scatter_a, rows)
+
+    joined_reps = []
+
+    def out_of(rel):
+        first = place.replica * length + place.chip_at(rel) * 2 * rows
+        return narrow.at[pl.ds(pl.multiple_of(first, 2 * rows), 2 * rows)]
+
+    def done(rel, out):
+        copy = rep_copy(4 + rel, out, out)
+        copy.start()
+        joined_reps.append(copy)
+
+    feed_back(
+        place,
+        rows,
+        gather,
+        scatter,
+        full_a,
+        (wm, we, wr),
+        joined,
+        joined_load,
+        out_of,
+        done,
+    )
+    wide_load.wait()
+    own_saves, rep_copies = [], []
+    for at in range(hidden_width // depth):
+        take(at)
+        span = pl.ds(at * depth, depth)
+
+        @pl.loop(0, width // 512)
+        def _(chunk):
+            columns = pl.ds(pl.multiple_of(chunk * 512, 512), 512)
+            value = mm(turned[:, :length], wide[:, columns])
+            value += mm(turned[:, length:], full_a[:, columns])
+            wr[span, columns] = value.astype(jnp.bfloat16)
+
+        copy = rep_copy(at, wr.at[span], other_reduce.at[span])
+        copy.start()
+        rep_copies.append(copy)
+        copy = pltpu.make_async_copy(wr.at[span], own_reduce.at[span], save_sem.at[at])
+        copy.start()
+        own_saves.append(copy)
+        if at == 1:
+            scatter.relay()
+    grad_middle_load = load(4, grad_middle_all.at[0], wide)
+    middle_load.wait()
+    feed_input_back(place, rows, scatter, result, gains_ref, gains, current, result, full_b)
+    gather.finish()
+    gather_b = Gather(place, full_b, *buffers.gather_b, rows)
+    scatter_b = Scatter(place, *buffers.scatter, *buffers.scatter_b, rows)
+    gather_b.start()
+    for copy in loads:
+        copy.wait()
+    gather_b.relay()
+    gather_b.near()
+    gather_b.far()
+    for rel, at in ((0, 4), (1, 7), (2, 8), (3, 9)):
+        gather_b.wait(at)
+        span = block_rows(place, rel, rows)
+        grad_mixed[span, :] = mm_t(full_b[span, :], wm[...]).astype(jnp.bfloat16)
+    attention_back(
+        buffers.heads,
+        grad_mixed,
+        buffers.tables[2],
+        *buffers.attention_grads,
+        2 * rows,
+    )
+    project_back(place, rows, scatter_b, buffers, head_gain_ref, head_gain, wh)
+    job = hidden_width // depth
+    grad_middle_load.wait()
+    take(job)
+    job += 1
+
+    @pl.loop(0, width // 512)
+    def _(chunk):
+        columns = pl.ds(pl.multiple_of(chunk * 512, 512), 512)
+        value = mm(turned[:, :length], wide[:, columns])
+        value += mm(turned[:, length:], full_b[:, columns])
+        wm[:, columns] = value.astype(jnp.bfloat16)
+
+    merge_rep = rep_copy(3, wm, other_merge)
+    merge_rep.start()
+    merge_save = pltpu.make_async_copy(wm, own_merge, save_sem.at[3])
+    merge_save.start()
+    scatter_b.relay()
+    scatter_b.pair(0)
+    input_back(scatter_b, inputs, gains_ref, gains, result, None)
+    result_save = pltpu.make_async_copy(result, out_result, save_sem.at[10])
+    result_save.start()
+
+    gain_copies = []
+    gains[...] += first_gains[0]
+    head_gain[...] += first_head_gain[0]
+    per_row = PLANE // 2
+    count = 2 * HEAD_SIZE // PLANE
+    for shard in range(PLANE):
+        part = slice(shard * depth, (shard + 1) * depth)
+        lanes = slice(shard % per_row * count, (shard % per_row + 1) * count)
+        row = shard // per_row
+        gain_out[shard] = jnp.zeros_like(gain_out[shard])
+        gain_out[shard, :, :depth] = gains[0:1, part]
+        gain_out[shard, :, depth : 2 * depth] = gains[1:2, part]
+        gain_out[shard, :, 2 * depth : 2 * depth + count] = head_gain[row : row + 1, lanes]
+    for at, device in others:
+        copy = spread(at, device, 5, gain_out.at[device], gain_in.at[place.index])
+        copy.start()
+        gain_copies.append(copy)
+
+    projected_load.wait()
+    heads_copies = []
+    for at, device in others:
+        take(job)
+        job += 1
+        value = mm(turned[:, :length], first_projected[...])
+        value += mm(turned[:, length:], grad_projected[...])
+        block = pl.ds(at * depth, depth)
+        wh[block, :] = value.astype(jnp.bfloat16)
+        for piece, first, count, start in (
+            (2, 0, MERGED, 0),
+            (3, query_width, HEAD_SIZE, MERGED),
+            (4, query_width + key_width, HEAD_SIZE, MERGED + HEAD_SIZE),
+        ):
+            copy = spread(
+                at,
+                device,
+                piece,
+                wh.at[block, pl.ds(start, count)],
+                own_heads.at[:, shard_columns(first, place.index, count)],
+            )
+            copy.start()
+            heads_copies.append(copy)
+    def first_loads(at, device):
+        block = pl.ds(pl.multiple_of(device * depth, depth), depth)
+        return [
+            pltpu.make_async_copy(
+                src.at[block],
+                wide.at[
+                    pl.ds((2 * (at % 2) + part) * depth, depth), pl.ds(0, 2 * hidden_width)
+                ],
+                load_sem.at[14 + 2 * (at % 2) + part],
+            )
+            for part, src in enumerate((own_first, other_first))
+        ]
+
+    for at, device in others[:2]:
+        for copy in first_loads(at, device):
+            copy.start()
+    for copy in joined_reps:
+        copy.wait_recv()
+    expand_copies = []
+    for at, device in others:
+        take(job)
+        job += 1
+        block = pl.ds(at * depth, depth)
+        for copy in first_loads(at, device):
+            copy.wait()
+        mine = pl.ds(2 * (at % 2) * depth, depth)
+        theirs = pl.ds((2 * (at % 2) + 1) * depth, depth)
+
+        @pl.loop(0, narrow.shape[1] // 512)
+        def _(chunk):
+            columns = pl.ds(pl.multiple_of(chunk * 512, 512), 512)
+            value = wide[mine, columns].astype(jnp.float32)
+            value += wide[theirs, columns].astype(jnp.float32)
+            value += mm(turned[...], narrow[:, columns])
+            we[block, columns] = value.astype(jnp.bfloat16)
+
+        if at + 2 < PLANE:
+            for copy in first_loads(*others[at + 2]):
+                copy.start()
+        for piece in range(2):
+            copy = spread(
+                at,
+                device,
+                piece,
+                we.at[block, pl.ds(piece * hidden_width, hidden_width)],
+                own_expand.at[:, shard_columns(piece * FF, place.index, hidden_width)],
+            )
+            copy.start()
+            expand_copies.append(copy)
+        if at == 3:
+            for copy in heads_copies[:21]:
+                copy.wait_recv()
+            for copy in heads_copies[21:]:
+                copy.wait()
+            heads_rep = rep_copy(8, own_heads, other_heads)
+            heads_rep.start()
+            for copy in gain_copies[:7]:
+                copy.wait_recv()
+            gain_copies[7].wait()
+            total = gain_in[0]
+            for shard in range(1, PLANE):
+                total += gain_in[shard]
+            gain_sum[...] = total
+            gain_rep = rep_copy(9, gain_sum, gain_other)
+            gain_rep.start()
+    gain_rep.wait()
+    out_gain[...] = gain_sum[...] + gain_other[...]
+    gather_b.finish()
+    for copy in expand_copies[:14]:
+        copy.wait_recv()
+    for copy in expand_copies[14:] + own_saves + [result_save, merge_save]:
+        copy.wait()
+    for copy in expand_copies[:14] + heads_copies[:21] + gain_copies[:7] + joined_reps:
+        copy.wait_send()
+    for copy in rep_copies + [merge_rep, heads_rep]:
+        copy.wait()
+
+
+def sems(*counts):
+    return [pltpu.SemaphoreType.DMA((count,)) for count in counts]
+
+
+def vmem(*shapes):
+    return [pltpu.VMEM(shape, dtype) for *shape, dtype in shapes]
+
+
+def any_specs(count):
+    return [pl.BlockSpec(memory_space=pl.ANY)] * count
+
+
+def vmem_specs(count):
+    return [pl.BlockSpec(memory_space=pltpu.VMEM)] * count
+
+
+def kernel_params(collective_id):
+    return pltpu.CompilerParams(
+        collective_id=collective_id, has_side_effects=True, vmem_limit_bytes=VMEM_BYTES
+    )
+
+
+def weight_buffers(width, hidden_width):
+    b16 = jnp.bfloat16
+    return vmem(
+        (width, JOINT, b16),
+        (MERGED, width, b16),
+        (width, 2 * hidden_width, b16),
+        (hidden_width, width, b16),
+    )
+
+
+def table_buffers(length):
+    return vmem(
+        (length, HEAD_SIZE, jnp.float32),
+        (length, HEAD_SIZE, jnp.float32),
+        (length, 1, jnp.int32),
+    )
+
+
+def attention_buffers(length):
+    return vmem(
+        (length, MERGED, jnp.float32),
+        (length, HEAD_SIZE, jnp.float32),
+        (length, HEAD_SIZE, jnp.float32),
+    )
+
+
+def scatter_buffers(rows, width):
+    half, b16 = rows // 2, jnp.bfloat16
+    return vmem(
+        (4, rows, width, jnp.float32),
+        (4, rows, width, b16),
+        (4, rows, width, b16),
+        *(((3, half, width, b16),) * 4),
+    )
+
+
+def run_layers(own, gain_row, tables, weights):
+    micro, rows, width = own.shape
+    length = tables[0].shape[1]
+    hidden_width, depth = weights[3].shape[0], weights[0].shape[0]
+    f32, b16 = jnp.float32, jnp.bfloat16
+    shape = jax.ShapeDtypeStruct
+    stashes = (
+        (rows, width, b16),
+        (length, width, b16),
+        (length, JOINT, f32),
+        (length, JOINT, b16),
+        (length, MERGED, b16),
+        (rows, width, f32),
+        (length, width, b16),
+        (length, 2 * hidden_width, f32),
+        (length, hidden_width, b16),
+        (length, width, b16),
+        (length, width, b16),
+        (length, JOINT, b16),
+    )
+    out = pl.pallas_call(
+        functools.partial(layers_kernel, rows),
+        out_shape=(
+            shape((micro, rows, width), f32),
+            *(shape((micro, *size), dtype) for *size, dtype in stashes),
+            shape((rows, width), b16),
+            shape((width, 2 * hidden_width), b16),
+            shape((width, 2 * hidden_width), b16),
+            shape((length, width), b16),
+            shape((width, JOINT), b16),
+            shape((width, 2 * hidden_width), b16),
+            shape((2, width), f32),
+            shape((2, HEAD_SIZE), f32),
+            shape((micro, 2, width), f32),
+            shape((micro, 2, HEAD_SIZE), f32),
+        ),
+        in_specs=vmem_specs(2) + any_specs(7),
+        out_specs=any_specs(19) + vmem_specs(4),
+        scratch_shapes=vmem((PLANE, *gain_row.shape, f32))
+        + weight_buffers(width, hidden_width)
+        + vmem(
+            (micro, rows, width, b16),
+            (rows, width, b16),
+            (rows, width, b16),
+            (rows, width, f32),
+            (rows, width, f32),
+            (rows, width, b16),
+            (length, width, b16),
+            (length, width, b16),
+            (length, JOINT, f32),
+            (length, JOINT, b16),
+            (length, MERGED, b16),
+            (2, 2 * rows, 2 * hidden_width, f32),
+            (length, hidden_width, b16),
+            (length, 2 * hidden_width, b16),
+            (length, JOINT, b16),
+        )
+        + table_buffers(length)
+        + attention_buffers(length)
+        + scatter_buffers(rows, width)
+        + vmem(
+            (2, length, depth, b16),
+            (depth, length, b16),
+            (2, depth, 2 * hidden_width, b16),
+        )
+        + sems(10)
+        + [pltpu.SemaphoreType.DMA((6, PLANE - 1))] * 2
+        + [pltpu.SemaphoreType.DMA((2, 2))] * 2
+        + sems(2, 2, PLANE, PLANE, 2, 2)
+        + sems(10, 7, 2, micro, micro, 2, *((10,) * 8)),
+        compiler_params=kernel_params(1),
+    )(own, gain_row, *tables, *weights)
+    return Layers(out[0], Saved(*out[1:13]), *out[13:])
+
+
+def run_gradients(layers, tables, merge_w, reduce_w):
+    saved = layers.saved
+    micro, rows, width = saved.inputs.shape
+    length = tables[0].shape[1]
+    hidden_width, depth = reduce_w.shape[0], merge_w.shape[0]
+    f32, b16 = jnp.float32, jnp.bfloat16
+    shape = jax.ShapeDtypeStruct
+    heads_term, merge_term = (depth, PLANE * JOINT), (depth, width)
+    expand_term, reduce_term = (depth, 2 * FF), (hidden_width, width)
+    terms = (heads_term,) * 2 + (merge_term,) * 2 + (expand_term,) + (reduce_term,) * 2
+    gain_width = -(-(2 * depth + 2 * HEAD_SIZE // PLANE) // 128) * 128
+
+    def flat(array):
+        return array.reshape(micro * length, -1)
+
+    return pl.pallas_call(
+        functools.partial(gradient_kernel, rows),
+        out_shape=(shape((rows, width), f32),)
+        + tuple(shape(term, b16) for term in terms)
+        + (shape((1, gain_width), f32),),
+        in_specs=vmem_specs(4) + any_specs(23),
+        out_specs=any_specs(8) + vmem_specs(1),
+        scratch_shapes=weight_buffers(width, hidden_width)
+        + vmem(
+            (rows, width, b16),
+            (rows, width, b16),
+            (rows, width, f32),
+            (length, width, b16),
+            (length, width, b16),
+            (length, JOINT, f32),
+            (length, JOINT, b16),
+            (length, MERGED, b16),
+            (2, 2 * rows, 2 * hidden_width, f32),
+            (length, JOINT, b16),
+        )
+        + table_buffers(length)
+        + attention_buffers(length)
+        + scatter_buffers(rows, width)
+        + vmem(
+            (2, micro * length, depth, b16),
+            (depth, micro * length, b16),
+            (length, width, b16),
+            (2 * length, 2 * hidden_width, b16),
+            (length, JOINT, b16),
+            (2, width, f32),
+            (2, HEAD_SIZE, f32),
+            (PLANE, 1, gain_width, f32),
+            (PLANE, 1, gain_width, f32),
+            (1, gain_width, f32),
+            (1, gain_width, f32),
+        )
+        + sems(18)
+        + [pltpu.SemaphoreType.DMA((2, 2))]
+        + sems(2, 11, *((10,) * 8))
+        + [pltpu.SemaphoreType.DMA((6, PLANE - 1))] * 2
+        + sems(10, 10),
+        compiler_params=kernel_params(2),
+    )(
+        layers.gains,
+        layers.head_gain,
+        layers.gain_terms,
+        layers.head_terms,
+        *tables,
+        layers.heads_w,
+        merge_w,
+        layers.expand_w,
+        reduce_w,
+        layers.handed,
+        saved.inputs,
+        saved.projected,
+        saved.heads,
+        saved.middle,
+        saved.joined,
+        flat(saved.hidden),
+        saved.upstream,
+        saved.normal_b,
+        layers.other_normal,
+        flat(saved.mixed),
+        saved.grad_middle,
+        flat(saved.normal_a),
+        saved.grad_projected,
+        layers.own_first,
+        layers.other_first,
+    )
+
+
+def position_tables(lengths, length):
+    document_index, positions = places(lengths, length)
+    half_width = HEAD_SIZE // 2
+    frequency = jnp.exp(
+        jnp.arange(half_width, dtype=jnp.float32) * (-2.0 * math.log(ROPE_BASE) / HEAD_SIZE)
+    )
+    angles = positions.astype(jnp.float32)[:, None] * frequency[None, :]
+    cosine, sine = jnp.cos(angles), jnp.sin(angles)
+    first_key = jnp.arange(length, dtype=jnp.int32) - positions
+    return (
+        jnp.concatenate([cosine, cosine], axis=-1),
+        jnp.concatenate([-sine, sine], axis=-1),
+        first_key[:, None],
+    )
+
+
+def tensor_parallel_body(
+    section_inputs,
+    doc_lengths,
+    mixer_gain,
+    heads_weight,
+    merge_weight,
+    head_gain,
+    feed_gain,
+    expand_weight,
+    reduce_weight,
+):
+    shards = lax.axis_size("fsdp")
+    own = section_inputs[0, :, 0]
+    micro, rows, width = own.shape
+    length = rows * shards
+    depth = heads_weight.shape[1]
+    hidden_width = reduce_weight.shape[1]
+    query_width = QUERY_HEADS * HEAD_SIZE
+
+    gain_row = jnp.concatenate([mixer_gain[0], feed_gain[0], head_gain[0]]).astype(jnp.float32)
+    gain_row = jnp.pad(gain_row, (0, -gain_row.shape[0] % 128))[None]
+    tables = [position_tables(doc_lengths[at, 0], length) for at in range(micro)]
+    cosine, sine, first_key = (jnp.stack(entry) for entry in zip(*tables))
+
+    table_rows = (cosine, sine, first_key)
+    layers = run_layers(
+        own,
+        gain_row,
+        table_rows,
+        (heads_weight[0], merge_weight[0], expand_weight[0], reduce_weight[0]),
+    )
+    last_rows, *terms, gain_sums = run_gradients(
+        layers, table_rows, merge_weight[0], reduce_weight[0]
+    )
+    grad_expand = terms.pop(4).astype(jnp.float32)[None]
+    grad_heads, grad_merge, grad_reduce = (
+        (terms[at].astype(jnp.float32) + terms[at + 1].astype(jnp.float32))[None]
+        for at in range(0, 6, 2)
+    )
+    head_count = head_gain.shape[1]
+    head = lax.axis_index("section") == 0
+    last_rows = jnp.where(head, last_rows, layers.rows[-1])
+    return (
+        jnp.concatenate([layers.rows[:-1], last_rows[None]])[None, :, None],
+        gain_sums[:, :depth],
+        grad_heads,
+        grad_merge,
+        gain_sums[:, 2 * depth : 2 * depth + head_count],
+        gain_sums[:, depth : 2 * depth],
+        grad_expand,
+        grad_reduce,
+    )
+
+
 def solution(mesh):
+    plane = mesh.shape["fsdp"] == PLANE
     return jax.shard_map(
-        body,
+        tensor_parallel_body if plane else body,
         mesh=mesh,
         in_specs=(
             P("section", None, "rep", "fsdp", None),

time: 2500 us -> 860 us (0.34)
  waiting for transfers between devices: 1430 us -> 0 us
  Pallas kernels: 0 us -> 822 us
  matrix products: 498 us -> 0 us
  local copies, waits for them, and re-layouts: 239 us -> 4.17 us
  other arithmetic: 224 us -> 27.6 us
  blocking collectives: 61.1 us -> 0 us
    pallas_call x0 -> x2, Pallas kernels: none -> 822 us  [the longest x1 605 us: run_layers(): pl.pallas_call(functools.partial(layers_kernel, rows), out_shape=(shape((...]
    all_gather x10 -> x0, waiting for transfers between devices: 516 us -> none  [the longest x1 229 us: body(): lax.all_gather(expand_weight, 'fsdp', axis=1, tiled=True)]
    dot_general x49 -> x0, matrix products: 498 us -> none  [the longest x12 190 us: times_transposed(): lax.dot_general(left_side, right_side, (((1,), (1,)), ((), ())), preferre...]
    reduce_scatter x6 -> x0, waiting for transfers between devices: 348 us -> none  [the longest x1 161 us: reduce_grads(): lax.psum_scatter(product_term(hidden, upstream_b).astype(jnp.bfloat16), '...]
    unnamed x25 -> x0, waiting for transfers between devices: 292 us -> none
    psum x1 -> x0, waiting for transfers between devices: 228 us -> none  [reduce_grads(): lax.psum(heads_gradient, 'rep').astype(jnp.float32)]
    select_n x51 -> x0, other arithmetic: 122 us -> none  [the longest x48 116 us: body(): jnp.where(is_live, buffer.at[micro_slot].set(current), buffer)]
    unnamed x484 -> x22, local copies, waits for them, and re-layouts: 105 us -> 1.31 us
  transfers between devices with their start and end apart: 25 -> 0, of which waited for: 21 -> 0; matrix products, arithmetic and copies ran while one was open for 18% -> 0% of each run, Pallas kernels for 0% -> 0%
where the time goes in v3:
time: 860 us; the launch traced here: 855 us
  Pallas kernels  822 us (96%)
  other arithmetic  27.6 us (3%)
    pallas_call x1, Pallas kernels, run_layers(): pl.pallas_call(functools.partial(layers_kernel, rows), out_shape=(shape((...  605 us
    pallas_call x1, Pallas kernels, run_gradients(): pl.pallas_call(functools.partial(gradient_kernel, rows), out_shape=(shape...  217 us

profile of v3, /device:TPU:0, one launch (start us, length us, event | category | flops | bytes accessed | tf_op | source)
XLA Modules:
  0.0 854.7 jit_solution(6138847724625931453)
XLA Ops:
  0.6 0.7 slice_bitcast_fusion.3
  1.3 0.2 reduce-window.16
  1.5 0.2 reduce-window.17
  1.7 0.1 select_reduce_fusion
  1.8 3.7 fusion.1
  5.5 0.2 maximum_bitcast_fusion.3
  5.7 0.2 maximum_bitcast_fusion.4
  5.9 1.0 pad_maximum_fusion.1.refs_3_.refs_5_
  7.0 0.2 maximum_bitcast_fusion.1
  7.2 0.2 maximum_bitcast_fusion.2
  7.4 1.0 pad_maximum_fusion.refs_2_.refs_4_
  8.4 0.0 copy-start.8
  8.4 0.0 copy-start.9
  8.4 0.0 copy-start.10
  8.4 0.2 copy.27
  8.7 0.1 subtract_subtract_fusion
  8.7 0.2 copy.26
  9.0 0.1 subtract_subtract_fusion.1
  9.0 1.0 pad_add_fusion.refs_4_.refs_6_
  10.1 0.0 copy-done.8
  10.1 0.0 copy-done.9
  10.1 0.0 copy-done.10
  10.1 0.6 reshape.139.refs_1_
  10.7 605.0 %shard_map.152 = (f32[2,128,2048]{2,1,0:T(8,128)}, bf16[2,128,2048]{2,1,0:T(8,128)(2,1)}, bf16[2,1024,2048]{2,1,0:T(8,128)(2,1)}, f32[2,1024,512]{2,1,0:T(8,128)...) custom-call(bf16[2,128,2048]{2,1,0:T(8,128)(2,1)} %bitcast.57, ...), custom_call_target="tpu_custom_call" | custom-call | tf_op jit(solution)/shard_map/pallas_call | solution.py:1995
  615.7 217.0 %shard_map.153 = (f32[128,2048]{1,0:T(8,128)}, bf16[256,4096]{1,0:T(8,128)(2,1)}, bf16[256,4096]{1,0:T(8,128)(2,1)}, bf16[256,2048]{1,0:T(8,128)(2,1)}, bf16[256...) custom-call(f32[2,2048]{1,0:T(2,128)} %get-tuple-element.41.refs_0_,, ...), custom_call_target="tpu_custom_call" | custom-call | tf_op jit(solution)/shard_map/pallas_call | solution.py:2065
  832.7 0.0 copy-start
  832.7 7.0 add_bitcast_fusion
  839.7 0.0 copy-done
  839.7 0.0 copy-start.5
  839.7 6.3 bitcast_convert_fusion
  846.0 0.0 copy-start.2
  846.0 0.0 copy-start.3
  846.0 0.0 copy-done.5
  846.0 0.0 copy-done.6
  846.0 1.7 add_bitcast_fusion.2
  847.7 0.5 copy-done.2
  848.1 0.8 copy-done.3
  849.0 0.0 copy-start.1
  849.0 2.7 add_bitcast_fusion.1
  851.7 0.0 copy-done.1
  851.7 0.0 copy-done.4
  851.7 0.1 fusion
  851.8 0.0 copy-start.7
  851.8 0.1 slice.23
  851.9 1.5 maximum_bitcast_fusion
  853.4 0.0 copy-done.7
  853.4 0.6 fusion.9
  854.0 0.5 slice.26
  (8 shorter events, 0.1 us)
Async XLA Ops:
  8.4 1.6 copy-start.8
  8.4 1.7 copy-start.9
  8.4 1.7 copy-start.10
  832.7 7.1 copy-start
  839.7 6.3 copy-start.5
  839.7 6.3 copy-start.6
  846.0 2.2 copy-start.2
  846.0 3.0 copy-start.3
  849.0 2.7 copy-start.1
  849.0 2.7 copy-start.4
  851.8 1.6 copy-start.7

commit v4 on v3

--- a/solution.py
+++ b/solution.py
@@ -695,6 +695,23 @@
             entry.wait_send()
 
 
+def turn_tile(tile, turned, first, last):
+    for at in range(last - first):
+        span = pl.ds(pl.multiple_of((first + at) * 256, 256), 256)
+        turned[:, span] = tile[span, :].T
+
+
+def product_and_turn(width, product, tile, turned):
+    step, quarter = width // 4, turned.shape[1] // 1024
+
+    @pl.loop(0, 4)
+    def _(chunk):
+        product(pl.ds(pl.multiple_of(chunk * step, 128), step))
+        for at in range(quarter):
+            span = pl.ds(pl.multiple_of((chunk * quarter + at) * 256, 256), 256)
+            turned[:, span] = tile[span, :].T
+
+
 def by_rows(count, body):
     @pl.loop(0, count // 16)
     def _(at):
@@ -750,7 +767,7 @@
     )
     full_a, full_b = buffers.full_a, buffers.full_b
     projected, heads, mixed = buffers.projected, buffers.heads, buffers.mixed
-    joined, hidden = buffers.joined, buffers.hidden
+    joined = buffers.joined
     chip_rows, width, hidden_width = 2 * rows, current.shape[1], wr.shape[0]
     save_sem = buffers.save_sem
     tables = [
@@ -846,11 +863,12 @@
         copy.wait()
     gather_b = Gather(place, full_b, *buffers.gather_b, rows)
     scatter_b = Scatter(place, *buffers.scatter, *buffers.scatter_b, rows)
-    joined_copies = {}
+    joined_copies, hidden_copies = {}, []
 
     def feed_block(rel):
         span = block_rows(place, rel, rows)
         stage = joined.at[rel % 2]
+        hidden = buffers.blocks.at[rel // 2, :, pl.ds(rel % 2 * hidden_width, hidden_width)]
         if rel == 0:
             hooks.feed()
         if rel >= 2:
@@ -864,22 +882,28 @@
             up = mm(full_b[span, :], we[:, later])
             stage[:, columns] = gate
             stage[:, later] = up
-            hidden[span, columns] = (gate * jax.nn.sigmoid(gate) * up).astype(jnp.bfloat16)
+            hidden[:, columns] = (gate * jax.nn.sigmoid(gate) * up).astype(jnp.bfloat16)
 
         copy = pltpu.make_async_copy(
             stage, refs.joined.at[slot, span], save_sem.at[8 + rel % 2]
         )
         copy.start()
         joined_copies[rel] = copy
-        scatter_b.put(rel, lambda columns: mm(hidden[span, :], wr[:, columns]), width)
+        copy = pltpu.make_async_copy(
+            hidden, refs.hidden.at[slot, span], buffers.hidden_sem.at[rel]
+        )
+        copy.start()
+        hidden_copies.append(copy)
+        scatter_b.put(rel, lambda columns: mm(hidden[...], wr[:, columns]), width)
         if rel in (1, 2):
             scatter_b.pair(rel - 1)
 
     gather_b.over_blocks(feed_block, lambda: scatter_b.pair(2))
-    later_saves = [save(6, full_b, refs.normal_b), save(7, hidden, refs.hidden)]
+    later_saves = [save(6, full_b, refs.normal_b)] + hidden_copies
     scatter_b.pair(3)
     scatter_b.relay()
     hooks.finish()
+    saves[5].wait()
 
     def finish(span, value):
         values = value + middle[span, :]
@@ -889,7 +913,7 @@
     scatter_b.total(finish)
     hooks.hand()
     gather_b.finish()
-    for copy in [saves[5]] + later_saves + [joined_copies[2], joined_copies[3]]:
+    for copy in later_saves + [joined_copies[2], joined_copies[3]]:
         copy.wait()
     hooks.after()
 
@@ -939,8 +963,29 @@
     scatter.total(feed_norm)
 
 
+def kept_probs(held, joined, at, block, chip_rows):
+    rows, seen = chip_rows // 2, (block + 1) * chip_rows
+    if at == 0:
+        first, columns = ((2, 2 * chip_rows), (2, 0), (0, 4 * chip_rows), (0, 0))[block]
+        return held.at[pl.ds(first, 2), pl.ds(0, rows), pl.ds(columns, seen)]
+    first, columns = ((1, 3 * chip_rows), (0, 4 * chip_rows), (1, 0), (0, 0))[block]
+    return joined.at[first, pl.ds(0, chip_rows), pl.ds(columns, seen)]
+
+
+def attention_probs(held, joined, heads, first_key, chip_rows):
+    for block in range(heads.shape[0] // chip_rows):
+        span = pl.ds(block * chip_rows, chip_rows)
+        seen = (block + 1) * chip_rows
+        keys = heads[:seen, 2 * HEAD_SIZE : 3 * HEAD_SIZE]
+        for at in range(2):
+            queries = heads[span, pl.ds(at * HEAD_SIZE, HEAD_SIZE)]
+            probs = probabilities(queries, keys, first_key[span, :], block * chip_rows)
+            kept = kept_probs(held, joined, at, block, chip_rows)
+            kept[...] = probs.reshape(kept.shape)
+
+
 def attention_back(
-    heads, grad_mixed, first_key, grad_queries, grad_keys, grad_values, chip_rows
+    held, joined, heads, grad_mixed, grad_queries, grad_keys, grad_values, chip_rows
 ):
     grad_keys[...] = jnp.zeros_like(grad_keys)
     grad_values[...] = jnp.zeros_like(grad_values)
@@ -953,7 +998,8 @@
             columns = pl.ds(at * HEAD_SIZE, HEAD_SIZE)
             queries = heads[span, columns]
             grad = grad_mixed[span, columns]
-            probs = probabilities(queries, keys, first_key[span, :], block * chip_rows)
+            probs = kept_probs(held, joined, at, block, chip_rows)[...]
+            probs = probs.reshape(chip_rows, seen)
             grad_probs = mm_t(grad, values)
             grad_scores = (
                 probs * (grad_probs - jnp.sum(probs * grad_probs, axis=-1, keepdims=True))
@@ -1055,8 +1101,11 @@
 
     gather = Gather(place, full_a, *buffers.gather_a, rows)
     scatter = Scatter(place, *buffers.scatter, *buffers.scatter_a, rows)
+    length = full_a.shape[0]
+
     def out_of(rel):
-        return grad_joined.at[block_rows(place, rel, rows)]
+        first = place.replica * length + place.chip_at(rel) * 2 * rows
+        return grad_joined.at[pl.ds(pl.multiple_of(first, 2 * rows), 2 * rows)]
 
     feed_back(
         place,
@@ -1068,7 +1117,7 @@
         joined,
         joined_load,
         out_of,
-        lambda rel, out: None,
+        hooks.done,
     )
     upstream_save = save(0, full_a, refs.upstream)
     scatter.relay()
@@ -1078,6 +1127,8 @@
     feed_input_back(place, rows, scatter, middle, gains_ref, out_gains, current, result, full_b)
     gather.finish()
     upstream_save.wait()
+    for rel in range(4):
+        hooks.settled(rel, out_of(rel))
     gather_b = Gather(place, full_b, *buffers.gather_b, rows)
     scatter_b = Scatter(place, *buffers.scatter, *buffers.scatter_b, rows)
     grad_mixed = buffers.mixed
@@ -1086,15 +1137,16 @@
         span = block_rows(place, rel, rows)
         grad_mixed[span, :] = mm_t(full_b[span, :], wm[...]).astype(jnp.bfloat16)
 
-    gather_b.over_blocks(mixed_block, early=hooks.early)
+    held, heads = buffers.scatter[0], buffers.heads
+
+    def early(at):
+        hooks.early(at)
+        if at == 0:
+            attention_probs(held, joined, heads, buffers.tables[2], 2 * rows)
+
+    gather_b.over_blocks(mixed_block, early=early)
     middle_save = save(1, full_b, refs.grad_middle)
-    attention_back(
-        buffers.heads,
-        grad_mixed,
-        buffers.tables[2],
-        *buffers.attention_grads,
-        2 * rows,
-    )
+    attention_back(held, joined, heads, grad_mixed, *buffers.attention_grads, 2 * rows)
     project_back(
         place, rows, scatter_b, buffers, refs.head_gain, refs.out_head_gain.at[slot], wh
     )
@@ -1102,6 +1154,7 @@
     hooks.early(5)
     scatter_b.relay()
     scatter_b.pair(0)
+    hooks.early(6)
     hooks.finish()
     input_back(scatter_b, inputs, gains_ref, out_gains, result, result_b)
     hooks.hand()
@@ -1129,8 +1182,9 @@
     rows: typing.Any
     saved: Saved
     handed: typing.Any
-    own_first: typing.Any
-    other_first: typing.Any
+    own_joined: typing.Any
+    other_joined: typing.Any
+    first_sum: typing.Any
     other_normal: typing.Any
     heads_w: typing.Any
     expand_w: typing.Any
@@ -1143,7 +1197,6 @@
 class LayerBuffers(typing.NamedTuple):
     current: typing.Any
     inputs: typing.Any
-    middle: typing.Any
     result: typing.Any
     result_b: typing.Any
     full_a: typing.Any
@@ -1152,7 +1205,6 @@
     heads: typing.Any
     mixed: typing.Any
     joined: typing.Any
-    hidden: typing.Any
     grad_joined: typing.Any
     grad_projected: typing.Any
 
@@ -1183,19 +1235,21 @@
     heads_w, merge_w, expand_w, reduce_w = some(4)
     (out_rows,) = some(1)
     saved = types.SimpleNamespace(**Saved(*some(12))._asdict())
-    out_handed, own_first, other_first, other_normal = some(4)
+    out_handed, own_joined, other_joined, first_sum, other_normal = some(5)
     out_heads_w, out_expand_w = some(2)
     gains_ref, head_gain_ref, out_gains, out_head_gain = some(4)
     all_gains, wh, wm, we, wr, arrived = some(6)
-    buffers = types.SimpleNamespace(**LayerBuffers(*some(14))._asdict())
+    buffers = types.SimpleNamespace(**LayerBuffers(*some(12))._asdict())
+    buffers.middle = buffers.result
     buffers.tables = some(3)
     buffers.attention_grads = some(3)
     buffers.scatter = some(7)
     first_tiles, first_turned, first_stage = some(3)
+    buffers.blocks = first_stage
     load_sem, spread_send, spread_recv = some(3)
     share_send, share_recv = some(2)
     tile_sem, first_sem, first_send, first_recv, normal_send, normal_recv = some(6)
-    buffers.save_sem, buffers.table_sem, buffers.joined_sem = some(3)
+    buffers.save_sem, buffers.table_sem, buffers.joined_sem, buffers.hidden_sem = some(4)
     hand_send, hand_recv, out_sem = some(3)
     buffers.gather_a, buffers.scatter_a = some(2), some(2)
     buffers.gather_b, buffers.scatter_b = some(2), some(2)
@@ -1330,71 +1384,126 @@
     current, result, result_b = buffers.current, buffers.result, buffers.result_b
     length = buffers.full_a.shape[0]
 
-    def tile_rows(at):
-        return pl.ds(at * depth, depth)
-
-    def first_tile(at):
+    def joined_save(rel, out):
         return pltpu.make_async_copy(
-            saved.normal_b.at[0, :, tile_rows(at)], first_tiles.at[at % 2], tile_sem.at[at % 2]
-        )
-
-    def first_save(at):
-        return pltpu.make_async_copy(
-            first_stage.at[at % 2], own_first.at[tile_rows(at)], first_sem.at[at % 2]
-        )
-
-    def first_copy(at):
-        block = tile_rows(at)
+            out, own_joined.at[block_rows(place, rel, rows)], first_sem.at[rel]
+        )
+
+    def joined_copy(rel, out):
         return remote(
-            own_first.at[block],
-            other_first.at[block],
-            first_send.at[at],
-            first_recv.at[at],
+            out,
+            other_joined.at[block_rows(place, rel, rows)],
+            first_send.at[rel],
+            first_recv.at[rel],
             place.rep_peer,
         )
 
-    def early_tile(at):
-        first_tile(at).wait()
-
-        @pl.loop(0, length // 256)
-        def _(chunk):
-            span = pl.ds(pl.multiple_of(chunk * 256, 256), 256)
-            first_turned[:, span] = first_tiles[at % 2, span, :].T
-
-        if at + 2 < PLANE:
-            first_tile(at + 2).start()
-
-        @pl.loop(0, 2 * hidden_width // 512)
-        def _(chunk):
-            columns = pl.ds(pl.multiple_of(chunk * 512, 512), 512)
-            first_stage[at % 2, :, columns] = mm(
-                first_turned[...], buffers.grad_joined[:, columns]
-            ).astype(jnp.bfloat16)
-
-        first_save(at).start()
-        if at:
-            first_save(at - 1).wait()
-            pl.when(head)(first_copy(at - 1).start)
-        if at == PLANE - 1:
-            first_save(at).wait()
-            pl.when(head)(first_copy(at).start)
+    def saved_block(rel):
+        return own_joined.at[block_rows(place, rel, rows)]
 
     half = length // 2
     half_rows = pl.ds(pl.multiple_of(place.core * half, half), half)
-    normal_copy = remote(
-        saved.normal_b.at[1, half_rows],
-        other_normal.at[half_rows],
-        normal_send.at[0],
-        normal_recv.at[0],
-        place.rep_peer,
-    )
-    normal_pass = remote(
-        other_normal.at[half_rows],
-        other_normal.at[half_rows],
-        normal_send.at[1],
-        normal_recv.at[1],
-        place.core_peer,
-    )
+
+    def normal_copy(slot):
+        return remote(
+            saved.normal_b.at[slot, half_rows],
+            other_normal.at[slot, half_rows],
+            normal_send.at[slot],
+            normal_recv.at[slot],
+            place.rep_peer,
+        )
+
+    def normal_pass(slot):
+        block = other_normal.at[slot, half_rows]
+        return remote(
+            block, block, normal_send.at[2 + slot], normal_recv.at[2 + slot], place.core_peer
+        )
+
+    def token_rows(replica):
+        return pl.ds(pl.multiple_of(replica * length, length), length)
+
+    def first_loads(at):
+        columns = pl.ds(pl.multiple_of(at * depth, depth), depth)
+        parts = (
+            (saved.normal_b.at[0, :, columns], place.replica),
+            (other_normal.at[0, :, columns], 1 - place.replica),
+        )
+        into = lax.rem(at, 2)
+        return [
+            pltpu.make_async_copy(
+                src, first_tiles.at[into, token_rows(replica)], tile_sem.at[into, part]
+            )
+            for part, (src, replica) in enumerate(parts)
+        ]
+
+    def first_save(at):
+        rows_at = pl.ds(pl.multiple_of(at * depth, depth), depth)
+        return pltpu.make_async_copy(
+            first_stage.at[lax.rem(at, 2)], first_sum.at[rows_at], first_sem.at[lax.rem(at, 2)]
+        )
+
+    def whole_load(part):
+        src, replica = ((own_joined, place.replica), (other_joined, 1 - place.replica))[part]
+        return pltpu.make_async_copy(
+            src, buffers.grad_joined.at[token_rows(replica)], first_sem.at[2 + part]
+        )
+
+    def first_begin():
+        normal_copy(0).wait_recv()
+        normal_pass(0).start()
+        for rel in range(4):
+            joined_copy(rel, saved_block(rel)).wait()
+        for part in range(2):
+            whole_load(part).start()
+        normal_pass(0).wait_recv()
+        for at in range(2):
+            for copy in first_loads(jnp.int32(at)):
+                copy.start()
+
+    def first_turn():
+        for part in range(2):
+            whole_load(part).wait()
+        for copy in first_loads(jnp.int32(0)):
+            copy.wait()
+        turn_tile(first_tiles.at[0], first_turned.at[0], 0, 2 * length // 256)
+        for copy in first_loads(jnp.int32(2)):
+            copy.start()
+
+    def first_job(at):
+        into, later = lax.rem(at, 2), lax.rem(at + 1, 2)
+
+        @pl.when(at + 1 < PLANE)
+        def _():
+            for copy in first_loads(at + 1):
+                copy.wait()
+
+        @pl.when(at >= 2)
+        def _():
+            first_save(at - 2).wait()
+
+        def product(columns):
+            first_stage[into, :, columns] = mm(
+                first_turned[into], buffers.grad_joined[:, columns]
+            ).astype(jnp.bfloat16)
+
+        product_and_turn(
+            2 * hidden_width, product, first_tiles.at[later], first_turned.at[later]
+        )
+        first_save(at).start()
+
+        @pl.when(at + 3 < PLANE)
+        def _():
+            for copy in first_loads(at + 3):
+                copy.start()
+
+    def first_jobs(first, last):
+        @pl.loop(first, last)
+        def _(at):
+            first_job(at)
+
+    def first_end():
+        for at in (PLANE - 2, PLANE - 1):
+            first_save(jnp.int32(at)).wait()
 
     def hand(slot):
         return remote(
@@ -1471,7 +1580,7 @@
                     save_rows(slot)
 
             def after():
-                pl.when(slot == 1)(normal_copy.start)
+                normal_copy(slot).start()
 
             layer_forward_step(
                 place,
@@ -1515,26 +1624,53 @@
 
                 @pl.when(rest & (slot == 0))
                 def _():
-                    for at in range(PLANE):
-                        first_copy(at).start()
+                    for rel in range(4):
+                        joined_copy(rel, saved_block(rel)).start()
 
                 @pl.when(head)
                 def _():
                     rows_copy(slot).start()
 
-            def early(at):
-                groups = ((), (0, 1, 2), (3,), (4,), (5, 6), (7,))
-
+            def done(rel, out):
                 @pl.when(slot == 0)
                 def _():
+                    joined_save(rel, out).start()
+
+                @pl.when(head)
+                def _():
+                    joined_copy(rel, out).start()
+
+            def settled(rel, out):
+                pl.when(slot == 0)(lambda: joined_save(rel, out).wait())
+
+            def early(at):
+                @pl.when(rest & (slot == 1))
+                def _():
                     if at == 0:
-                        first_tile(0).start()
-                        first_tile(1).start()
-                    for tile in groups[at]:
-                        early_tile(tile)
-
-            hooks = types.SimpleNamespace(finish=finish, hand=handing, early=early)
+                        first_begin()
+                    elif at == 2:
+                        first_turn()
+                    elif at == 3:
+                        first_jobs(0, 2)
+                    elif at == 6:
+                        first_jobs(2, 5)
+
+            hooks = types.SimpleNamespace(
+                finish=finish, hand=handing, done=done, settled=settled, early=early
+            )
             layer_backward_step(place, rows, saved, buffers, slot, hooks)
+
+    @pl.when(head)
+    def _():
+        first_begin()
+        first_turn()
+        first_jobs(0, 5)
+
+    first_jobs(5, PLANE)
+
+    first_end()
+    normal_copy(1).wait_recv()
+    normal_pass(1).start()
 
     @pl.when(head)
     def _():
@@ -1548,18 +1684,16 @@
 
     handed = pltpu.make_async_copy(current, out_handed, out_sem.at[1])
     handed.start()
-    normal_copy.wait_recv()
-    normal_pass.start()
+    normal_pass(1).wait_recv()
     heads_out.wait()
     expand_out.wait()
     for copy in gain_copies[:7]:
         copy.wait_send()
     sent(heads_copies, 3, 0, wh, 2)
     sent(expand_copies, 2, 1, we, 2)
-    for at in range(PLANE):
-        first_copy(at).wait()
-    normal_copy.wait_send()
-    normal_pass.wait()
+    for slot in range(2):
+        normal_copy(slot).wait_send()
+        normal_pass(slot).wait_send()
     handed.wait()
     pl.when(head)(lambda: rows_copy(0).wait())
 
@@ -1578,8 +1712,7 @@
     in_handed, in_inputs, in_projected, in_heads, in_middle, in_joined = some(6)
     hidden_all, upstream_all, normal_b_all, other_normal = some(4)
     mixed_all, grad_middle_all, normal_a_all, grad_projected_all = some(4)
-    own_first, other_first = some(2)
-    (out_result,) = some(1)
+    first_sum, out_result = some(2)
     own_heads, other_heads, own_merge, other_merge = some(4)
     own_expand, own_reduce, other_reduce = some(3)
     (out_gain,) = some(1)
@@ -1645,7 +1778,7 @@
             ]
         parts = (
             (normal_b_all.at[last, :, columns], place.replica),
-            (other_normal.at[:, columns], 1 - place.replica),
+            (other_normal.at[last, :, columns], 1 - place.replica),
         )
         return [
             pltpu.make_async_copy(
@@ -1658,17 +1791,16 @@
         for copy in tile_loads(job):
             copy.start()
 
-    def take(job):
-        for copy in tile_loads(job):
-            copy.wait()
-
-        @pl.loop(0, tokens // 256)
-        def _(at):
-            span = pl.ds(pl.multiple_of(at * 256, 256), 256)
-            turned[:, span] = tiles[job % 2, span, :].T
-
-        if job + 2 < job_count:
-            tile_start(job + 2)
+    def run_job(job, width, product):
+        now, later = turned.at[job % 2], (job + 1) % 2
+        if job + 1 < job_count:
+            for copy in tile_loads(job + 1):
+                copy.wait()
+        product_and_turn(
+            width, lambda columns: product(now, columns), tiles.at[later], turned.at[later]
+        )
+        if job + 3 < job_count:
+            tile_start(job + 3)
 
     tile_start(0)
     tile_start(1)
@@ -1700,14 +1832,15 @@
     upstream_load.wait()
     own_rows = pl.ds(pl.multiple_of(place.index * rows, rows), rows)
     full_a[own_rows, :] = current[...]
-    reduce_load.wait()
-    expand_load.wait()
     gather = Gather(place, full_a, *buffers.gather_a, rows)
     scatter = Scatter(place, *buffers.scatter, *buffers.scatter_a, rows)
 
     joined_reps = []
 
     def out_of(rel):
+        if rel == 0:
+            reduce_load.wait()
+            expand_load.wait()
         first = place.replica * length + place.chip_at(rel) * 2 * rows
         return narrow.at[pl.ds(pl.multiple_of(first, 2 * rows), 2 * rows)]
 
@@ -1729,18 +1862,20 @@
         done,
     )
     wide_load.wait()
+    for copy in tile_loads(0):
+        copy.wait()
+    turn_tile(tiles.at[0], turned.at[0], 0, tokens // 256)
+    tile_start(2)
     own_saves, rep_copies = [], []
     for at in range(hidden_width // depth):
-        take(at)
         span = pl.ds(at * depth, depth)
 
-        @pl.loop(0, width // 512)
-        def _(chunk):
-            columns = pl.ds(pl.multiple_of(chunk * 512, 512), 512)
-            value = mm(turned[:, :length], wide[:, columns])
-            value += mm(turned[:, length:], full_a[:, columns])
+        def product(tile, columns):
+            value = mm(tile[:, :length], wide[:, columns])
+            value += mm(tile[:, length:], full_a[:, columns])
             wr[span, columns] = value.astype(jnp.bfloat16)
 
+        run_job(at, width, product)
         copy = rep_copy(at, wr.at[span], other_reduce.at[span])
         copy.start()
         rep_copies.append(copy)
@@ -1758,6 +1893,8 @@
     gather_b.start()
     for copy in loads:
         copy.wait()
+    held = buffers.scatter[0]
+    attention_probs(held, joined, buffers.heads, buffers.tables[2], 2 * rows)
     gather_b.relay()
     gather_b.near()
     gather_b.far()
@@ -1766,29 +1903,49 @@
         span = block_rows(place, rel, rows)
         grad_mixed[span, :] = mm_t(full_b[span, :], wm[...]).astype(jnp.bfloat16)
     attention_back(
-        buffers.heads,
-        grad_mixed,
-        buffers.tables[2],
-        *buffers.attention_grads,
-        2 * rows,
+        held, joined, buffers.heads, grad_mixed, *buffers.attention_grads, 2 * rows
     )
     project_back(place, rows, scatter_b, buffers, head_gain_ref, head_gain, wh)
     job = hidden_width // depth
     grad_middle_load.wait()
-    take(job)
+
+    def merge_product(tile, columns):
+        value = mm(tile[:, :length], wide[:, columns])
+        value += mm(tile[:, length:], full_b[:, columns])
+        wm[:, columns] = value.astype(jnp.bfloat16)
+
+    run_job(job, width, merge_product)
     job += 1
-
-    @pl.loop(0, width // 512)
-    def _(chunk):
-        columns = pl.ds(pl.multiple_of(chunk * 512, 512), 512)
-        value = mm(turned[:, :length], wide[:, columns])
-        value += mm(turned[:, length:], full_b[:, columns])
-        wm[:, columns] = value.astype(jnp.bfloat16)
-
     merge_rep = rep_copy(3, wm, other_merge)
     merge_rep.start()
     merge_save = pltpu.make_async_copy(wm, own_merge, save_sem.at[3])
     merge_save.start()
+    projected_load.wait()
+    heads_copies = []
+    for at, device in others:
+        block = pl.ds(at * depth, depth)
+
+        def product(tile, columns):
+            value = mm(tile[:, :length], first_projected[:, columns])
+            value += mm(tile[:, length:], grad_projected[:, columns])
+            wh[block, columns] = value.astype(jnp.bfloat16)
+
+        run_job(job, JOINT, product)
+        job += 1
+        for piece, first, count, start in (
+            (2, 0, MERGED, 0),
+            (3, query_width, HEAD_SIZE, MERGED),
+            (4, query_width + key_width, HEAD_SIZE, MERGED + HEAD_SIZE),
+        ):
+            copy = spread(
+                at,
+                device,
+                piece,
+                wh.at[block, pl.ds(start, count)],
+                own_heads.at[:, shard_columns(first, place.index, count)],
+            )
+            copy.start()
+            heads_copies.append(copy)
     scatter_b.relay()
     scatter_b.pair(0)
     input_back(scatter_b, inputs, gains_ref, gains, result, None)
@@ -1813,68 +1970,30 @@
         copy.start()
         gain_copies.append(copy)
 
-    projected_load.wait()
-    heads_copies = []
-    for at, device in others:
-        take(job)
-        job += 1
-        value = mm(turned[:, :length], first_projected[...])
-        value += mm(turned[:, length:], grad_projected[...])
-        block = pl.ds(at * depth, depth)
-        wh[block, :] = value.astype(jnp.bfloat16)
-        for piece, first, count, start in (
-            (2, 0, MERGED, 0),
-            (3, query_width, HEAD_SIZE, MERGED),
-            (4, query_width + key_width, HEAD_SIZE, MERGED + HEAD_SIZE),
-        ):
-            copy = spread(
-                at,
-                device,
-                piece,
-                wh.at[block, pl.ds(start, count)],
-                own_heads.at[:, shard_columns(first, place.index, count)],
-            )
-            copy.start()
-            heads_copies.append(copy)
-    def first_loads(at, device):
+    def first_load(at, device):
         block = pl.ds(pl.multiple_of(device * depth, depth), depth)
-        return [
-            pltpu.make_async_copy(
-                src.at[block],
-                wide.at[
-                    pl.ds((2 * (at % 2) + part) * depth, depth), pl.ds(0, 2 * hidden_width)
-                ],
-                load_sem.at[14 + 2 * (at % 2) + part],
-            )
-            for part, src in enumerate((own_first, other_first))
-        ]
+        into = wide.at[pl.ds(at % 2 * depth, depth), pl.ds(0, 2 * hidden_width)]
+        return pltpu.make_async_copy(first_sum.at[block], into, load_sem.at[14 + at % 2])
 
     for at, device in others[:2]:
-        for copy in first_loads(at, device):
-            copy.start()
+        first_load(at, device).start()
     for copy in joined_reps:
         copy.wait_recv()
     expand_copies = []
     for at, device in others:
-        take(job)
+        block = pl.ds(at * depth, depth)
+        first_load(at, device).wait()
+        before = pl.ds(at % 2 * depth, depth)
+
+        def product(tile, columns):
+            value = wide[before, columns].astype(jnp.float32)
+            value += mm(tile[...], narrow[:, columns])
+            we[block, columns] = value.astype(jnp.bfloat16)
+
+        run_job(job, narrow.shape[1], product)
         job += 1
-        block = pl.ds(at * depth, depth)
-        for copy in first_loads(at, device):
-            copy.wait()
-        mine = pl.ds(2 * (at % 2) * depth, depth)
-        theirs = pl.ds((2 * (at % 2) + 1) * depth, depth)
-
-        @pl.loop(0, narrow.shape[1] // 512)
-        def _(chunk):
-            columns = pl.ds(pl.multiple_of(chunk * 512, 512), 512)
-            value = wide[mine, columns].astype(jnp.float32)
-            value += wide[theirs, columns].astype(jnp.float32)
-            value += mm(turned[...], narrow[:, columns])
-            we[block, columns] = value.astype(jnp.bfloat16)
-
         if at + 2 < PLANE:
-            for copy in first_loads(*others[at + 2]):
-                copy.start()
+            first_load(*others[at + 2]).start()
         for piece in range(2):
             copy = spread(
                 at,
@@ -1998,9 +2117,10 @@
             shape((micro, rows, width), f32),
             *(shape((micro, *size), dtype) for *size, dtype in stashes),
             shape((rows, width), b16),
+            shape((length, 2 * hidden_width), b16),
+            shape((length, 2 * hidden_width), b16),
             shape((width, 2 * hidden_width), b16),
-            shape((width, 2 * hidden_width), b16),
-            shape((length, width), b16),
+            shape((micro, length, width), b16),
             shape((width, JOINT), b16),
             shape((width, 2 * hidden_width), b16),
             shape((2, width), f32),
@@ -2009,14 +2129,13 @@
             shape((micro, 2, HEAD_SIZE), f32),
         ),
         in_specs=vmem_specs(2) + any_specs(7),
-        out_specs=any_specs(19) + vmem_specs(4),
+        out_specs=any_specs(20) + vmem_specs(4),
         scratch_shapes=vmem((PLANE, *gain_row.shape, f32))
         + weight_buffers(width, hidden_width)
         + vmem(
             (micro, rows, width, b16),
             (rows, width, b16),
             (rows, width, b16),
-            (rows, width, f32),
             (rows, width, f32),
             (rows, width, b16),
             (length, width, b16),
@@ -2025,23 +2144,23 @@
             (length, JOINT, b16),
             (length, MERGED, b16),
             (2, 2 * rows, 2 * hidden_width, f32),
-            (length, hidden_width, b16),
-            (length, 2 * hidden_width, b16),
+            (2 * length, 2 * hidden_width, b16),
             (length, JOINT, b16),
         )
         + table_buffers(length)
         + attention_buffers(length)
         + scatter_buffers(rows, width)
         + vmem(
-            (2, length, depth, b16),
-            (depth, length, b16),
+            (2, 2 * length, depth, b16),
+            (2, depth, 2 * length, b16),
             (2, depth, 2 * hidden_width, b16),
         )
         + sems(10)
         + [pltpu.SemaphoreType.DMA((6, PLANE - 1))] * 2
         + [pltpu.SemaphoreType.DMA((2, 2))] * 2
-        + sems(2, 2, PLANE, PLANE, 2, 2)
-        + sems(10, 7, 2, micro, micro, 2, *((10,) * 8)),
+        + [pltpu.SemaphoreType.DMA((2, 2))]
+        + sems(4, 4, 4, 4, 4)
+        + sems(10, 7, 2, 4, micro, micro, 2, *((10,) * 8)),
         compiler_params=kernel_params(1),
     )(own, gain_row, *tables, *weights)
     return Layers(out[0], Saved(*out[1:13]), *out[13:])
@@ -2067,7 +2186,7 @@
         out_shape=(shape((rows, width), f32),)
         + tuple(shape(term, b16) for term in terms)
         + (shape((1, gain_width), f32),),
-        in_specs=vmem_specs(4) + any_specs(23),
+        in_specs=vmem_specs(4) + any_specs(22),
         out_specs=any_specs(8) + vmem_specs(1),
         scratch_shapes=weight_buffers(width, hidden_width)
         + vmem(
@@ -2087,7 +2206,7 @@
         + scatter_buffers(rows, width)
         + vmem(
             (2, micro * length, depth, b16),
-            (depth, micro * length, b16),
+            (2, depth, micro * length, b16),
             (length, width, b16),
             (2 * length, 2 * hidden_width, b16),
             (length, JOINT, b16),
@@ -2128,8 +2247,7 @@
         saved.grad_middle,
         flat(saved.normal_a),
         saved.grad_projected,
-        layers.own_first,
-        layers.other_first,
+        layers.first_sum,
     )
 
 
@@ -2183,10 +2301,15 @@
     last_rows, *terms, gain_sums = run_gradients(
         layers, table_rows, merge_weight[0], reduce_weight[0]
     )
-    grad_expand = terms.pop(4).astype(jnp.float32)[None]
+    own_heads, other_heads, own_merge, other_merge, own_expand, own_reduce, other_reduce = terms
+    grad_expand = own_expand.astype(jnp.float32)[None]
     grad_heads, grad_merge, grad_reduce = (
-        (terms[at].astype(jnp.float32) + terms[at + 1].astype(jnp.float32))[None]
-        for at in range(0, 6, 2)
+        (mine.astype(jnp.float32) + theirs.astype(jnp.float32))[None]
+        for mine, theirs in (
+            (own_heads, other_heads),
+            (own_merge, other_merge),
+            (own_reduce, other_reduce),
+        )
     )
     head_count = head_gain.shape[1]
     head = lax.axis_index("section") == 0

time: 860 us -> 847 us (0.985)
  Pallas kernels: 822 us -> 804 us
    pallas_call x1, Pallas kernels: 605 us -> 574 us  [run_layers(): pl.pallas_call(functools.partial(layers_kernel, rows), out_shape=(shape((...]
    pallas_call x1, Pallas kernels: 217 us -> 230 us  [run_gradients(): pl.pallas_call(functools.partial(gradient_kernel, rows), out_shape=(shape...]
where the time goes in v4:
time: 847 us; the launch traced here: 837 us
  Pallas kernels  804 us (95%)
  other arithmetic  27.6 us (3%)
    pallas_call x1, Pallas kernels, run_layers(): pl.pallas_call(functools.partial(layers_kernel, rows), out_shape=(shape((...  574 us
    pallas_call x1, Pallas kernels, run_gradients(): pl.pallas_call(functools.partial(gradient_kernel, rows), out_shape=(shape...  230 us

profile of v4, /device:TPU:0, one launch (start us, length us, event | category | flops | bytes accessed | tf_op | source)
XLA Modules:
  0.0 837.3 jit_solution(14204169010900676013)
XLA Ops:
  0.6 0.7 slice_bitcast_fusion.3
  1.3 0.2 reduce-window.16
  1.5 0.2 reduce-window.17
  1.7 0.1 select_reduce_fusion
  1.8 3.7 fusion.1
  5.5 0.2 maximum_bitcast_fusion.3
  5.7 0.2 maximum_bitcast_fusion.4
  5.9 1.0 pad_maximum_fusion.1.refs_3_.refs_5_
  7.0 0.2 maximum_bitcast_fusion.1
  7.2 0.2 maximum_bitcast_fusion.2
  7.4 1.0 pad_maximum_fusion.refs_2_.refs_4_
  8.4 0.0 copy-start.9
  8.4 0.0 copy-start.10
  8.4 0.2 copy.27
  8.7 0.1 subtract_subtract_fusion
  8.7 0.2 copy.26
  9.0 0.1 subtract_subtract_fusion.1
  9.0 1.0 pad_add_fusion.refs_4_.refs_6_
  10.1 0.0 copy-done.8
  10.1 0.0 copy-done.9
  10.1 0.0 copy-done.10
  10.1 0.6 reshape.139.refs_1_
  10.7 574.1 %shard_map.152 = (f32[2,128,2048]{2,1,0:T(8,128)}, bf16[2,128,2048]{2,1,0:T(8,128)(2,1)}, bf16[2,1024,2048]{2,1,0:T(8,128)(2,1)}, f32[2,1024,512]{2,1,0:T(8,128)...) custom-call(bf16[2,128,2048]{2,1,0:T(8,128)(2,1)} %bitcast.57, ...), custom_call_target="tpu_custom_call" | custom-call | tf_op jit(solution)/shard_map/pallas_call | solution.py:2114
  584.9 230.1 %shard_map.153 = (f32[128,2048]{1,0:T(8,128)}, bf16[256,4096]{1,0:T(8,128)(2,1)}, bf16[256,4096]{1,0:T(8,128)(2,1)}, bf16[256,2048]{1,0:T(8,128)(2,1)}, bf16[256...) custom-call(f32[2,2048]{1,0:T(2,128)} %get-tuple-element.40.refs_0_,, ...), custom_call_target="tpu_custom_call" | custom-call | tf_op jit(solution)/shard_map/pallas_call | solution.py:2184
  815.0 0.0 copy-start
  815.0 7.0 add_bitcast_fusion
  822.1 0.0 copy-done
  822.1 0.0 copy-start.5
  822.1 0.0 copy-start.6
  822.1 6.3 bitcast_convert_fusion
  828.3 0.0 copy-start.3
  828.3 0.0 copy-done.5
  828.3 0.0 copy-done.6
  828.3 1.7 add_bitcast_fusion.2
  830.0 0.5 copy-done.2
  830.5 0.8 copy-done.3
  831.3 0.0 copy-start.1
  831.3 0.0 copy-start.4
  831.3 2.7 add_bitcast_fusion.1
  834.0 0.0 copy-done.1
  834.1 0.0 copy-done.4
  834.1 0.1 fusion
  834.2 0.0 copy-start.7
  834.2 0.1 slice.23
  834.3 1.5 maximum_bitcast_fusion
  835.7 0.0 copy-done.7
  835.7 0.6 fusion.9
  836.3 0.5 slice.26
  (8 shorter events, 0.1 us)
Async XLA Ops:
  8.4 1.6 copy-start.8
  8.4 1.7 copy-start.9
  8.4 1.7 copy-start.10
  815.0 7.1 copy-start
  822.1 6.3 copy-start.5
  822.1 6.3 copy-start.6
  828.3 2.2 copy-start.2
  828.3 3.0 copy-start.3
  831.3 2.7 copy-start.1
  831.3 2.7 copy-start.4
  834.2 1.6 copy-start.7

commit v5 on v4

--- a/solution.py
+++ b/solution.py
@@ -702,13 +702,14 @@
 
 
 def product_and_turn(width, product, tile, turned):
-    step, quarter = width // 4, turned.shape[1] // 1024
-
-    @pl.loop(0, 4)
+    parts = 4 if width >= 1024 else 2
+    step, share = width // parts, turned.shape[1] // (256 * parts)
+
+    @pl.loop(0, parts)
     def _(chunk):
         product(pl.ds(pl.multiple_of(chunk * step, 128), step))
-        for at in range(quarter):
-            span = pl.ds(pl.multiple_of((chunk * quarter + at) * 256, 256), 256)
+        for at in range(share):
+            span = pl.ds(pl.multiple_of((chunk * share + at) * 256, 256), 256)
             turned[:, span] = tile[span, :].T
 
 
@@ -1161,6 +1162,7 @@
     gather_b.finish()
     for copy in (middle_save, projected_save):
         copy.wait()
+    hooks.after()
 
 
 class Saved(typing.NamedTuple):
@@ -1186,6 +1188,8 @@
     other_joined: typing.Any
     first_sum: typing.Any
     other_normal: typing.Any
+    other_normal_a: typing.Any
+    other_projected: typing.Any
     heads_w: typing.Any
     expand_w: typing.Any
     gains: typing.Any
@@ -1211,7 +1215,6 @@
 
 class GradientBuffers(typing.NamedTuple):
     current: typing.Any
-    inputs: typing.Any
     result: typing.Any
     full_a: typing.Any
     full_b: typing.Any
@@ -1219,7 +1222,6 @@
     heads: typing.Any
     mixed: typing.Any
     joined: typing.Any
-    grad_projected: typing.Any
 
 
 def layers_kernel(rows, *refs):
@@ -1236,6 +1238,7 @@
     (out_rows,) = some(1)
     saved = types.SimpleNamespace(**Saved(*some(12))._asdict())
     out_handed, own_joined, other_joined, first_sum, other_normal = some(5)
+    other_normal_a, other_projected = some(2)
     out_heads_w, out_expand_w = some(2)
     gains_ref, head_gain_ref, out_gains, out_head_gain = some(4)
     all_gains, wh, wm, we, wr, arrived = some(6)
@@ -1249,6 +1252,7 @@
     load_sem, spread_send, spread_recv = some(3)
     share_send, share_recv = some(2)
     tile_sem, first_sem, first_send, first_recv, normal_send, normal_recv = some(6)
+    projected_send, projected_recv = some(2)
     buffers.save_sem, buffers.table_sem, buffers.joined_sem, buffers.hidden_sem = some(4)
     hand_send, hand_recv, out_sem = some(3)
     buffers.gather_a, buffers.scatter_a = some(2), some(2)
@@ -1404,20 +1408,33 @@
     half = length // 2
     half_rows = pl.ds(pl.multiple_of(place.core * half, half), half)
 
-    def normal_copy(slot):
+    def normal_copy(slot, kind=0):
+        src, dst = ((saved.normal_b, other_normal), (saved.normal_a, other_normal_a))[kind]
         return remote(
-            saved.normal_b.at[slot, half_rows],
-            other_normal.at[slot, half_rows],
-            normal_send.at[slot],
-            normal_recv.at[slot],
+            src.at[slot, half_rows],
+            dst.at[slot, half_rows],
+            normal_send.at[kind, slot],
+            normal_recv.at[kind, slot],
             place.rep_peer,
         )
 
-    def normal_pass(slot):
-        block = other_normal.at[slot, half_rows]
+    def normal_pass(slot, kind=0):
+        block = (other_normal, other_normal_a)[kind].at[slot, half_rows]
         return remote(
-            block, block, normal_send.at[2 + slot], normal_recv.at[2 + slot], place.core_peer
-        )
+            block,
+            block,
+            normal_send.at[kind, 2 + slot],
+            normal_recv.at[kind, 2 + slot],
+            place.core_peer,
+        )
+
+    projected_copy = remote(
+        saved.grad_projected.at[0],
+        other_projected,
+        projected_send.at[0],
+        projected_recv.at[0],
+        place.rep_peer,
+    )
 
     def token_rows(replica):
         return pl.ds(pl.multiple_of(replica * length, length), length)
@@ -1581,6 +1598,7 @@
 
             def after():
                 normal_copy(slot).start()
+                normal_copy(slot, 1).start()
 
             layer_forward_step(
                 place,
@@ -1655,8 +1673,16 @@
                     elif at == 6:
                         first_jobs(2, 5)
 
+            def after():
+                pl.when(slot == 0)(projected_copy.start)
+
             hooks = types.SimpleNamespace(
-                finish=finish, hand=handing, done=done, settled=settled, early=early
+                finish=finish,
+                hand=handing,
+                done=done,
+                settled=settled,
+                early=early,
+                after=after,
             )
             layer_backward_step(place, rows, saved, buffers, slot, hooks)
 
@@ -1671,6 +1697,9 @@
     first_end()
     normal_copy(1).wait_recv()
     normal_pass(1).start()
+    for slot in range(2):
+        normal_copy(slot, 1).wait_recv()
+        normal_pass(slot, 1).start()
 
     @pl.when(head)
     def _():
@@ -1685,6 +1714,9 @@
     handed = pltpu.make_async_copy(current, out_handed, out_sem.at[1])
     handed.start()
     normal_pass(1).wait_recv()
+    for slot in range(2):
+        normal_pass(slot, 1).wait_recv()
+    projected_copy.wait()
     heads_out.wait()
     expand_out.wait()
     for copy in gain_copies[:7]:
@@ -1692,8 +1724,9 @@
     sent(heads_copies, 3, 0, wh, 2)
     sent(expand_copies, 2, 1, we, 2)
     for slot in range(2):
-        normal_copy(slot).wait_send()
-        normal_pass(slot).wait_send()
+        for kind in range(2):
+            normal_copy(slot, kind).wait_send()
+            normal_pass(slot, kind).wait_send()
     handed.wait()
     pl.when(head)(lambda: rows_copy(0).wait())
 
@@ -1711,25 +1744,25 @@
     heads_w, merge_w, expand_w, reduce_w = some(4)
     in_handed, in_inputs, in_projected, in_heads, in_middle, in_joined = some(6)
     hidden_all, upstream_all, normal_b_all, other_normal = some(4)
-    mixed_all, grad_middle_all, normal_a_all, grad_projected_all = some(4)
-    first_sum, out_result = some(2)
-    own_heads, other_heads, own_merge, other_merge = some(4)
+    mixed_all, grad_middle_all, normal_a_all, other_normal_a = some(4)
+    grad_projected_all, other_projected, first_sum, out_result = some(4)
+    own_heads, own_merge, other_merge = some(3)
     own_expand, own_reduce, other_reduce = some(3)
     (out_gain,) = some(1)
     wh, wm, we, wr = some(4)
-    buffers = types.SimpleNamespace(**GradientBuffers(*some(10))._asdict())
+    buffers = types.SimpleNamespace(**GradientBuffers(*some(8))._asdict())
     buffers.tables = some(3)
     buffers.attention_grads = some(3)
     buffers.scatter = some(7)
-    tiles, turned, wide, narrow, first_projected = some(5)
+    tiles, turned, wide, narrow, first_projected, last_projected = some(6)
     gains, head_gain, gain_out, gain_in, gain_sum, gain_other = some(6)
     load_sem, tile_sem, joined_sem, save_sem = some(4)
     buffers.gather_a, buffers.scatter_a = some(2), some(2)
     buffers.gather_b, buffers.scatter_b = some(2), some(2)
     spread_send, spread_recv, rep_send, rep_recv = some(4)
-    current, inputs, result = buffers.current, buffers.inputs, buffers.result
+    current, result = buffers.current, buffers.result
     full_a, full_b, grad_mixed = buffers.full_a, buffers.full_b, buffers.mixed
-    joined, grad_projected = buffers.joined, buffers.grad_projected
+    joined = buffers.joined
 
     place = Place()
     length, width = full_a.shape
@@ -1760,29 +1793,34 @@
     expand_load = load(2, expand_w, we)
     middle_load = load(3, in_middle.at[last], result)
     wide_load = load(4, upstream_all.at[0], wide)
-    plain = [(hidden_all, at) for at in range(hidden_width // depth)] + [(mixed_all, 0)]
-    plain += [(normal_a_all, device) for _, device in others]
-    job_count = len(plain) + len(others)
-
     def token_rows(replica):
         return pl.ds(pl.multiple_of(replica * length, length), length)
 
+    buffers.grad_projected = last_projected.at[token_rows(place.replica)]
+    jobs = [((hidden_all, None), at) for at in range(hidden_width // depth)]
+    pair = (normal_b_all.at[last], other_normal.at[last])
+    jobs += [(pair, device) for _, device in others]
+    jobs += [((mixed_all, None), 0)]
+    for slot in (0, last):
+        pair = (normal_a_all.at[slot], other_normal_a.at[slot])
+        jobs += [(pair, device) for _, device in others]
+    job_count = len(jobs)
+
     def tile_loads(job):
-        source, at = plain[job] if job < len(plain) else (None, others[job - len(plain)][1])
+        (mine, theirs), at = jobs[job]
         columns = pl.ds(pl.multiple_of(at * depth, depth), depth)
-        if source is not None:
+        if theirs is None:
             return [
                 pltpu.make_async_copy(
-                    source.at[:, columns], tiles.at[job % 2], tile_sem.at[job % 2, 0]
+                    mine.at[:, columns], tiles.at[job % 2], tile_sem.at[job % 2, 0]
                 )
             ]
-        parts = (
-            (normal_b_all.at[last, :, columns], place.replica),
-            (other_normal.at[last, :, columns], 1 - place.replica),
-        )
+        parts = ((mine, place.replica), (theirs, 1 - place.replica))
         return [
             pltpu.make_async_copy(
-                src, tiles.at[job % 2, token_rows(replica)], tile_sem.at[job % 2, part]
+                src.at[:, columns],
+                tiles.at[job % 2, token_rows(replica)],
+                tile_sem.at[job % 2, part],
             )
             for part, (src, replica) in enumerate(parts)
         ]
@@ -1804,7 +1842,15 @@
 
     tile_start(0)
     tile_start(1)
-    projected_load = load(5, grad_projected_all.at[0], first_projected)
+    projected_loads = [
+        load(
+            at, src, first_projected.at[token_rows(replica)]
+        )
+        for at, (src, replica) in (
+            (5, (grad_projected_all.at[0], place.replica)),
+            (16, (other_projected, 1 - place.replica)),
+        )
+    ]
     loads = [
         load(at + 6, src, dst)
         for at, (src, dst) in enumerate(
@@ -1813,7 +1859,6 @@
             + [
                 (in_projected.at[last], buffers.projected),
                 (in_heads.at[last], buffers.heads),
-                (in_inputs.at[last], inputs),
             ]
         )
     ]
@@ -1876,17 +1921,17 @@
             wr[span, columns] = value.astype(jnp.bfloat16)
 
         run_job(at, width, product)
-        copy = rep_copy(at, wr.at[span], other_reduce.at[span])
-        copy.start()
-        rep_copies.append(copy)
+        rep_copies.append(rep_copy(at, wr.at[span], other_reduce.at[span]))
+        if at == 0:
+            rep_copies[at].start()
         copy = pltpu.make_async_copy(wr.at[span], own_reduce.at[span], save_sem.at[at])
         copy.start()
         own_saves.append(copy)
         if at == 1:
             scatter.relay()
-    grad_middle_load = load(4, grad_middle_all.at[0], wide)
     middle_load.wait()
     feed_input_back(place, rows, scatter, result, gains_ref, gains, current, result, full_b)
+    inputs_load = load(13, in_inputs.at[last], current)
     gather.finish()
     gather_b = Gather(place, full_b, *buffers.gather_b, rows)
     scatter_b = Scatter(place, *buffers.scatter, *buffers.scatter_b, rows)
@@ -1906,7 +1951,46 @@
         held, joined, buffers.heads, grad_mixed, *buffers.attention_grads, 2 * rows
     )
     project_back(place, rows, scatter_b, buffers, head_gain_ref, head_gain, wh)
+    projected_rep = rep_copy(8, buffers.grad_projected, buffers.grad_projected)
+    projected_rep.start()
     job = hidden_width // depth
+
+    def first_load(at, device):
+        block = pl.ds(pl.multiple_of(device * depth, depth), depth)
+        into = wide.at[pl.ds(at % 2 * depth, depth), pl.ds(0, 2 * hidden_width)]
+        return pltpu.make_async_copy(first_sum.at[block], into, load_sem.at[14 + at % 2])
+
+    for at, device in others[:2]:
+        first_load(at, device).start()
+    for copy in joined_reps:
+        copy.wait_recv()
+    expand_copies = []
+    for at, device in others:
+        block = pl.ds(at * depth, depth)
+        first_load(at, device).wait()
+        before = pl.ds(at % 2 * depth, depth)
+
+        def product(tile, columns):
+            value = wide[before, columns].astype(jnp.float32)
+            value += mm(tile[...], narrow[:, columns])
+            we[block, columns] = value.astype(jnp.bfloat16)
+
+        run_job(job, narrow.shape[1], product)
+        job += 1
+        if at + 2 < PLANE:
+            first_load(*others[at + 2]).start()
+        for piece in range(2):
+            copy = spread(
+                at,
+                device,
+                piece,
+                we.at[block, pl.ds(piece * hidden_width, hidden_width)],
+                own_expand.at[:, shard_columns(piece * FF, place.index, hidden_width)],
+            )
+            copy.start()
+            expand_copies.append(copy)
+    grad_middle_load = load(4, grad_middle_all.at[0], wide)
+    rep_copies[1].start()
     grad_middle_load.wait()
 
     def merge_product(tile, columns):
@@ -1916,18 +2000,29 @@
 
     run_job(job, width, merge_product)
     job += 1
+    rep_copies[2].start()
     merge_rep = rep_copy(3, wm, other_merge)
     merge_rep.start()
     merge_save = pltpu.make_async_copy(wm, own_merge, save_sem.at[3])
     merge_save.start()
-    projected_load.wait()
+    for copy in projected_loads:
+        copy.wait()
+    for at, device in others:
+        block = pl.ds(at * depth, depth)
+
+        def product(tile, columns):
+            wh[block, columns] = mm(tile[...], first_projected[:, columns]).astype(jnp.bfloat16)
+
+        run_job(job, JOINT, product)
+        job += 1
+    projected_rep.wait_recv()
     heads_copies = []
     for at, device in others:
         block = pl.ds(at * depth, depth)
 
         def product(tile, columns):
-            value = mm(tile[:, :length], first_projected[:, columns])
-            value += mm(tile[:, length:], grad_projected[:, columns])
+            value = wh[block, columns].astype(jnp.float32)
+            value += mm(tile[...], last_projected[:, columns])
             wh[block, columns] = value.astype(jnp.bfloat16)
 
         run_job(job, JOINT, product)
@@ -1948,7 +2043,8 @@
             heads_copies.append(copy)
     scatter_b.relay()
     scatter_b.pair(0)
-    input_back(scatter_b, inputs, gains_ref, gains, result, None)
+    inputs_load.wait()
+    input_back(scatter_b, current, gains_ref, gains, result, None)
     result_save = pltpu.make_async_copy(result, out_result, save_sem.at[10])
     result_save.start()
 
@@ -1970,56 +2066,19 @@
         copy.start()
         gain_copies.append(copy)
 
-    def first_load(at, device):
-        block = pl.ds(pl.multiple_of(device * depth, depth), depth)
-        into = wide.at[pl.ds(at % 2 * depth, depth), pl.ds(0, 2 * hidden_width)]
-        return pltpu.make_async_copy(first_sum.at[block], into, load_sem.at[14 + at % 2])
-
-    for at, device in others[:2]:
-        first_load(at, device).start()
-    for copy in joined_reps:
+    for copy in gain_copies[:7]:
         copy.wait_recv()
-    expand_copies = []
-    for at, device in others:
-        block = pl.ds(at * depth, depth)
-        first_load(at, device).wait()
-        before = pl.ds(at % 2 * depth, depth)
-
-        def product(tile, columns):
-            value = wide[before, columns].astype(jnp.float32)
-            value += mm(tile[...], narrow[:, columns])
-            we[block, columns] = value.astype(jnp.bfloat16)
-
-        run_job(job, narrow.shape[1], product)
-        job += 1
-        if at + 2 < PLANE:
-            first_load(*others[at + 2]).start()
-        for piece in range(2):
-            copy = spread(
-                at,
-                device,
-                piece,
-                we.at[block, pl.ds(piece * hidden_width, hidden_width)],
-                own_expand.at[:, shard_columns(piece * FF, place.index, hidden_width)],
-            )
-            copy.start()
-            expand_copies.append(copy)
-        if at == 3:
-            for copy in heads_copies[:21]:
-                copy.wait_recv()
-            for copy in heads_copies[21:]:
-                copy.wait()
-            heads_rep = rep_copy(8, own_heads, other_heads)
-            heads_rep.start()
-            for copy in gain_copies[:7]:
-                copy.wait_recv()
-            gain_copies[7].wait()
-            total = gain_in[0]
-            for shard in range(1, PLANE):
-                total += gain_in[shard]
-            gain_sum[...] = total
-            gain_rep = rep_copy(9, gain_sum, gain_other)
-            gain_rep.start()
+    gain_copies[7].wait()
+    total = gain_in[0]
+    for shard in range(1, PLANE):
+        total += gain_in[shard]
+    gain_sum[...] = total
+    gain_rep = rep_copy(9, gain_sum, gain_other)
+    gain_rep.start()
+    for copy in heads_copies[:21]:
+        copy.wait_recv()
+    for copy in heads_copies[21:]:
+        copy.wait()
     gain_rep.wait()
     out_gain[...] = gain_sum[...] + gain_other[...]
     gather_b.finish()
@@ -2029,7 +2088,8 @@
         copy.wait()
     for copy in expand_copies[:14] + heads_copies[:21] + gain_copies[:7] + joined_reps:
         copy.wait_send()
-    for copy in rep_copies + [merge_rep, heads_rep]:
+    projected_rep.wait_send()
+    for copy in rep_copies + [merge_rep]:
         copy.wait()
 
 
@@ -2121,6 +2181,8 @@
             shape((length, 2 * hidden_width), b16),
             shape((width, 2 * hidden_width), b16),
             shape((micro, length, width), b16),
+            shape((micro, length, width), b16),
+            shape((length, JOINT), b16),
             shape((width, JOINT), b16),
             shape((width, 2 * hidden_width), b16),
             shape((2, width), f32),
@@ -2129,7 +2191,7 @@
             shape((micro, 2, HEAD_SIZE), f32),
         ),
         in_specs=vmem_specs(2) + any_specs(7),
-        out_specs=any_specs(20) + vmem_specs(4),
+        out_specs=any_specs(22) + vmem_specs(4),
         scratch_shapes=vmem((PLANE, *gain_row.shape, f32))
         + weight_buffers(width, hidden_width)
         + vmem(
@@ -2159,7 +2221,9 @@
         + [pltpu.SemaphoreType.DMA((6, PLANE - 1))] * 2
         + [pltpu.SemaphoreType.DMA((2, 2))] * 2
         + [pltpu.SemaphoreType.DMA((2, 2))]
-        + sems(4, 4, 4, 4, 4)
+        + sems(4, 4, 4)
+        + [pltpu.SemaphoreType.DMA((2, 4))] * 2
+        + sems(1, 1)
         + sems(10, 7, 2, 4, micro, micro, 2, *((10,) * 8)),
         compiler_params=kernel_params(1),
     )(own, gain_row, *tables, *weights)
@@ -2175,7 +2239,7 @@
     shape = jax.ShapeDtypeStruct
     heads_term, merge_term = (depth, PLANE * JOINT), (depth, width)
     expand_term, reduce_term = (depth, 2 * FF), (hidden_width, width)
-    terms = (heads_term,) * 2 + (merge_term,) * 2 + (expand_term,) + (reduce_term,) * 2
+    terms = (heads_term,) + (merge_term,) * 2 + (expand_term,) + (reduce_term,) * 2
     gain_width = -(-(2 * depth + 2 * HEAD_SIZE // PLANE) // 128) * 128
 
     def flat(array):
@@ -2186,11 +2250,10 @@
         out_shape=(shape((rows, width), f32),)
         + tuple(shape(term, b16) for term in terms)
         + (shape((1, gain_width), f32),),
-        in_specs=vmem_specs(4) + any_specs(22),
-        out_specs=any_specs(8) + vmem_specs(1),
+        in_specs=vmem_specs(4) + any_specs(24),
+        out_specs=any_specs(7) + vmem_specs(1),
         scratch_shapes=weight_buffers(width, hidden_width)
         + vmem(
-            (rows, width, b16),
             (rows, width, b16),
             (rows, width, f32),
             (length, width, b16),
@@ -2199,7 +2262,6 @@
             (length, JOINT, b16),
             (length, MERGED, b16),
             (2, 2 * rows, 2 * hidden_width, f32),
-            (length, JOINT, b16),
         )
         + table_buffers(length)
         + attention_buffers(length)
@@ -2209,7 +2271,8 @@
             (2, depth, micro * length, b16),
             (length, width, b16),
             (2 * length, 2 * hidden_width, b16),
-            (length, JOINT, b16),
+            (2 * length, JOINT, b16),
+            (2 * length, JOINT, b16),
             (2, width, f32),
             (2, HEAD_SIZE, f32),
             (PLANE, 1, gain_width, f32),
@@ -2245,8 +2308,10 @@
         layers.other_normal,
         flat(saved.mixed),
         saved.grad_middle,
-        flat(saved.normal_a),
+        saved.normal_a,
+        layers.other_normal_a,
         saved.grad_projected,
+        layers.other_projected,
         layers.first_sum,
     )
 
@@ -2301,15 +2366,12 @@
     last_rows, *terms, gain_sums = run_gradients(
         layers, table_rows, merge_weight[0], reduce_weight[0]
     )
-    own_heads, other_heads, own_merge, other_merge, own_expand, own_reduce, other_reduce = terms
+    own_heads, own_merge, other_merge, own_expand, own_reduce, other_reduce = terms
+    grad_heads = own_heads.astype(jnp.float32)[None]
     grad_expand = own_expand.astype(jnp.float32)[None]
-    grad_heads, grad_merge, grad_reduce = (
+    grad_merge, grad_reduce = (
         (mine.astype(jnp.float32) + theirs.astype(jnp.float32))[None]
-        for mine, theirs in (
-            (own_heads, other_heads),
-            (own_merge, other_merge),
-            (own_reduce, other_reduce),
-        )
+        for mine, theirs in ((own_merge, other_merge), (own_reduce, other_reduce))
     )
     head_count = head_gain.shape[1]
     head = lax.axis_index("section") == 0

time: 847 us -> 834 us (0.985)
  Pallas kernels: 804 us -> 785 us
    pallas_call x1, Pallas kernels: 230 us -> 210 us  [run_gradients(): pl.pallas_call(functools.partial(gradient_kernel, rows), out_shape=(shape...]
where the time goes in v5:
time: 834 us; the launch traced here: 819 us
  Pallas kernels  785 us (94%)
  other arithmetic  27.4 us (3%)
    pallas_call x1, Pallas kernels, run_layers(): pl.pallas_call(functools.partial(layers_kernel, rows), out_shape=(shape((...  575 us
    pallas_call x1, Pallas kernels, run_gradients(): pl.pallas_call(functools.partial(gradient_kernel, rows), out_shape=(shape...  210 us

profile of v5, /device:TPU:0, one launch (start us, length us, event | category | flops | bytes accessed | tf_op | source)
XLA Modules:
  0.0 818.6 jit_solution(4836553477156749413)
XLA Ops:
  0.6 0.7 slice_bitcast_fusion.3
  1.3 0.2 reduce-window.16
  1.5 0.2 reduce-window.17
  1.7 0.1 select_reduce_fusion
  1.8 3.7 fusion.1
  5.5 0.2 maximum_bitcast_fusion.3
  5.7 0.2 maximum_bitcast_fusion.4
  5.9 1.0 pad_maximum_fusion.1.refs_3_.refs_5_
  7.0 0.2 maximum_bitcast_fusion.1
  7.2 0.2 maximum_bitcast_fusion.2
  7.4 1.0 pad_maximum_fusion.refs_2_.refs_4_
  8.4 0.0 copy-start.7
  8.4 0.0 copy-start.8
  8.4 0.0 copy-start.9
  8.4 0.2 copy.27
  8.7 0.1 subtract_subtract_fusion
  8.7 0.2 copy.26
  9.0 0.1 subtract_subtract_fusion.1
  9.0 1.0 pad_add_fusion.refs_4_.refs_6_
  10.1 0.0 copy-done.7
  10.1 0.0 copy-done.8
  10.1 0.0 copy-done.9
  10.1 0.6 reshape.135.refs_1_
  10.7 575.0 %shard_map.152 = (f32[2,128,2048]{2,1,0:T(8,128)}, bf16[2,128,2048]{2,1,0:T(8,128)(2,1)}, bf16[2,1024,2048]{2,1,0:T(8,128)(2,1)}, f32[2,1024,512]{2,1,0:T(8,128)...) custom-call(bf16[2,128,2048]{2,1,0:T(8,128)(2,1)} %bitcast.56, ...), custom_call_target="tpu_custom_call" | custom-call | tf_op jit(solution)/shard_map/pallas_call | solution.py:2174
  585.7 210.4 %shard_map.153 = (f32[128,2048]{1,0:T(8,128)}, bf16[256,4096]{1,0:T(8,128)(2,1)}, bf16[256,2048]{1,0:T(8,128)(2,1)}, bf16[256,2048]{1,0:T(8,128)(2,1)}, bf16[256...) custom-call(f32[2,2048]{1,0:T(2,128)} %get-tuple-element.41.refs_0_, ...), custom_call_target="tpu_custom_call" | custom-call | tf_op jit(solution)/shard_map/pallas_call | solution.py:2248
  796.1 0.0 copy-start
  796.1 7.0 add_bitcast_fusion
  803.2 0.0 copy-done
  803.2 0.0 copy-start.4
  803.2 0.0 copy-start.5
  803.2 6.3 bitcast_convert_fusion
  809.4 0.0 copy-start.2
  809.5 0.0 copy-start.3
  809.5 0.0 copy-done.4
  809.5 0.0 copy-done.5
  809.5 1.7 add_bitcast_fusion.1
  811.2 0.5 copy-done.2
  811.6 0.5 copy-done.3
  812.1 0.1 fusion
  812.2 0.0 copy-start.1
  812.2 0.1 slice.23
  812.3 1.5 maximum_bitcast_fusion
  813.7 0.8 copy-done.1
  814.5 0.0 copy-start.6
  814.5 2.5 bitcast_convert_fusion.1
  817.0 0.0 copy-done.6
  817.0 0.6 fusion.9
  817.6 0.5 slice.26
  (6 shorter events, 0.1 us)
Async XLA Ops:
  8.4 1.6 copy-start.7
  8.4 1.7 copy-start.8
  8.4 1.7 copy-start.9
  796.1 7.1 copy-start
  803.2 6.3 copy-start.4
  803.2 6.3 copy-start.5
  809.4 2.2 copy-start.2
  809.5 2.6 copy-start.3
  812.2 2.3 copy-start.1
  814.5 2.5 copy-start.6
